TPU v7x, 32 devices: a whole 2x2x4 slice. The times are simulated.
32 devices in a mesh: row: 8 (over z, y), col: 4 (over x, core).
Axes of the slice: x: 2, y: 2, z: 4, core: 2. Of those that a mesh axis runs over, the one named last changes fastest.
Arguments:
- matrix: bfloat16 [4096, 4096], P('row', 'col'), may hold values from 0 to 0.0048828125, as said below
- in_mask: int32 [16, 16], P('row', 'col'), may hold values from 0 to 1, as said below
- out_mask: int32 [16, 16], P('row', 'col'), may hold values from 0 to 1, as said below
Outputs:
- flow: float32 [4096, 4096], P('row', 'col')
Inputs may be any that keep to these rules, and one draw needn't show every extreme that they name: `matrix`: every diagonal entry is positive; all other entries are zero or positive. `in_mask`: tiles on the diagonal are 1. The block of tiles of one device holds at most 6 ones, and some device's block holds exactly 6. `out_mask`: tiles on the diagonal are 1.
All inputs are finite; a program needn't handle non-finite values.
Results may differ from a plain program's by a relative error of at most 0.0003.
Values may be sent and summed in bfloat16 or wider, within the bound.
No kernel may reach another device: no remote copies, remote signals or barrier semaphores. Data moves between devices by JAX's collectives and lax.ppermute only.
A program may use at most 128 MiB of HBM per device.

v0:
```python
import jax
import jax.numpy as jnp
from jax import lax
from jax.sharding import PartitionSpec as P


def expand_mask(values, tile_flags):
    tile_rows, tile_cols = tile_flags.shape
    shaped = values.reshape(
        tile_rows, values.shape[0] // tile_rows, tile_cols, values.shape[1] // tile_cols
    )
    return (shaped * tile_flags.astype(values.dtype)[:, None, :, None]).reshape(values.shape)


def masked_product(left_part, left_flags, right_part, right_flags):
    return jnp.dot(
        expand_mask(left_part, left_flags),
        expand_mask(right_part, right_flags),
        preferred_element_type=jnp.float32,
    )


def per_device(matrix, in_mask, out_mask):
    local_rows, local_cols = matrix.shape
    col_values, col_flags = (
        lax.all_gather(matrix, "row", axis=0, tiled=True),
        lax.all_gather(in_mask, "row", axis=0, tiled=True),
    )
    piece_values = lax.all_gather(matrix, "col", axis=1, tiled=True)
    piece_flags = lax.all_gather(in_mask, "col", axis=1, tiled=True)
    product = masked_product(piece_values, piece_flags, col_values, col_flags)
    inflated = expand_mask(product * product, out_mask)
    partial_sums = jnp.sum(inflated, axis=0)
    totals = lax.psum(partial_sums, "row")
    total_rows = float(local_rows * lax.axis_size("row"))
    return total_rows * inflated / totals[None, :]


def solution(mesh):
    placed = (P("row", "col"), P("row", "col"), P("row", "col"))
    return jax.shard_map(
        per_device, mesh=mesh, in_specs=placed, out_specs=P("row", "col"), check_vma=False
    )
```

profile of v0, /device:TPU:0, one launch (start us, length us, event | category | flops | bytes accessed | tf_op | source)
XLA Modules:
  0.0 213.5 jit_solution(2757397026888427738)
XLA Ops:
  6.5 0.0 all-gather.5.cloned.1.call-start
  6.5 0.7 all-gather.5.cloned.1.call-update
  7.3 0.0 all-gather.7.cloned.1.call-start
  7.3 0.7 all-gather.7.cloned.1.call-update
  8.0 6.3 %all-gather = s32[4,4,2]{1,2,0:T(2,128)S(1)} all-gather(s32[1,4,2]{1,2,0:T(2,128)} %bitcast.24), channel_id=1, replica_groups=mesh['row'=8,'col'=4] {'col'}, dimensions={0}, use_global_device_ids=true | all-gather | bytes 160 | tf_op jit(solution)/shard_map/all_gather | solution.py:30
  14.3 21.5 %all-gather.1 = s32[8,2,4]{2,1,0:T(2,128)S(1)} all-gather(s32[1,2,4]{2,1,0:T(2,128)} %bitcast.25), channel_id=1, replica_groups=mesh['row'=8,'col'=4] {'row'}, dimensions={0}, use_global_device_ids=true | all-gather | bytes 288 | tf_op jit(solution)/shard_map/all_gather | solution.py:27
  35.8 5.5 %mul.45 = bf16[16,256,4,256]{3,2,1,0:T(4,128)(2,1)} broadcast(bf16[16,4]{1,0:T(8,128)(2,1)S(1)} %bitcast.23), dimensions={0,2} | broadcast | bytes 8388736 | tf_op jit(solution)/shard_map/mul | solution.py:12
  41.2 9.4 %copy.7 = bf16[512,8,4,256]{3,1,2,0:T(8,128)(2,1)} copy(bf16[512,8,4,256]{3,2,1,0:T(4,128)(2,1)} %bitcast.17) | data formatting | bytes 16777216
  50.7 0.1 reshape.18
  50.8 0.3 mul.42
  51.1 0.0 copy-start
  51.1 4.1 %copy.6 = bf16[64,8,16,256]{3,1,2,0:T(8,128)(2,1)} copy(bf16[64,8,16,256]{3,2,1,0:T(8,128)(2,1)S(1)} %bitcast.18) | data formatting | bytes 8388608
  55.3 0.0 copy-done
  55.3 0.3 mul.49
  55.6 1.8 copy.8
  57.4 0.0 all-gather.5.cloned.1.call-done
  57.4 115.8 %all-gather.7.cloned.1.call-done = bf16[4096,1024]{1,0:T(8,128)(2,1)} async-done(((bf16[512,1024]{1,0:T(8,128)(2,1)}), bf16[4096,1024]{1,0:T(8,128)(2,1)}) %all-gather.7.cloned.1.call-update) | async-done | bytes 8388624 | tf_op jit(solution)/shard_map/all_gather | solution.py:26
  173.2 13.4 %fusion.7 = (f32[1024]{0:T(1024)S(1)}, f32[512,1024]{1,0:T(8,128)S(1)}) fusion(f32[512,1024]{1,0:T(8,128)} %bitcast.22, bf16[4096,1024]{1,0:T(8,128)(2,1)} %all-gather.7.cloned.1.call-done, bf16[4096,1024]{1,0:T(8,128)(2,1)} %bitcast.19, bf16[512,4096]{1,0:T(8,128)(2,1)} %all-gather.5.cloned.1.call-done, bf16[512,4096]{1,0:T(8,128)(2,1)} %bitcast.21), kind=kOutput, calls=%fused_computation.5 | convolution fusion | flops 4302830592 | bytes 29364224 | tf_op jit(solution)/shard_map/dot_general | solution.py:16
  186.6 18.4 %psum.7 = f32[1024]{0:T(1024)S(1)} all-reduce(f32[1024]{0:T(1024)S(1)} %get-tuple-element.5), channel_id=1, replica_groups=mesh['row'=8,'col'=4] {'row'}, use_global_device_ids=true, to_apply=%region_1.0 | all-reduce | flops 1024 | bytes 8192 | tf_op jit(solution)/shard_map/psum | solution.py:34
  205.0 1.6 multiply_divide_fusion
  (4 shorter events, 0.0 us)
Async XLA Ops:
  6.5 50.9 %all-gather.5.cloned.1.call-start = ((), (), s32[]{:S(2)}) async-start(), calls=%async_computation | async-start | bytes 5242880 | tf_op jit(solution)/shard_map/all_gather | solution.py:29
  7.3 166.0 %all-gather.7.cloned.1.call-start = ((), (), s32[]{:S(2)}) async-start(), calls=%async_computation.1 | async-start | bytes 9437184 | tf_op jit(solution)/shard_map/all_gather | solution.py:26
  51.1 4.2 %copy-start = (s32[2,4]{1,0:T(2,128)S(1)}, s32[2,4]{1,0:T(2,128)}, u32[]{:S(2)}) copy-start(s32[2,4]{1,0:T(2,128)} %param.5) | copy-start | bytes 100
Sparse Core Ops, SparseCore 0:
  8.9 37.1 all-gather.4
  48.3 124.9 all-gather.6
where the time goes:
time: 214 us; the launch traced here: 213 us
  waiting for transfers between devices  117 us (55%)
  blocking collectives  46.2 us (22%)
  local copies, waits for them, and re-layouts  21.6 us (10%)
  matrix products  13.4 us (6%)
  between operations  13.4 us (6%)
    all_gather x1, waiting for transfers between devices, per_device(): lax.all_gather(matrix, 'row', axis=0, tiled=True)  116 us
    all_gather x1, blocking collectives, per_device(): lax.all_gather(in_mask, 'row', axis=0, tiled=True)  21.5 us
    psum x1, blocking collectives, per_device(): totals = lax.psum(partial_sums, 'row')  18.4 us
    unnamed x5, local copies, waits for them, and re-layouts  15.3 us
    dot_general x1, matrix products, masked_product(): jnp.dot(expand_mask(left_part, left_flags), expand_mask(right_part, right...  13.4 us
    all_gather x1, blocking collectives, per_device(): piece_flags = lax.all_gather(in_mask, 'col', axis=1, tiled=True)  6.25 us
    mul x3, local copies, waits for them, and re-layouts, expand_mask(): shaped * tile_flags.astype(values.dtype)[:, None, :, None]  6.13 us
  transfers between devices with their start and end apart: 2, of which 1 were waited for; matrix products, arithmetic and copies ran while one was open for 10% of the time, Pallas kernels for 0%

commit v1 on v0

v1 whole, which is shorter than its diff:
```python
import functools

import jax
import jax.numpy as jnp
from jax import lax
from jax.experimental import pallas as pl
from jax.experimental.pallas import tpu as pltpu
from jax.sharding import PartitionSpec as P

CODE_ROWS = 16
VMEM_LIMIT = 16 * 1024 * 1024


def cost(weight=1):
    return pl.CostEstimate(flops=weight << 29, bytes_accessed=0, transcendentals=0)


class Sizes:
    def __init__(self, matrix, in_mask, n_row, n_col):
        self.rows, self.cols = matrix.shape
        self.tr, self.tc = in_mask.shape
        self.tile = self.rows // self.tr
        self.cap = self.tr * self.tc * 3 // 4
        self.pay_rows = CODE_ROWS + self.cap * self.tile
        self.buf_rows = self.pay_rows + self.tile
        self.cut = CODE_ROWS + (self.cap + 1) // 2 * self.tile
        self.chunks = ((0, self.cut), (self.cut, self.pay_rows - self.cut))
        self.n_row, self.n_col = n_row, n_col


def ring_order(n_row):
    n_out = 4 if n_row % 4 == 0 else 2
    n_in = n_row // n_out
    ring = [(0, 0)]
    for o in range(n_out):
        inner = list(range(1, n_in))
        ring += [(o, i) for i in (inner if o % 2 == 0 else inner[::-1])]
    ring += [(o, 0) for o in range(n_out - 1, 0, -1)]
    return [o * n_in + i for o, i in ring]


def pick(values, index):
    out = jnp.int32(values[0])
    for i, value in enumerate(values[1:], 1):
        out = jnp.where(index == i, value, out)
    return out


def origin(sz, key):
    ring = ring_order(sz.n_row)
    rows = [ring[(ring.index(q) - key) % sz.n_row] for q in range(sz.n_row)]
    return pick(rows, lax.axis_index("row"))


def pack_kernel(sz, mask_ref, matrix_ref, whole_ref, *chunk_refs):
    flags = [
        (mask_ref[t // sz.tc, t % sz.tc] != 0).astype(jnp.int32) for t in range(sz.tr * sz.tc)
    ]
    before, count = [], jnp.int32(0)
    for flag in flags:
        before.append(count)
        count = count + flag
    code = jnp.int32(0)
    for t, flag in enumerate(flags):
        code = code + flag * (1 << t)
    codes = jnp.full((CODE_ROWS, sz.tile), code.astype(jnp.float32), jnp.float32)
    codes = codes.astype(jnp.bfloat16)
    whole_ref[0:CODE_ROWS, :] = codes
    chunk_refs[0][0:CODE_ROWS, :] = codes
    for s in range(sz.cap):
        which = jnp.int32(0)
        for t, flag in enumerate(flags):
            which = jnp.where((flag == 1) & (before[t] == s), t, which)
        row = pl.multiple_of(which // sz.tc * sz.tile, sz.tile)
        col = pl.multiple_of(which % sz.tc * sz.tile, sz.tile)
        values = matrix_ref[pl.ds(row, sz.tile), pl.ds(col, sz.tile)]
        at = CODE_ROWS + s * sz.tile
        whole_ref[at : at + sz.tile, :] = values
        for ref, (start, size) in zip(chunk_refs, sz.chunks):
            if start <= at < start + size:
                ref[at - start : at - start + sz.tile, :] = values


def pack(sz, matrix, in_mask):
    vmem = pl.BlockSpec(memory_space=pltpu.VMEM)
    sizes = [sz.pay_rows] + [size for _, size in sz.chunks]
    return pl.pallas_call(
        functools.partial(pack_kernel, sz),
        out_shape=[pltpu.VMEM((size, sz.tile), jnp.bfloat16) for size in sizes],
        in_specs=[pl.BlockSpec(memory_space=pltpu.SMEM), vmem],
        out_specs=[vmem] * len(sizes),
        compiler_params=pltpu.CompilerParams(vmem_limit_bytes=VMEM_LIMIT),
        name="pack_tiles",
    )(*(pltpu.with_memory_space_constraint(x, pltpu.HBM) for x in (in_mask, matrix)))


def slots_of(sz, code_block):
    code = jnp.max(code_block.astype(jnp.float32)).astype(jnp.int32)
    slots, count = [], jnp.int32(0)
    for t in range(sz.tr * sz.tc):
        flag = lax.rem(lax.shift_right_logical(code, jnp.int32(t)), jnp.int32(2))
        slots.append(jnp.where(flag == 1, count, sz.cap))
        count = count + flag
    return slots


def slot_rows(sz, slot):
    return pl.ds(pl.multiple_of(CODE_ROWS + slot * sz.tile, 16), sz.tile)


def expand_kernel(sz, n, *refs):
    pays, dense, (buf, sems) = refs[:n], refs[n : 2 * n], refs[2 * n :]
    copies = []
    for p in range(n):
        copy = pltpu.make_async_copy(pays[p], buf.at[p, pl.ds(0, sz.pay_rows)], sems.at[p])
        copy.start()
        copies.append(copy)
        buf[p, sz.pay_rows :, :] = jnp.zeros((sz.tile, sz.tile), jnp.bfloat16)
    for p in range(n):
        copies[p].wait()
        slots = slots_of(sz, buf[p, 0:CODE_ROWS, 0:128])
        for t in range(sz.tr * sz.tc):
            a, k = t // sz.tc, t % sz.tc
            dense[p][a * sz.tile : (a + 1) * sz.tile, k * sz.tile : (k + 1) * sz.tile] = buf[
                p, slot_rows(sz, slots[t]), :
            ]


def expand(sz, pays, weight=1):
    n = len(pays)
    return pl.pallas_call(
        functools.partial(expand_kernel, sz, n),
        out_shape=[jax.ShapeDtypeStruct((sz.rows, sz.cols), jnp.bfloat16)] * n,
        in_specs=[pl.BlockSpec(memory_space=pltpu.HBM)] * n,
        out_specs=[pl.BlockSpec(memory_space=pltpu.VMEM)] * n,
        scratch_shapes=[
            pltpu.VMEM((n, sz.buf_rows, sz.tile), jnp.bfloat16),
            pltpu.SemaphoreType.DMA((n,)),
        ],
        compiler_params=pltpu.CompilerParams(vmem_limit_bytes=2 * VMEM_LIMIT),
        cost_estimate=cost(weight),
        name="expand_tiles",
    )(*pays)


def load_right(sz, buf, slots, b):
    tiles = [buf[slot_rows(sz, slots[k * sz.tc + b]), :] for k in range(sz.tr)]
    return jnp.concatenate(tiles, axis=0)


def start_left(sz, dist, blocks, key, into, sem):
    row = origin(sz, key)
    per_block = sz.cols // sz.rows
    column = pl.multiple_of(lax.rem(row, per_block) * sz.rows, sz.rows)
    apart = (row // per_block) ^ lax.axis_index("col")
    for d, block in zip(dist, blocks):

        @pl.when(apart == d)
        def _():
            pltpu.make_async_copy(block.at[:, pl.ds(column, sz.rows)], into, sem).start()


def wait_left(sz, blocks, into, sem):
    pltpu.make_async_copy(blocks[0].at[:, pl.ds(0, sz.rows)], into, sem).wait()


def on_core(core):
    if core is None:
        return jnp.bool_(True)
    return lax.axis_index("col") % 2 == core


def product_kernel(sz, dist, keys, first, then, *refs):
    refs = list(refs)
    blocks = [refs.pop(0) for _ in dist]
    pays = [[refs.pop(0) for _ in sz.chunks] for _ in keys]
    before_ref = None if first else refs.pop(0)
    out_ref = refs.pop(0)
    then_ref = None if then is None else refs.pop(0)
    buf, left, sems = refs
    per_piece = len(sz.chunks) + 1

    def copies(p):
        return [
            pltpu.make_async_copy(
                pays[p][h], buf.at[p, pl.ds(*chunk)], sems.at[p * per_piece + 1 + h]
            )
            for h, chunk in enumerate(sz.chunks)
        ]

    def begin(p, key):
        start_left(sz, dist, blocks, key, left.at[p], sems.at[p * per_piece])
        for copy in copies(p):
            copy.start()

    def add(p):
        buf[p, sz.pay_rows :, :] = jnp.zeros((sz.tile, sz.tile), jnp.bfloat16)
        wait_left(sz, blocks, left.at[p], sems.at[p * per_piece])
        for copy in copies(p):
            copy.wait()
        slots = slots_of(sz, buf[p, 0:CODE_ROWS, 0:128])
        for b in range(sz.tc):
            cols = slice(b * sz.tile, (b + 1) * sz.tile)
            term = jnp.dot(
                left[p], load_right(sz, buf.at[p], slots, b), preferred_element_type=jnp.float32
            )
            if p:
                term = term + out_ref[:, cols]
            elif not first:
                term = term + before_ref[:, cols]
            out_ref[:, cols] = term

    for p, (key, core) in enumerate(keys):
        if core is None:
            begin(p, key)
        else:
            pl.when(on_core(core))(functools.partial(begin, p, key))
    if then is not None:
        start_left(sz, dist, blocks, then, then_ref, sems.at[len(keys) * per_piece])
    for p, (key, core) in enumerate(keys):
        if core is None:
            add(p)
        else:
            pl.when(on_core(core))(functools.partial(add, p))
    if then is not None:
        wait_left(sz, blocks, then_ref, sems.at[len(keys) * per_piece])


def product(sz, before, dist, blocks, pieces, keys, then=None):
    n = len(keys)
    first = before is None
    vmem = pl.BlockSpec(memory_space=pltpu.VMEM)
    chunks = [chunk for piece in pieces for chunk in piece]
    in_specs = [pl.BlockSpec(memory_space=pl.ANY)] * len(blocks)
    in_specs += [pl.BlockSpec(memory_space=pltpu.HBM)] * len(chunks)
    args = [*blocks, *chunks]
    if not first:
        in_specs.append(vmem)
        args.append(before)
    out_shape = [jax.ShapeDtypeStruct((sz.rows, sz.cols), jnp.float32)]
    if then is not None:
        out_shape.append(jax.ShapeDtypeStruct((sz.rows, sz.rows), jnp.bfloat16))
    return pl.pallas_call(
        functools.partial(product_kernel, sz, dist, keys, first, then),
        out_shape=out_shape,
        in_specs=in_specs,
        out_specs=[vmem] * len(out_shape),
        scratch_shapes=[
            pltpu.VMEM((n, sz.buf_rows, sz.tile), jnp.bfloat16),
            pltpu.VMEM((n, sz.rows, sz.rows), jnp.bfloat16),
            pltpu.SemaphoreType.DMA((n * (len(sz.chunks) + 1) + 1,)),
        ],
        compiler_params=pltpu.CompilerParams(vmem_limit_bytes=VMEM_LIMIT),
        cost_estimate=cost(),
        name="product",
    )(*args)


def keep_kernel(sz, out_mask_ref, keep_ref):
    for a in range(sz.tr):
        for b in range(sz.tc):
            rows, cols = slice(a * 8, (a + 1) * 8), slice(b * sz.tile, (b + 1) * sz.tile)
            kept = (out_mask_ref[a, b] != 0).astype(jnp.float32)
            keep_ref[rows, cols] = jnp.full((8, sz.tile), kept, jnp.float32)


def keep_rows(sz, out_mask):
    return pl.pallas_call(
        functools.partial(keep_kernel, sz),
        out_shape=jax.ShapeDtypeStruct((8 * sz.tr, sz.cols), jnp.float32),
        in_specs=[pl.BlockSpec(memory_space=pltpu.SMEM)],
        out_specs=pl.BlockSpec(memory_space=pltpu.VMEM),
        compiler_params=pltpu.CompilerParams(vmem_limit_bytes=VMEM_LIMIT),
        cost_estimate=cost(),
        name="keep_rows",
    )(out_mask)


def last_kernel(sz, core, keep_ref, left_ref, *refs):
    refs = list(refs)
    pays = [refs.pop(0) for _ in sz.chunks]
    before_ref = refs.pop(0)
    known_ref = refs.pop(0) if core else None
    out_ref, sums_ref, buf = refs
    here = lax.axis_index("col") % 2 == core

    @pl.when(here)
    def _():
        for ref, chunk in zip(pays, sz.chunks):
            buf[pl.ds(*chunk), :] = ref[...]
        buf[sz.pay_rows :, :] = jnp.zeros((sz.tile, sz.tile), jnp.bfloat16)
        slots = slots_of(sz, buf[0:CODE_ROWS, 0:128])
        for b in range(sz.tc):
            cols = slice(b * sz.tile, (b + 1) * sz.tile)
            block = before_ref[:, cols] + jnp.dot(
                left_ref[...], load_right(sz, buf, slots, b), preferred_element_type=jnp.float32
            )
            total = jnp.zeros((1, sz.tile), jnp.float32)
            for a in range(sz.tr):
                rows = slice(a * sz.tile, (a + 1) * sz.tile)
                part = block[rows]
                kept = keep_ref[a * 8 : a * 8 + 1, cols] != 0
                part = jnp.where(kept, part * part, jnp.zeros_like(part))
                out_ref[rows, cols] = part
                total = total + jnp.sum(part, axis=0, keepdims=True)
            sums_ref[:, cols] = total

    @pl.when(jnp.logical_not(here))
    def _():
        sums_ref[...] = jnp.zeros_like(sums_ref) if known_ref is None else known_ref[...]


def last_product(sz, core, before, left, piece, keep, known=None):
    vmem = pl.BlockSpec(memory_space=pltpu.VMEM)
    args = [keep, left, *piece, before] + ([] if known is None else [known])
    return pl.pallas_call(
        functools.partial(last_kernel, sz, core),
        out_shape=[
            jax.ShapeDtypeStruct((sz.rows, sz.cols), jnp.float32),
            jax.ShapeDtypeStruct((1, sz.cols), jnp.float32),
        ],
        in_specs=[vmem] * len(args),
        out_specs=[vmem] * 2,
        scratch_shapes=[pltpu.VMEM((sz.buf_rows, sz.tile), jnp.bfloat16)],
        compiler_params=pltpu.CompilerParams(vmem_limit_bytes=VMEM_LIMIT),
        cost_estimate=cost(),
        name="product_last",
    )(*args)


def scale_kernel(sz, steps, first_ref, second_ref, totals_ref, flow_ref, buf, sems):
    total_rows = float(sz.rows * sz.n_row)
    size = sz.rows // steps
    totals = totals_ref[...]
    copies = []
    for s in range(steps):
        rows = pl.ds(s * size, size)
        for core, ref in enumerate((first_ref, second_ref)):

            @pl.when(lax.axis_index("col") % 2 == core)
            def _():
                buf[rows, :] = total_rows * ref[rows, :] / totals

        copies.append(pltpu.make_async_copy(buf.at[rows], flow_ref.at[rows], sems.at[s]))
        copies[-1].start()
    for copy in copies:
        copy.wait()


def scale(sz, first, second, totals):
    vmem = pl.BlockSpec(memory_space=pltpu.VMEM)
    steps = 4
    return pl.pallas_call(
        functools.partial(scale_kernel, sz, steps),
        out_shape=jax.ShapeDtypeStruct((sz.rows, sz.cols), jnp.float32),
        in_specs=[vmem] * 3,
        out_specs=pl.BlockSpec(memory_space=pltpu.HBM),
        scratch_shapes=[
            pltpu.VMEM((sz.rows, sz.cols), jnp.float32),
            pltpu.SemaphoreType.DMA((steps,)),
        ],
        compiler_params=pltpu.CompilerParams(vmem_limit_bytes=VMEM_LIMIT),
        cost_estimate=cost(),
        name="scale",
    )(first, second, totals)


def column_sums(sz, sums):
    if sz.n_row % 2:
        return lax.psum(sums, "row")
    pair = sums + lax.ppermute(sums, "row", [(q, q ^ 1) for q in range(sz.n_row)])
    others = [
        lax.ppermute(pair, "row", [(q, (q + 2 * t) % sz.n_row) for q in range(sz.n_row)])
        for t in range(1, sz.n_row // 2)
    ]
    return functools.reduce(jnp.add, others, pair)


def after(values, *anchors):
    return lax.optimization_barrier((*values, *anchors))[: len(values)]


def per_device(n_row, n_col, matrix, in_mask, out_mask):
    sz = Sizes(matrix, in_mask, n_row, n_col)
    ring = ring_order(n_row)
    half = n_row // 2

    whole, *own = pack(sz, matrix, in_mask)

    def hop(chunk, way):
        pairs = [(ring[p], ring[(p + way) % n_row]) for p in range(n_row)]
        return lax.ppermute(chunk, "row", pairs)

    def last_hop(chunk, way, core):
        pairs = [
            (ring[p] * n_col + c, (ring[(p + way) % n_row] if c % 2 == core else ring[p]) * n_col + c)
            for p in range(n_row)
            for c in range(n_col)
        ]
        return lax.ppermute(chunk, ("row", "col"), pairs)

    def apart(value, far):
        return lax.ppermute(value, "col", [(q, q ^ far) for q in range(n_col)])

    lead = {1: 0, -1: 1}
    pieces = {0: list(own)}
    arrivals = [(step, h) for step in range(1, half + 1) for h in (0, 1)][:-1]

    def send(step, h, sources):
        key = {way: way * step if step < half else half for way in (1, -1)}
        for way, source in zip((1, -1), sources):
            pieces.setdefault(key[way], [None] * 2)[lead[way] ^ h] = hop(source, way)

    def arrived(step, h):
        return [pieces[way * step if step < half else half][lead[way] ^ h] for way in (1, -1)]

    for h in (0, 1):
        send(1, h, [own[lead[way] ^ h] for way in (1, -1)])
    far = n_col // 2
    blocks, dense = {0: whole, 1: apart(whole, 1)}, {}
    acc, more, gate = None, [], []
    for i, (step, h) in enumerate(arrivals[:-1]):
        here = after(arrived(step, h), *gate)
        if i + 3 < len(arrivals):
            send(step + 1, h, here)
        elif i + 2 < len(arrivals):
            final = list(here)
            first = [last_hop(chunk, way, 0) for chunk, way in zip(final, (1, -1))]
        gate = list(here)
        if i == 0:
            mine, near = after([blocks[0], blocks[1]], *here)
            (dense[0],) = expand(sz, [mine], 12)
            if far > 1:
                blocks[far] = apart(after([whole], blocks[1])[0], far)
            gate += [dense[0], near]
        if i == 1:
            (dense[1],) = expand(sz, after([blocks[1]], *here), 12)
            gate += [dense[1]]
        if i == 1 and far > 1:
            (blocks[far],) = after([blocks[far]], *here)
        if i == 3:
            bit = far
            while bit > 2:
                bit //= 2
                for d in [d for d in blocks if d != 1]:
                    blocks[d ^ bit] = apart(blocks[d], bit)
            for d in [d for d in blocks if d > 1]:
                blocks[d ^ 1] = apart(blocks[d], 1)
            rest = sorted(d for d in blocks if d > 1)
            if rest:
                dense.update(zip(rest, expand(sz, after([blocks[d] for d in rest], *here))))
        if i == 1:
            keep = keep_rows(sz, after([out_mask], *here)[0])
            gate.append(keep)
        keys = None
        if i == 3:
            keys = [(0, None), (1, 0), (-1, 0)]
        elif i == 4:
            keys = [(2, None), (-2, None), (1, 1), (-1, 1)]
        elif i > 4 and h == 1:
            keys = [(step, None), (-step, None)]
        if keys:
            dist = sorted(dense)
            then = half if keys[0][0] == half - 1 else None
            chunks = [list(pieces[key]) for key, _ in keys]
            (chunks[0][0],) = after([chunks[0][0]], *here)
            acc, *more = product(sz, acc, dist, [dense[d] for d in dist], chunks, keys, then)
            gate.append(acc)
        if i + 3 == len(arrivals):
            final = after(final, acc)
            second = [last_hop(chunk, way, 1) for chunk, way in zip(final, (1, -1))]
    (left,) = more
    mine, sums = last_product(sz, 0, acc, left, first, keep)
    other, sums = last_product(sz, 1, acc, left, second, keep, sums)
    return scale(sz, mine, other, column_sums(sz, sums))


def solution(mesh):
    placed = (P("row", "col"), P("row", "col"), P("row", "col"))
    return jax.shard_map(
        functools.partial(per_device, mesh.shape["row"], mesh.shape["col"]),
        mesh=mesh,
        in_specs=placed,
        out_specs=P("row", "col"),
        check_vma=False,
    )
```

time: 214 us -> 77 us (0.36)
  waiting for transfers between devices: 117 us -> 31.7 us
  blocking collectives: 46.2 us -> 0 us
  starting transfers between devices: 0.04 us -> 29.3 us
  local copies, waits for them, and re-layouts: 21.6 us -> 0.01 us
  Pallas kernels: 0 us -> 15.6 us
  matrix products: 13.4 us -> 0 us
  between operations: 13.4 us -> 0.18 us
    all_gather x2 -> x0, waiting for transfers between devices: 116 us -> none  [the longest x1 116 us: per_device(): lax.all_gather(matrix, 'row', axis=0, tiled=True)]
    ppermute x0 -> x23, waiting for transfers between devices: none -> 31.7 us  [the longest x12 27.5 us: hop(): return lax.ppermute(chunk, 'row', pairs)]
    ppermute x0 -> x23, starting transfers between devices: none -> 29.3 us  [the longest x12 12.9 us: hop(): return lax.ppermute(chunk, 'row', pairs)]
    all_gather x2 -> x0, blocking collectives: 27.8 us -> none  [the longest x1 21.5 us: per_device(): lax.all_gather(in_mask, 'row', axis=0, tiled=True)]
    psum x1 -> x0, blocking collectives: 18.4 us -> none  [per_device(): totals = lax.psum(partial_sums, 'row')]
    pallas_call x0 -> x11, Pallas kernels: none -> 15.6 us  [the longest x3 9.97 us: product(): pl.pallas_call(functools.partial(product_kernel, sz, dist, keys, first, t...]
    unnamed x5 -> x2, local copies, waits for them, and re-layouts: 15.3 us -> 0.01 us
    dot_general x1 -> x0, matrix products: 13.4 us -> none  [masked_product(): jnp.dot(expand_mask(left_part, left_flags), expand_mask(right_part, right...]
  transfers between devices with their start and end apart: 2 -> 23, of which waited for: 1 -> 12; matrix products, arithmetic and copies ran while one was open for 10% -> 0% of each run, Pallas kernels for 0% -> 17%
where the time goes in v1:
time: 77 us; the launch traced here: 76.7 us
  waiting for transfers between devices  31.7 us (41%)
  starting transfers between devices  29.3 us (38%)
  Pallas kernels  15.6 us (20%)
    ppermute x12, waiting for transfers between devices, hop(): return lax.ppermute(chunk, 'row', pairs)  27.5 us
    ppermute x12, starting transfers between devices, hop(): return lax.ppermute(chunk, 'row', pairs)  12.9 us
    pallas_call x3, Pallas kernels, product(): pl.pallas_call(functools.partial(product_kernel, sz, dist, keys, first, t...  9.97 us
    ppermute x4, starting transfers between devices, last_hop(): return lax.ppermute(chunk, ('row', 'col'), pairs)  7.2 us
    ppermute x3, starting transfers between devices, column_sums(): lax.ppermute(pair, 'row', [(q, (q + 2 * t) % sz.n_row) for q in range(sz....  5 us
    ppermute x3, starting transfers between devices, apart(): return lax.ppermute(value, 'col', [(q, q ^ far) for q in range(n_col)])  2.58 us
    ppermute x1, waiting for transfers between devices, column_sums(): lax.ppermute(sums, 'row', [(q, q ^ 1) for q in range(sz.n_row)])  2.03 us
    ppermute x3, waiting for transfers between devices, column_sums(): lax.ppermute(pair, 'row', [(q, (q + 2 * t) % sz.n_row) for q in range(sz....  2.01 us
  transfers between devices with their start and end apart: 23, of which 12 were waited for; matrix products, arithmetic and copies ran while one was open for 0% of the time, Pallas kernels for 17%

profile of v1, /device:TPU:0, one launch (start us, length us, event | category | flops | bytes accessed | tf_op | source)
XLA Modules:
  0.0 76.7 jit_solution(15251038656293488796)
XLA Ops:
  0.0 1.4 %pack_tiles.1 = (bf16[1552,256]{1,0:T(8,128)(2,1)S(1)}, bf16[784,256]{1,0:T(8,128)(2,1)S(1)}, bf16[768,256]{1,0:T(8,128)(2,1)S(1)}) custom-call(s32[2,4]{1,0:T(2,128)} %mask_ref.1, bf16[512,1024]{1,0:T(8,128)(2,1)} %matrix_ref.1), custom_call_target="tpu_custom_call" | custom-call | tf_op jit(solution)/shard_map/pack_tiles/pallas_call | solution.py:87
  1.4 0.5 collective-permute-start.4
  1.9 2.6 %collective-permute-start.2 = (bf16[784,256]{1,0:T(8,128)(2,1)S(1)}, bf16[784,256]{1,0:T(8,128)(2,1)S(1)}, u32[]{:S(2)}, u32[]{:S(2)}) collective-permute-start(bf16[784,256]{1,0:T(8,128)(2,1)S(1)} %get-tuple-element.57.refs_4_), channel_id=1, source_target_pairs={{0,4},{4,12},{12,20},{20,28},{28,24},{24,16},{16,8},{8,0},{1,5},{5... | collective-permute-start | bytes 1204232 | tf_op jit(solution)/shard_map/ppermute | solution.py:392
  4.5 0.1 collective-permute-start.3
  4.6 0.0 collective-permute-done.4.refs_0_
  4.6 2.1 %collective-permute-start.5 = (bf16[1552,256]{1,0:T(8,128)(2,1)S(1)}, bf16[1552,256]{1,0:T(8,128)(2,1)S(1)}, u32[]{:S(2)}, u32[]{:S(2)}) collective-permute-start(bf16[1552,256]{1,0:T(8,128)(2,1)S(1)} %get-tuple-element.47.refs_0_), channel_id=1, source_target_pairs={{0,2},{1,3},{2,0},{3,1},{4,6},{5,7},{6,4},{7,5},{8,10},{9,11},{10,... | collective-permute-start | bytes 2383880 | tf_op jit(solution)/shard_map/ppermute | solution.py:403
  6.7 1.6 %collective-permute-start.1 = (bf16[784,256]{1,0:T(8,128)(2,1)S(1)}, bf16[784,256]{1,0:T(8,128)(2,1)S(1)}, u32[]{:S(2)}, u32[]{:S(2)}) collective-permute-start(bf16[784,256]{1,0:T(8,128)(2,1)S(1)} %get-tuple-element.57.refs_4_), channel_id=1, source_target_pairs={{0,8},{4,0},{12,4},{20,12},{28,20},{24,28},{16,24},{8,16},{1,9},{5... | collective-permute-start | bytes 1204232 | tf_op jit(solution)/shard_map/ppermute | solution.py:392
  8.3 0.4 collective-permute-start
  8.7 7.7 %collective-permute-done.3.refs_9_.refs_11_ = bf16[768,256]{1,0:T(8,128)(2,1)S(1)} collective-permute-done((bf16[768,256]{1,0:T(8,128)(2,1)S(1)}, bf16[768,256]{1,0:T(8,128)(2,1)S(1)}, u32[]{:S(2)}, u32[]{:S(2)}) %collective-permute-start.3) | collective-permute-done | bytes 393248 | tf_op jit(solution)/shard_map/ppermute | solution.py:392
  16.5 1.6 %collective-permute-start.9 = (bf16[784,256]{1,0:T(8,128)(2,1)S(1)}, bf16[784,256]{1,0:T(8,128)(2,1)S(1)}, u32[]{:S(2)}, u32[]{:S(2)}) collective-permute-start(bf16[784,256]{1,0:T(8,128)(2,1)S(1)} %collective-permute-done.2.refs_6_.refs_8_), channel_id=1, source_target_pairs={{0,4},{4,12},{12,20},{20,28},{28,24},{24,16},{16,8},{8,0},{1,5},{5... | collective-permute-start | bytes 1204232 | tf_op jit(solution)/shard_map/ppermute | solution.py:392
  18.0 0.4 collective-permute-start.10
  18.5 0.3 expand_tiles.3.refs_0_
  18.8 0.0 copy-start
  18.8 4.3 %collective-permute-done.refs_7_.refs_9_ = bf16[768,256]{1,0:T(8,128)(2,1)S(1)} collective-permute-done((bf16[768,256]{1,0:T(8,128)(2,1)S(1)}, bf16[768,256]{1,0:T(8,128)(2,1)S(1)}, u32[]{:S(2)}, u32[]{:S(2)}) %collective-permute-start) | collective-permute-done | bytes 393248 | tf_op jit(solution)/shard_map/ppermute | solution.py:392
  23.1 1.9 %collective-permute-done.1.refs_8_.refs_10_ = bf16[784,256]{1,0:T(8,128)(2,1)S(1)} collective-permute-done((bf16[784,256]{1,0:T(8,128)(2,1)S(1)}, bf16[784,256]{1,0:T(8,128)(2,1)S(1)}, u32[]{:S(2)}, u32[]{:S(2)}) %collective-permute-start.1) | collective-permute-done | bytes 401440 | tf_op jit(solution)/shard_map/ppermute | solution.py:392
  25.1 0.1 collective-permute-start.8
  25.2 1.9 %collective-permute-start.7 = (bf16[768,256]{1,0:T(8,128)(2,1)S(1)}, bf16[768,256]{1,0:T(8,128)(2,1)S(1)}, u32[]{:S(2)}, u32[]{:S(2)}) collective-permute-start(bf16[768,256]{1,0:T(8,128)(2,1)S(1)} %collective-permute-done.refs_7_.refs_9_), channel_id=1, source_target_pairs={{0,4},{4,12},{12,20},{20,28},{28,24},{24,16},{16,8},{8,0},{1,5},{5... | collective-permute-start | bytes 1179656 | tf_op jit(solution)/shard_map/ppermute | solution.py:392
  27.1 0.0 collective-permute-done.5.refs_0_
  27.1 0.0 collective-permute-start.6
  27.1 0.3 expand_tiles.4.refs_1_
  27.4 0.6 keep_rows.1.keep_ref
  28.0 5.5 %collective-permute-done.10.refs_7_ = bf16[768,256]{1,0:T(8,128)(2,1)S(1)} collective-permute-done((bf16[768,256]{1,0:T(8,128)(2,1)S(1)}, bf16[768,256]{1,0:T(8,128)(2,1)S(1)}, u32[]{:S(2)}, u32[]{:S(2)}) %collective-permute-start.10) | collective-permute-done | bytes 393248 | tf_op jit(solution)/shard_map/ppermute | solution.py:392
  33.5 1.6 %collective-permute-start.11 = (bf16[784,256]{1,0:T(8,128)(2,1)S(1)}, bf16[784,256]{1,0:T(8,128)(2,1)S(1)}, u32[]{:S(2)}, u32[]{:S(2)}) collective-permute-start(bf16[784,256]{1,0:T(8,128)(2,1)S(1)} %collective-permute-done.9.refs_4_), channel_id=1, source_target_pairs={{0,4},{4,12},{12,20},{20,28},{28,24},{24,16},{16,8},{8,0},{1,5},{5... | collective-permute-start | bytes 1204232 | tf_op jit(solution)/shard_map/ppermute | solution.py:392
  35.1 0.4 collective-permute-start.14
  35.5 4.6 %collective-permute-done.7.refs_5_ = bf16[768,256]{1,0:T(8,128)(2,1)S(1)} collective-permute-done((bf16[768,256]{1,0:T(8,128)(2,1)S(1)}, bf16[768,256]{1,0:T(8,128)(2,1)S(1)}, u32[]{:S(2)}, u32[]{:S(2)}) %collective-permute-start.7) | collective-permute-done | bytes 393248 | tf_op jit(solution)/shard_map/ppermute | solution.py:392
  40.1 1.9 %collective-permute-done.8.refs_6_ = bf16[784,256]{1,0:T(8,128)(2,1)S(1)} collective-permute-done((bf16[784,256]{1,0:T(8,128)(2,1)S(1)}, bf16[784,256]{1,0:T(8,128)(2,1)S(1)}, u32[]{:S(2)}, u32[]{:S(2)}) %collective-permute-start.8) | collective-permute-done | bytes 401440 | tf_op jit(solution)/shard_map/ppermute | solution.py:392
  42.1 1.6 %collective-permute-start.12 = (bf16[768,256]{1,0:T(8,128)(2,1)S(1)}, bf16[768,256]{1,0:T(8,128)(2,1)S(1)}, u32[]{:S(2)}, u32[]{:S(2)}) collective-permute-start(bf16[768,256]{1,0:T(8,128)(2,1)S(1)} %collective-permute-done.7.refs_5_), channel_id=1, source_target_pairs={{0,4},{4,12},{12,20},{20,28},{28,24},{24,16},{16,8},{8,0},{1,5},{5... | collective-permute-start | bytes 1179656 | tf_op jit(solution)/shard_map/ppermute | solution.py:392
  43.7 0.4 collective-permute-start.13
  44.1 0.7 expand_tiles.5
  44.8 4.2 %product.3.refs_12_ = f32[512,1024]{1,0:T(8,128)S(1)} custom-call(bf16[512,1024]{1,0:T(8,128)(2,1)S(1)} %expand_tiles.3.refs_0_, bf16[512,1024]{1,0:T(8,128)(2,1)S(1)} %expand_tiles.4.refs_1_, bf16[512,1024]{1,0:T(8,128)(2,1)S(1)} %get-tuple-element.55.refs_2_, bf16[512,1024]{1,0:T(8,128)(2,1)S(1)} %get-tuple-element.56.refs_3_, ...), custom_call_target="tpu_custom_call" | custom-call | flops 536870912 | tf_op jit(solution)/shard_map/product/pallas_call | solution.py:243
  49.0 1.5 %collective-permute-done.14.refs_7_ = bf16[768,256]{1,0:T(8,128)(2,1)S(1)} collective-permute-done((bf16[768,256]{1,0:T(8,128)(2,1)S(1)}, bf16[768,256]{1,0:T(8,128)(2,1)S(1)}, u32[]{:S(2)}, u32[]{:S(2)}) %collective-permute-start.14) | collective-permute-done | bytes 393248 | tf_op jit(solution)/shard_map/ppermute | solution.py:392
  50.5 3.5 %collective-permute-start.15 = (bf16[784,256]{1,0:T(8,128)(2,1)S(1)}, bf16[784,256]{1,0:T(8,128)(2,1)S(1)}, u32[]{:S(2)}, u32[]{:S(2)}) collective-permute-start(bf16[784,256]{1,0:T(8,128)(2,1)S(1)} %collective-permute-done.11.refs_4_), channel_id=1, source_target_pairs={{0,4},{1,1},{2,6},{3,3},{4,12},{5,5},{6,14},{7,7},{12,20},{13,13},... | collective-permute-start | bytes 1204232 | tf_op jit(solution)/shard_map/ppermute | solution.py:400
  54.0 2.4 %collective-permute-start.16 = (bf16[768,256]{1,0:T(8,128)(2,1)S(1)}, bf16[768,256]{1,0:T(8,128)(2,1)S(1)}, u32[]{:S(2)}, u32[]{:S(2)}) collective-permute-start(bf16[768,256]{1,0:T(8,128)(2,1)S(1)} %collective-permute-done.14.refs_7_), channel_id=1, source_target_pairs={{0,8},{1,1},{2,10},{3,3},{4,0},{5,5},{6,2},{7,7},{12,4},{13,13},{1... | collective-permute-start | bytes 1179656 | tf_op jit(solution)/shard_map/ppermute | solution.py:400
  56.4 2.9 %product.4.refs_8_ = f32[512,1024]{1,0:T(8,128)S(1)} custom-call(bf16[512,1024]{1,0:T(8,128)(2,1)S(1)} %expand_tiles.3.refs_0_, bf16[512,1024]{1,0:T(8,128)(2,1)S(1)} %expand_tiles.4.refs_1_, bf16[512,1024]{1,0:T(8,128)(2,1)S(1)} %get-tuple-element.55.refs_2_, bf16[512,1024]{1,0:T(8,128)(2,1)S(1)} %get-tuple-element.56.refs_3_, ...), custom_call_target="tpu_custom_call" | custom-call | flops 536870912 | tf_op jit(solution)/shard_map/product/pallas_call | solution.py:243
  59.2 0.7 collective-permute-start.17
  59.9 0.7 collective-permute-start.18
  60.6 2.9 %product.5 = (f32[512,1024]{1,0:T(8,128)S(1)}, bf16[512,512]{1,0:T(8,128)(2,1)S(1)}) custom-call(bf16[512,1024]{1,0:T(8,128)(2,1)S(1)} %expand_tiles.3.refs_0_, bf16[512,1024]{1,0:T(8,128)(2,1)S(1)} %expand_tiles.4.refs_1_, bf16[512,1024]{1,0:T(8,128)(2,1)S(1)} %get-tuple-element.55.refs_2_, bf16[512,1024]{1,0:T(8,128)(2,1)S(1)} %get-tuple-element.56.refs_3_, ...), custom_call_target="tpu_custom_call" | custom-call | flops 536870912 | tf_op jit(solution)/shard_map/product/pallas_call | solution.py:243
  63.6 0.1 collective-permute-done.16.refs_1_
  63.7 0.9 %product_last.2 = (f32[512,1024]{1,0:T(8,128)S(1)}, f32[1,1024]{1,0:T(1,128)S(1)}) custom-call(f32[16,1024]{1,0:T(8,128)S(1)} %keep_rows.1.keep_ref, bf16[512,512]{1,0:T(8,128)(2,1)S(1)} %get-tuple-element.61.left_ref, bf16[784,256]{1,0:T(8,128)(2,1)S(1)} %collective-permute-done.15.refs_0_, bf16[768,256]{1,0:T(8,128)(2,1)S(1)} %collective-permute-done.16.refs_1_, ...), custom_call_target="tpu_custom_call" | custom-call | flops 536870912 | tf_op jit(solution)/shard_map/product_last/pallas_call | solution.py:316
  64.6 1.6 %collective-permute-start.19 = (f32[1,1024]{1,0:T(1,128)S(1)}, f32[1,1024]{1,0:T(1,128)S(1)}, u32[]{:S(2)}, u32[]{:S(2)}) collective-permute-start(f32[1,1024]{1,0:T(1,128)S(1)} %get-tuple-element.68), channel_id=1, source_target_pairs={{0,4},{4,0},{8,12},{12,8},{16,20},{20,16},{24,28},{28,24},{1,5},{5... | collective-permute-start | bytes 12296 | tf_op jit(solution)/shard_map/ppermute | solution.py:371
  66.3 2.0 %collective-permute-done.19 = f32[1,1024]{1,0:T(1,128)S(1)} collective-permute-done((f32[1,1024]{1,0:T(1,128)S(1)}, f32[1,1024]{1,0:T(1,128)S(1)}, u32[]{:S(2)}, u32[]{:S(2)}) %collective-permute-start.19) | collective-permute-done | bytes 4128 | tf_op jit(solution)/shard_map/ppermute | solution.py:371
  68.3 1.1 %collective-permute-start.20 = (f32[1,1024]{1,0:T(1,128)S(1)}, f32[1,1024]{1,0:T(1,128)S(1)}, u32[]{:S(2)}, u32[]{:S(2)}) collective-permute-start(f32[1,1024]{1,0:T(1,128)S(1)} %add.12), channel_id=1, source_target_pairs={{0,8},{4,12},{8,16},{12,20},{16,24},{20,28},{24,0},{28,4},{1,9},{5... | collective-permute-start | bytes 12296 | tf_op jit(solution)/shard_map/ppermute | solution.py:373
  69.4 2.3 %collective-permute-start.21 = (f32[1,1024]{1,0:T(1,128)S(1)}, f32[1,1024]{1,0:T(1,128)S(1)}, u32[]{:S(2)}, u32[]{:S(2)}) collective-permute-start(f32[1,1024]{1,0:T(1,128)S(1)} %add.12), channel_id=1, source_target_pairs={{0,16},{4,20},{8,24},{12,28},{16,0},{20,4},{24,8},{28,12},{1,17},{... | collective-permute-start | bytes 12296 | tf_op jit(solution)/shard_map/ppermute | solution.py:373
  71.7 1.6 %collective-permute-start.22 = (f32[1,1024]{1,0:T(1,128)S(1)}, f32[1,1024]{1,0:T(1,128)S(1)}, u32[]{:S(2)}, u32[]{:S(2)}) collective-permute-start(f32[1,1024]{1,0:T(1,128)S(1)} %add.12), channel_id=1, source_target_pairs={{0,24},{4,28},{8,0},{12,4},{16,8},{20,12},{24,16},{28,20},{1,25},{... | collective-permute-start | bytes 12296 | tf_op jit(solution)/shard_map/ppermute | solution.py:373
  73.3 0.4 collective-permute-done.20
  73.7 0.2 collective-permute-done.21
  73.9 1.4 %collective-permute-done.22 = f32[1,1024]{1,0:T(1,128)S(1)} collective-permute-done((f32[1,1024]{1,0:T(1,128)S(1)}, f32[1,1024]{1,0:T(1,128)S(1)}, u32[]{:S(2)}, u32[]{:S(2)}) %collective-permute-start.22) | collective-permute-done | bytes 4128 | tf_op jit(solution)/shard_map/ppermute | solution.py:373
  75.3 1.4 %scale.1 = f32[512,1024]{1,0:T(8,128)} custom-call(f32[512,1024]{1,0:T(8,128)S(1)} %get-tuple-element.63.first_ref, f32[512,1024]{1,0:T(8,128)S(1)} %get-tuple-element.67.second_ref, f32[1,1024]{1,0:T(1,128)S(1)} %add_add_fusion.totals_ref), custom_call_target="tpu_custom_call" | custom-call | flops 536870912 | tf_op jit(solution)/shard_map/scale/pallas_call | solution.py:353
  (13 shorter events, 0.1 us)
Async XLA Ops:
  1.4 3.2 %collective-permute-start.4 = (bf16[1552,256]{1,0:T(8,128)(2,1)S(1)}, bf16[1552,256]{1,0:T(8,128)(2,1)S(1)}, u32[]{:S(2)}, u32[]{:S(2)}) collective-permute-start(bf16[1552,256]{1,0:T(8,128)(2,1)S(1)} %get-tuple-element.47.refs_0_), channel_id=1, source_target_pairs={{0,1},{1,0},{2,3},{3,2},{4,5},{5,4},{6,7},{7,6},{8,9},{9,8},{10,11... | collective-permute-start | bytes 2383880 | tf_op jit(solution)/shard_map/ppermute | solution.py:403
  1.9 14.5 %collective-permute-start.2 = (bf16[784,256]{1,0:T(8,128)(2,1)S(1)}, bf16[784,256]{1,0:T(8,128)(2,1)S(1)}, u32[]{:S(2)}, u32[]{:S(2)}) collective-permute-start(bf16[784,256]{1,0:T(8,128)(2,1)S(1)} %get-tuple-element.57.refs_4_), channel_id=1, source_target_pairs={{0,4},{4,12},{12,20},{20,28},{28,24},{24,16},{16,8},{8,0},{1,5},{5... | collective-permute-start | bytes 1204232 | tf_op jit(solution)/shard_map/ppermute | solution.py:392
  4.5 12.0 %collective-permute-start.3 = (bf16[768,256]{1,0:T(8,128)(2,1)S(1)}, bf16[768,256]{1,0:T(8,128)(2,1)S(1)}, u32[]{:S(2)}, u32[]{:S(2)}) collective-permute-start(bf16[768,256]{1,0:T(8,128)(2,1)S(1)} %get-tuple-element.37.refs_5_), channel_id=1, source_target_pairs={{0,8},{4,0},{12,4},{20,12},{28,20},{24,28},{16,24},{8,16},{1,9},{5... | collective-permute-start | bytes 1179656 | tf_op jit(solution)/shard_map/ppermute | solution.py:392
  4.6 22.4 %collective-permute-start.5 = (bf16[1552,256]{1,0:T(8,128)(2,1)S(1)}, bf16[1552,256]{1,0:T(8,128)(2,1)S(1)}, u32[]{:S(2)}, u32[]{:S(2)}) collective-permute-start(bf16[1552,256]{1,0:T(8,128)(2,1)S(1)} %get-tuple-element.47.refs_0_), channel_id=1, source_target_pairs={{0,2},{1,3},{2,0},{3,1},{4,6},{5,7},{6,4},{7,5},{8,10},{9,11},{10,... | collective-permute-start | bytes 2383880 | tf_op jit(solution)/shard_map/ppermute | solution.py:403
  6.7 18.4 %collective-permute-start.1 = (bf16[784,256]{1,0:T(8,128)(2,1)S(1)}, bf16[784,256]{1,0:T(8,128)(2,1)S(1)}, u32[]{:S(2)}, u32[]{:S(2)}) collective-permute-start(bf16[784,256]{1,0:T(8,128)(2,1)S(1)} %get-tuple-element.57.refs_4_), channel_id=1, source_target_pairs={{0,8},{4,0},{12,4},{20,12},{28,20},{24,28},{16,24},{8,16},{1,9},{5... | collective-permute-start | bytes 1204232 | tf_op jit(solution)/shard_map/ppermute | solution.py:392
  8.3 14.8 %collective-permute-start = (bf16[768,256]{1,0:T(8,128)(2,1)S(1)}, bf16[768,256]{1,0:T(8,128)(2,1)S(1)}, u32[]{:S(2)}, u32[]{:S(2)}) collective-permute-start(bf16[768,256]{1,0:T(8,128)(2,1)S(1)} %get-tuple-element.37.refs_5_), channel_id=1, source_target_pairs={{0,4},{4,12},{12,20},{20,28},{28,24},{24,16},{16,8},{8,0},{1,5},{5... | collective-permute-start | bytes 1179656 | tf_op jit(solution)/shard_map/ppermute | solution.py:392
  16.5 17.0 %collective-permute-start.9 = (bf16[784,256]{1,0:T(8,128)(2,1)S(1)}, bf16[784,256]{1,0:T(8,128)(2,1)S(1)}, u32[]{:S(2)}, u32[]{:S(2)}) collective-permute-start(bf16[784,256]{1,0:T(8,128)(2,1)S(1)} %collective-permute-done.2.refs_6_.refs_8_), channel_id=1, source_target_pairs={{0,4},{4,12},{12,20},{20,28},{28,24},{24,16},{16,8},{8,0},{1,5},{5... | collective-permute-start | bytes 1204232 | tf_op jit(solution)/shard_map/ppermute | solution.py:392
  18.0 15.4 %collective-permute-start.10 = (bf16[768,256]{1,0:T(8,128)(2,1)S(1)}, bf16[768,256]{1,0:T(8,128)(2,1)S(1)}, u32[]{:S(2)}, u32[]{:S(2)}) collective-permute-start(bf16[768,256]{1,0:T(8,128)(2,1)S(1)} %collective-permute-done.3.refs_9_.refs_11_), channel_id=1, source_target_pairs={{0,8},{4,0},{12,4},{20,12},{28,20},{24,28},{16,24},{8,16},{1,9},{5... | collective-permute-start | bytes 1179656 | tf_op jit(solution)/shard_map/ppermute | solution.py:392
  18.8 8.6 %copy-start = (s32[2,4]{1,0:T(2,128)S(1)}, s32[2,4]{1,0:T(2,128)}, u32[]{:S(2)}) copy-start(s32[2,4]{1,0:T(2,128)} %out_mask_ref) | copy-start | bytes 100
  25.1 17.0 %collective-permute-start.8 = (bf16[784,256]{1,0:T(8,128)(2,1)S(1)}, bf16[784,256]{1,0:T(8,128)(2,1)S(1)}, u32[]{:S(2)}, u32[]{:S(2)}) collective-permute-start(bf16[784,256]{1,0:T(8,128)(2,1)S(1)} %collective-permute-done.1.refs_8_.refs_10_), channel_id=1, source_target_pairs={{0,8},{4,0},{12,4},{20,12},{28,20},{24,28},{16,24},{8,16},{1,9},{5... | collective-permute-start | bytes 1204232 | tf_op jit(solution)/shard_map/ppermute | solution.py:392
  25.2 15.0 %collective-permute-start.7 = (bf16[768,256]{1,0:T(8,128)(2,1)S(1)}, bf16[768,256]{1,0:T(8,128)(2,1)S(1)}, u32[]{:S(2)}, u32[]{:S(2)}) collective-permute-start(bf16[768,256]{1,0:T(8,128)(2,1)S(1)} %collective-permute-done.refs_7_.refs_9_), channel_id=1, source_target_pairs={{0,4},{4,12},{12,20},{20,28},{28,24},{24,16},{16,8},{8,0},{1,5},{5... | collective-permute-start | bytes 1179656 | tf_op jit(solution)/shard_map/ppermute | solution.py:392
  27.1 17.0 %collective-permute-start.6 = (bf16[1552,256]{1,0:T(8,128)(2,1)S(1)}, bf16[1552,256]{1,0:T(8,128)(2,1)S(1)}, u32[]{:S(2)}, u32[]{:S(2)}) collective-permute-start(bf16[1552,256]{1,0:T(8,128)(2,1)S(1)} %collective-permute-done.5.refs_0_), channel_id=1, source_target_pairs={{0,1},{1,0},{2,3},{3,2},{4,5},{5,4},{6,7},{7,6},{8,9},{9,8},{10,11... | collective-permute-start | bytes 2383880 | tf_op jit(solution)/shard_map/ppermute | solution.py:403
  33.5 17.0 %collective-permute-start.11 = (bf16[784,256]{1,0:T(8,128)(2,1)S(1)}, bf16[784,256]{1,0:T(8,128)(2,1)S(1)}, u32[]{:S(2)}, u32[]{:S(2)}) collective-permute-start(bf16[784,256]{1,0:T(8,128)(2,1)S(1)} %collective-permute-done.9.refs_4_), channel_id=1, source_target_pairs={{0,4},{4,12},{12,20},{20,28},{28,24},{24,16},{16,8},{8,0},{1,5},{5... | collective-permute-start | bytes 1204232 | tf_op jit(solution)/shard_map/ppermute | solution.py:392
  35.1 15.4 %collective-permute-start.14 = (bf16[768,256]{1,0:T(8,128)(2,1)S(1)}, bf16[768,256]{1,0:T(8,128)(2,1)S(1)}, u32[]{:S(2)}, u32[]{:S(2)}) collective-permute-start(bf16[768,256]{1,0:T(8,128)(2,1)S(1)} %collective-permute-done.10.refs_7_), channel_id=1, source_target_pairs={{0,8},{4,0},{12,4},{20,12},{28,20},{24,28},{16,24},{8,16},{1,9},{5... | collective-permute-start | bytes 1179656 | tf_op jit(solution)/shard_map/ppermute | solution.py:392
  42.1 17.9 %collective-permute-start.12 = (bf16[768,256]{1,0:T(8,128)(2,1)S(1)}, bf16[768,256]{1,0:T(8,128)(2,1)S(1)}, u32[]{:S(2)}, u32[]{:S(2)}) collective-permute-start(bf16[768,256]{1,0:T(8,128)(2,1)S(1)} %collective-permute-done.7.refs_5_), channel_id=1, source_target_pairs={{0,4},{4,12},{12,20},{20,28},{28,24},{24,16},{16,8},{8,0},{1,5},{5... | collective-permute-start | bytes 1179656 | tf_op jit(solution)/shard_map/ppermute | solution.py:392
  43.7 17.0 %collective-permute-start.13 = (bf16[784,256]{1,0:T(8,128)(2,1)S(1)}, bf16[784,256]{1,0:T(8,128)(2,1)S(1)}, u32[]{:S(2)}, u32[]{:S(2)}) collective-permute-start(bf16[784,256]{1,0:T(8,128)(2,1)S(1)} %collective-permute-done.8.refs_6_), channel_id=1, source_target_pairs={{0,8},{4,0},{12,4},{20,12},{28,20},{24,28},{16,24},{8,16},{1,9},{5... | collective-permute-start | bytes 1204232 | tf_op jit(solution)/shard_map/ppermute | solution.py:392
  50.5 13.2 %collective-permute-start.15 = (bf16[784,256]{1,0:T(8,128)(2,1)S(1)}, bf16[784,256]{1,0:T(8,128)(2,1)S(1)}, u32[]{:S(2)}, u32[]{:S(2)}) collective-permute-start(bf16[784,256]{1,0:T(8,128)(2,1)S(1)} %collective-permute-done.11.refs_4_), channel_id=1, source_target_pairs={{0,4},{1,1},{2,6},{3,3},{4,12},{5,5},{6,14},{7,7},{12,20},{13,13},... | collective-permute-start | bytes 1204232 | tf_op jit(solution)/shard_map/ppermute | solution.py:400
  54.0 9.7 %collective-permute-start.16 = (bf16[768,256]{1,0:T(8,128)(2,1)S(1)}, bf16[768,256]{1,0:T(8,128)(2,1)S(1)}, u32[]{:S(2)}, u32[]{:S(2)}) collective-permute-start(bf16[768,256]{1,0:T(8,128)(2,1)S(1)} %collective-permute-done.14.refs_7_), channel_id=1, source_target_pairs={{0,8},{1,1},{2,10},{3,3},{4,0},{5,5},{6,2},{7,7},{12,4},{13,13},{1... | collective-permute-start | bytes 1179656 | tf_op jit(solution)/shard_map/ppermute | solution.py:400
  59.2 5.3 %collective-permute-start.17 = (bf16[784,256]{1,0:T(8,128)(2,1)S(1)}, bf16[784,256]{1,0:T(8,128)(2,1)S(1)}, u32[]{:S(2)}, u32[]{:S(2)}) collective-permute-start(bf16[784,256]{1,0:T(8,128)(2,1)S(1)} %collective-permute-done.11.refs_4_), channel_id=1, source_target_pairs={{0,0},{1,5},{2,2},{3,7},{4,4},{5,13},{6,6},{7,15},{12,12},{13,21},... | collective-permute-start | bytes 1204232 | tf_op jit(solution)/shard_map/ppermute | solution.py:400
  59.9 4.6 %collective-permute-start.18 = (bf16[768,256]{1,0:T(8,128)(2,1)S(1)}, bf16[768,256]{1,0:T(8,128)(2,1)S(1)}, u32[]{:S(2)}, u32[]{:S(2)}) collective-permute-start(bf16[768,256]{1,0:T(8,128)(2,1)S(1)} %collective-permute-done.14.refs_7_), channel_id=1, source_target_pairs={{0,0},{1,9},{2,2},{3,11},{4,4},{5,1},{6,6},{7,3},{12,12},{13,5},{1... | collective-permute-start | bytes 1179656 | tf_op jit(solution)/shard_map/ppermute | solution.py:400
  64.6 3.7 %collective-permute-start.19 = (f32[1,1024]{1,0:T(1,128)S(1)}, f32[1,1024]{1,0:T(1,128)S(1)}, u32[]{:S(2)}, u32[]{:S(2)}) collective-permute-start(f32[1,1024]{1,0:T(1,128)S(1)} %get-tuple-element.68), channel_id=1, source_target_pairs={{0,4},{4,0},{8,12},{12,8},{16,20},{20,16},{24,28},{28,24},{1,5},{5... | collective-permute-start | bytes 12296 | tf_op jit(solution)/shard_map/ppermute | solution.py:371
  68.3 5.4 %collective-permute-start.20 = (f32[1,1024]{1,0:T(1,128)S(1)}, f32[1,1024]{1,0:T(1,128)S(1)}, u32[]{:S(2)}, u32[]{:S(2)}) collective-permute-start(f32[1,1024]{1,0:T(1,128)S(1)} %add.12), channel_id=1, source_target_pairs={{0,8},{4,12},{8,16},{12,20},{16,24},{20,28},{24,0},{28,4},{1,9},{5... | collective-permute-start | bytes 12296 | tf_op jit(solution)/shard_map/ppermute | solution.py:373
  69.4 4.5 %collective-permute-start.21 = (f32[1,1024]{1,0:T(1,128)S(1)}, f32[1,1024]{1,0:T(1,128)S(1)}, u32[]{:S(2)}, u32[]{:S(2)}) collective-permute-start(f32[1,1024]{1,0:T(1,128)S(1)} %add.12), channel_id=1, source_target_pairs={{0,16},{4,20},{8,24},{12,28},{16,0},{20,4},{24,8},{28,12},{1,17},{... | collective-permute-start | bytes 12296 | tf_op jit(solution)/shard_map/ppermute | solution.py:373
  71.7 3.6 %collective-permute-start.22 = (f32[1,1024]{1,0:T(1,128)S(1)}, f32[1,1024]{1,0:T(1,128)S(1)}, u32[]{:S(2)}, u32[]{:S(2)}) collective-permute-start(f32[1,1024]{1,0:T(1,128)S(1)} %add.12), channel_id=1, source_target_pairs={{0,24},{4,28},{8,0},{12,4},{16,8},{20,12},{24,16},{28,20},{1,25},{... | collective-permute-start | bytes 12296 | tf_op jit(solution)/shard_map/ppermute | solution.py:373

commit v2 on v1

--- a/solution.py
+++ b/solution.py
@@ -176,7 +176,7 @@
     pays = [[refs.pop(0) for _ in sz.chunks] for _ in keys]
     before_ref = None if first else refs.pop(0)
     out_ref = refs.pop(0)
-    then_ref = None if then is None else refs.pop(0)
+    then_refs = [refs.pop(0) for _ in then]
     buf, left, sems = refs
     per_piece = len(sz.chunks) + 1
 
@@ -215,18 +215,18 @@
             begin(p, key)
         else:
             pl.when(on_core(core))(functools.partial(begin, p, key))
-    if then is not None:
-        start_left(sz, dist, blocks, then, then_ref, sems.at[len(keys) * per_piece])
+    for t, (key, ref) in enumerate(zip(then, then_refs)):
+        start_left(sz, dist, blocks, key, ref, sems.at[len(keys) * per_piece + t])
     for p, (key, core) in enumerate(keys):
         if core is None:
             add(p)
         else:
             pl.when(on_core(core))(functools.partial(add, p))
-    if then is not None:
-        wait_left(sz, blocks, then_ref, sems.at[len(keys) * per_piece])
-
-
-def product(sz, before, dist, blocks, pieces, keys, then=None):
+    for t, ref in enumerate(then_refs):
+        wait_left(sz, blocks, ref, sems.at[len(keys) * per_piece + t])
+
+
+def product(sz, before, dist, blocks, pieces, keys, then=()):
     n = len(keys)
     first = before is None
     vmem = pl.BlockSpec(memory_space=pltpu.VMEM)
@@ -238,8 +238,7 @@
         in_specs.append(vmem)
         args.append(before)
     out_shape = [jax.ShapeDtypeStruct((sz.rows, sz.cols), jnp.float32)]
-    if then is not None:
-        out_shape.append(jax.ShapeDtypeStruct((sz.rows, sz.rows), jnp.bfloat16))
+    out_shape += [jax.ShapeDtypeStruct((sz.rows, sz.rows), jnp.bfloat16)] * len(then)
     return pl.pallas_call(
         functools.partial(product_kernel, sz, dist, keys, first, then),
         out_shape=out_shape,
@@ -248,11 +247,50 @@
         scratch_shapes=[
             pltpu.VMEM((n, sz.buf_rows, sz.tile), jnp.bfloat16),
             pltpu.VMEM((n, sz.rows, sz.rows), jnp.bfloat16),
-            pltpu.SemaphoreType.DMA((n * (len(sz.chunks) + 1) + 1,)),
+            pltpu.SemaphoreType.DMA((n * (len(sz.chunks) + 1) + max(1, len(then)),)),
         ],
         compiler_params=pltpu.CompilerParams(vmem_limit_bytes=VMEM_LIMIT),
         cost_estimate=cost(),
         name="product",
+    )(*args)
+
+
+def near_kernel(sz, n, *refs):
+    refs = list(refs)
+    lefts = [refs.pop(0) for _ in range(n)]
+    pays = [[refs.pop(0) for _ in sz.chunks] for _ in range(n)]
+    before_ref, out_ref, buf = refs
+    slots = []
+    for p in range(n):
+        for ref, chunk in zip(pays[p], sz.chunks):
+            buf[p, pl.ds(*chunk), :] = ref[...]
+        buf[p, sz.pay_rows :, :] = jnp.zeros((sz.tile, sz.tile), jnp.bfloat16)
+        slots.append(slots_of(sz, buf[p, 0:CODE_ROWS, 0:128]))
+    for b in range(sz.tc):
+        cols = slice(b * sz.tile, (b + 1) * sz.tile)
+        total = before_ref[:, cols]
+        for p in range(n):
+            total = total + jnp.dot(
+                lefts[p][...],
+                load_right(sz, buf.at[p], slots[p], b),
+                preferred_element_type=jnp.float32,
+            )
+        out_ref[:, cols] = total
+
+
+def near_product(sz, before, lefts, pieces):
+    n = len(pieces)
+    args = [*lefts, *(chunk for piece in pieces for chunk in piece), before]
+    vmem = pl.BlockSpec(memory_space=pltpu.VMEM)
+    return pl.pallas_call(
+        functools.partial(near_kernel, sz, n),
+        out_shape=jax.ShapeDtypeStruct((sz.rows, sz.cols), jnp.float32),
+        in_specs=[vmem] * len(args),
+        out_specs=vmem,
+        scratch_shapes=[pltpu.VMEM((n, sz.buf_rows, sz.tile), jnp.bfloat16)],
+        compiler_params=pltpu.CompilerParams(vmem_limit_bytes=VMEM_LIMIT),
+        cost_estimate=cost(),
+        name="product_near",
     )(*args)
 
 
@@ -331,7 +369,7 @@
 def scale_kernel(sz, steps, first_ref, second_ref, totals_ref, flow_ref, buf, sems):
     total_rows = float(sz.rows * sz.n_row)
     size = sz.rows // steps
-    totals = totals_ref[...]
+    share = 1.0 / totals_ref[...]
     copies = []
     for s in range(steps):
         rows = pl.ds(s * size, size)
@@ -339,7 +377,7 @@
 
             @pl.when(lax.axis_index("col") % 2 == core)
             def _():
-                buf[rows, :] = total_rows * ref[rows, :] / totals
+                buf[rows, :] = (total_rows * ref[rows, :]) * share
 
         copies.append(pltpu.make_async_copy(buf.at[rows], flow_ref.at[rows], sems.at[s]))
         copies[-1].start()
@@ -418,7 +456,7 @@
         send(1, h, [own[lead[way] ^ h] for way in (1, -1)])
     far = n_col // 2
     blocks, dense = {0: whole, 1: apart(whole, 1)}, {}
-    acc, more, gate = None, [], []
+    acc, lefts, gate = None, [], []
     for i, (step, h) in enumerate(arrivals[:-1]):
         here = after(arrived(step, h), *gate)
         if i + 3 < len(arrivals):
@@ -461,15 +499,18 @@
             keys = [(step, None), (-step, None)]
         if keys:
             dist = sorted(dense)
-            then = half if keys[0][0] == half - 1 else None
             chunks = [list(pieces[key]) for key, _ in keys]
             (chunks[0][0],) = after([chunks[0][0]], *here)
-            acc, *more = product(sz, acc, dist, [dense[d] for d in dist], chunks, keys, then)
+            if keys[0][0] == half - 1:
+                acc = near_product(sz, acc, lefts[:2], chunks)
+            else:
+                then = (half - 1, 1 - half, half) if keys[0][0] == half - 2 else ()
+                acc, *lefts = product(sz, acc, dist, [dense[d] for d in dist], chunks, keys, then)
             gate.append(acc)
         if i + 3 == len(arrivals):
             final = after(final, acc)
             second = [last_hop(chunk, way, 1) for chunk, way in zip(final, (1, -1))]
-    (left,) = more
+    left = lefts[2]
     mine, sums = last_product(sz, 0, acc, left, first, keep)
     other, sums = last_product(sz, 1, acc, left, second, keep, sums)
     return scale(sz, mine, other, column_sums(sz, sums))

time: 77 us -> 77.6 us (level); the launches traced: 76.7 us -> 76.4 us
  waiting for transfers between devices: 31.7 us -> 33.2 us
  Pallas kernels: 15.6 us -> 14.4 us
    pallas_call x3 -> x2, Pallas kernels: 9.97 us -> 7.37 us  [product(): pl.pallas_call(functools.partial(product_kernel, sz, dist, keys, first, t...]
    pallas_call x0 -> x1, Pallas kernels: none -> 1.43 us  [near_product(): pl.pallas_call(functools.partial(near_kernel, sz, n), out_shape=jax.Shape...]
    ppermute x4, waiting for transfers between devices: 0.11 us -> 1.28 us  [last_hop(): return lax.ppermute(chunk, ('row', 'col'), pairs)]
  transfers between devices with their start and end apart: 23 -> 23, of which waited for: 12 -> 12; matrix products, arithmetic and copies ran while one was open for 0% -> 0% of each run, Pallas kernels for 17% -> 15%
where the time goes in v2:
time: 77.6 us; the launch traced here: 76.4 us
  waiting for transfers between devices  33.2 us (43%)
  starting transfers between devices  28.6 us (37%)
  Pallas kernels  14.4 us (19%)
    ppermute x12, waiting for transfers between devices, hop(): return lax.ppermute(chunk, 'row', pairs)  27.5 us
    ppermute x12, starting transfers between devices, hop(): return lax.ppermute(chunk, 'row', pairs)  12.9 us
    pallas_call x2, Pallas kernels, product(): pl.pallas_call(functools.partial(product_kernel, sz, dist, keys, first, t...  7.37 us
    ppermute x4, starting transfers between devices, last_hop(): return lax.ppermute(chunk, ('row', 'col'), pairs)  7.2 us
    ppermute x3, starting transfers between devices, column_sums(): lax.ppermute(pair, 'row', [(q, (q + 2 * t) % sz.n_row) for q in range(sz....  4.32 us
    ppermute x3, starting transfers between devices, apart(): return lax.ppermute(value, 'col', [(q, q ^ far) for q in range(n_col)])  2.58 us
    ppermute x3, waiting for transfers between devices, column_sums(): lax.ppermute(pair, 'row', [(q, (q + 2 * t) % sz.n_row) for q in range(sz....  2.26 us
    ppermute x1, waiting for transfers between devices, column_sums(): lax.ppermute(sums, 'row', [(q, q ^ 1) for q in range(sz.n_row)])  2.11 us
  transfers between devices with their start and end apart: 23, of which 12 were waited for; matrix products, arithmetic and copies ran while one was open for 0% of the time, Pallas kernels for 15%

profile of v2, /device:TPU:0, one launch (start us, length us, event | category | flops | bytes accessed | tf_op | source)
XLA Modules:
  0.0 76.4 jit_solution(18160554126996744334)
XLA Ops:
  0.0 1.4 %pack_tiles.1 = (bf16[1552,256]{1,0:T(8,128)(2,1)S(1)}, bf16[784,256]{1,0:T(8,128)(2,1)S(1)}, bf16[768,256]{1,0:T(8,128)(2,1)S(1)}) custom-call(s32[2,4]{1,0:T(2,128)} %mask_ref.1, bf16[512,1024]{1,0:T(8,128)(2,1)} %matrix_ref.1), custom_call_target="tpu_custom_call" | custom-call | tf_op jit(solution)/shard_map/pack_tiles/pallas_call | solution.py:87
  1.4 0.5 collective-permute-start.4
  1.9 2.6 %collective-permute-start.2 = (bf16[784,256]{1,0:T(8,128)(2,1)S(1)}, bf16[784,256]{1,0:T(8,128)(2,1)S(1)}, u32[]{:S(2)}, u32[]{:S(2)}) collective-permute-start(bf16[784,256]{1,0:T(8,128)(2,1)S(1)} %get-tuple-element.59.refs_4_), channel_id=1, source_target_pairs={{0,4},{4,12},{12,20},{20,28},{28,24},{24,16},{16,8},{8,0},{1,5},{5... | collective-permute-start | bytes 1204232 | tf_op jit(solution)/shard_map/ppermute | solution.py:430
  4.5 0.1 collective-permute-start.3
  4.6 0.0 collective-permute-done.4.refs_0_
  4.6 2.1 %collective-permute-start.5 = (bf16[1552,256]{1,0:T(8,128)(2,1)S(1)}, bf16[1552,256]{1,0:T(8,128)(2,1)S(1)}, u32[]{:S(2)}, u32[]{:S(2)}) collective-permute-start(bf16[1552,256]{1,0:T(8,128)(2,1)S(1)} %get-tuple-element.49.refs_0_), channel_id=1, source_target_pairs={{0,2},{1,3},{2,0},{3,1},{4,6},{5,7},{6,4},{7,5},{8,10},{9,11},{10,... | collective-permute-start | bytes 2383880 | tf_op jit(solution)/shard_map/ppermute | solution.py:441
  6.7 1.6 %collective-permute-start.1 = (bf16[784,256]{1,0:T(8,128)(2,1)S(1)}, bf16[784,256]{1,0:T(8,128)(2,1)S(1)}, u32[]{:S(2)}, u32[]{:S(2)}) collective-permute-start(bf16[784,256]{1,0:T(8,128)(2,1)S(1)} %get-tuple-element.59.refs_4_), channel_id=1, source_target_pairs={{0,8},{4,0},{12,4},{20,12},{28,20},{24,28},{16,24},{8,16},{1,9},{5... | collective-permute-start | bytes 1204232 | tf_op jit(solution)/shard_map/ppermute | solution.py:430
  8.3 0.4 collective-permute-start
  8.7 7.7 %collective-permute-done.3.refs_9_.refs_11_ = bf16[768,256]{1,0:T(8,128)(2,1)S(1)} collective-permute-done((bf16[768,256]{1,0:T(8,128)(2,1)S(1)}, bf16[768,256]{1,0:T(8,128)(2,1)S(1)}, u32[]{:S(2)}, u32[]{:S(2)}) %collective-permute-start.3) | collective-permute-done | bytes 393248 | tf_op jit(solution)/shard_map/ppermute | solution.py:430
  16.4 0.0 collective-permute-done.2.refs_6_.refs_8_
  16.5 1.6 %collective-permute-start.9 = (bf16[784,256]{1,0:T(8,128)(2,1)S(1)}, bf16[784,256]{1,0:T(8,128)(2,1)S(1)}, u32[]{:S(2)}, u32[]{:S(2)}) collective-permute-start(bf16[784,256]{1,0:T(8,128)(2,1)S(1)} %collective-permute-done.2.refs_6_.refs_8_), channel_id=1, source_target_pairs={{0,4},{4,12},{12,20},{20,28},{28,24},{24,16},{16,8},{8,0},{1,5},{5... | collective-permute-start | bytes 1204232 | tf_op jit(solution)/shard_map/ppermute | solution.py:430
  18.0 0.4 collective-permute-start.10
  18.5 0.3 expand_tiles.3.refs_0_
  18.8 0.0 copy-start
  18.8 4.3 %collective-permute-done.refs_7_.refs_9_ = bf16[768,256]{1,0:T(8,128)(2,1)S(1)} collective-permute-done((bf16[768,256]{1,0:T(8,128)(2,1)S(1)}, bf16[768,256]{1,0:T(8,128)(2,1)S(1)}, u32[]{:S(2)}, u32[]{:S(2)}) %collective-permute-start) | collective-permute-done | bytes 393248 | tf_op jit(solution)/shard_map/ppermute | solution.py:430
  23.1 1.9 %collective-permute-done.1.refs_8_.refs_10_ = bf16[784,256]{1,0:T(8,128)(2,1)S(1)} collective-permute-done((bf16[784,256]{1,0:T(8,128)(2,1)S(1)}, bf16[784,256]{1,0:T(8,128)(2,1)S(1)}, u32[]{:S(2)}, u32[]{:S(2)}) %collective-permute-start.1) | collective-permute-done | bytes 401440 | tf_op jit(solution)/shard_map/ppermute | solution.py:430
  25.1 0.1 collective-permute-start.8
  25.2 1.9 %collective-permute-start.7 = (bf16[768,256]{1,0:T(8,128)(2,1)S(1)}, bf16[768,256]{1,0:T(8,128)(2,1)S(1)}, u32[]{:S(2)}, u32[]{:S(2)}) collective-permute-start(bf16[768,256]{1,0:T(8,128)(2,1)S(1)} %collective-permute-done.refs_7_.refs_9_), channel_id=1, source_target_pairs={{0,4},{4,12},{12,20},{20,28},{28,24},{24,16},{16,8},{8,0},{1,5},{5... | collective-permute-start | bytes 1179656 | tf_op jit(solution)/shard_map/ppermute | solution.py:430
  27.1 0.3 expand_tiles.4.refs_1_
  27.4 0.6 keep_rows.1.keep_ref
  28.0 5.5 %collective-permute-done.10.refs_7_ = bf16[768,256]{1,0:T(8,128)(2,1)S(1)} collective-permute-done((bf16[768,256]{1,0:T(8,128)(2,1)S(1)}, bf16[768,256]{1,0:T(8,128)(2,1)S(1)}, u32[]{:S(2)}, u32[]{:S(2)}) %collective-permute-start.10) | collective-permute-done | bytes 393248 | tf_op jit(solution)/shard_map/ppermute | solution.py:430
  33.5 1.6 %collective-permute-start.11 = (bf16[784,256]{1,0:T(8,128)(2,1)S(1)}, bf16[784,256]{1,0:T(8,128)(2,1)S(1)}, u32[]{:S(2)}, u32[]{:S(2)}) collective-permute-start(bf16[784,256]{1,0:T(8,128)(2,1)S(1)} %collective-permute-done.9.refs_4_), channel_id=1, source_target_pairs={{0,4},{4,12},{12,20},{20,28},{28,24},{24,16},{16,8},{8,0},{1,5},{5... | collective-permute-start | bytes 1204232 | tf_op jit(solution)/shard_map/ppermute | solution.py:430
  35.1 0.4 collective-permute-start.12
  35.5 4.6 %collective-permute-done.7.refs_5_ = bf16[768,256]{1,0:T(8,128)(2,1)S(1)} collective-permute-done((bf16[768,256]{1,0:T(8,128)(2,1)S(1)}, bf16[768,256]{1,0:T(8,128)(2,1)S(1)}, u32[]{:S(2)}, u32[]{:S(2)}) %collective-permute-start.7) | collective-permute-done | bytes 393248 | tf_op jit(solution)/shard_map/ppermute | solution.py:430
  40.1 1.9 %collective-permute-done.8.refs_6_ = bf16[784,256]{1,0:T(8,128)(2,1)S(1)} collective-permute-done((bf16[784,256]{1,0:T(8,128)(2,1)S(1)}, bf16[784,256]{1,0:T(8,128)(2,1)S(1)}, u32[]{:S(2)}, u32[]{:S(2)}) %collective-permute-start.8) | collective-permute-done | bytes 401440 | tf_op jit(solution)/shard_map/ppermute | solution.py:430
  42.1 1.6 %collective-permute-start.15 = (bf16[768,256]{1,0:T(8,128)(2,1)S(1)}, bf16[768,256]{1,0:T(8,128)(2,1)S(1)}, u32[]{:S(2)}, u32[]{:S(2)}) collective-permute-start(bf16[768,256]{1,0:T(8,128)(2,1)S(1)} %collective-permute-done.7.refs_5_), channel_id=1, source_target_pairs={{0,4},{4,12},{12,20},{20,28},{28,24},{24,16},{16,8},{8,0},{1,5},{5... | collective-permute-start | bytes 1179656 | tf_op jit(solution)/shard_map/ppermute | solution.py:430
  43.7 0.4 collective-permute-start.16
  44.1 0.7 expand_tiles.5
  44.8 4.2 %product.2.refs_12_ = f32[512,1024]{1,0:T(8,128)S(1)} custom-call(bf16[512,1024]{1,0:T(8,128)(2,1)S(1)} %expand_tiles.3.refs_0_, bf16[512,1024]{1,0:T(8,128)(2,1)S(1)} %expand_tiles.4.refs_1_, bf16[512,1024]{1,0:T(8,128)(2,1)S(1)} %get-tuple-element.57.refs_2_, bf16[512,1024]{1,0:T(8,128)(2,1)S(1)} %get-tuple-element.58.refs_3_, ...), custom_call_target="tpu_custom_call" | custom-call | flops 536870912 | tf_op jit(solution)/shard_map/product/pallas_call | solution.py:242
  49.0 1.5 %collective-permute-done.12.refs_5_ = bf16[768,256]{1,0:T(8,128)(2,1)S(1)} collective-permute-done((bf16[768,256]{1,0:T(8,128)(2,1)S(1)}, bf16[768,256]{1,0:T(8,128)(2,1)S(1)}, u32[]{:S(2)}, u32[]{:S(2)}) %collective-permute-start.12) | collective-permute-done | bytes 393248 | tf_op jit(solution)/shard_map/ppermute | solution.py:430
  50.5 3.5 %collective-permute-start.13 = (bf16[784,256]{1,0:T(8,128)(2,1)S(1)}, bf16[784,256]{1,0:T(8,128)(2,1)S(1)}, u32[]{:S(2)}, u32[]{:S(2)}) collective-permute-start(bf16[784,256]{1,0:T(8,128)(2,1)S(1)} %collective-permute-done.11.refs_2_), channel_id=1, source_target_pairs={{0,4},{1,1},{2,6},{3,3},{4,12},{5,5},{6,14},{7,7},{12,20},{13,13},... | collective-permute-start | bytes 1204232 | tf_op jit(solution)/shard_map/ppermute | solution.py:438
  54.0 2.4 %collective-permute-start.14 = (bf16[768,256]{1,0:T(8,128)(2,1)S(1)}, bf16[768,256]{1,0:T(8,128)(2,1)S(1)}, u32[]{:S(2)}, u32[]{:S(2)}) collective-permute-start(bf16[768,256]{1,0:T(8,128)(2,1)S(1)} %collective-permute-done.12.refs_5_), channel_id=1, source_target_pairs={{0,8},{1,1},{2,10},{3,3},{4,0},{5,5},{6,2},{7,7},{12,4},{13,13},{1... | collective-permute-start | bytes 1179656 | tf_op jit(solution)/shard_map/ppermute | solution.py:438
  56.4 3.2 %product.3 = (f32[512,1024]{1,0:T(8,128)S(1)}, bf16[512,512]{1,0:T(8,128)(2,1)S(1)}, bf16[512,512]{1,0:T(8,128)(2,1)S(1)}, bf16[512,512]{1,0:T(8,128)(2,1)S(1)}) custom-call(bf16[512,1024]{1,0:T(8,128)(2,1)S(1)} %expand_tiles.3.refs_0_, bf16[512,1024]{1,0:T(8,128)(2,1)S(1)} %expand_tiles.4.refs_1_, bf16[512,1024]{1,0:T(8,128)(2,1)S(1)} %get-tuple-element.57.refs_2_, ...), custom_call_target="tpu_custom_call" | custom-call | flops 536870912 | tf_op jit(solution)/shard_map/product/pallas_call | solution.py:242
  59.5 0.7 collective-permute-start.17
  60.3 0.7 collective-permute-start.18
  60.9 0.0 collective-permute-done.16.refs_4_
  61.0 1.4 %product_near.1.refs_2_ = f32[512,1024]{1,0:T(8,128)S(1)} custom-call(bf16[512,512]{1,0:T(8,128)(2,1)S(1)} %get-tuple-element.64.refs_0_, bf16[512,512]{1,0:T(8,128)(2,1)S(1)} %get-tuple-element.65.refs_1_, bf16[784,256]{1,0:T(8,128)(2,1)S(1)} %collective-permute-done.11.refs_2_, bf16[768,256]{1,0:T(8,128)(2,1)S(1)} %collective-permute-done.15.refs_3_, ...), custom_call_target="tpu_custom_call" | custom-call | flops 536870912 | tf_op jit(solution)/shard_map/product_near/pallas_call | solution.py:285
  62.4 1.3 %collective-permute-done.14.refs_1_ = bf16[768,256]{1,0:T(8,128)(2,1)S(1)} collective-permute-done((bf16[768,256]{1,0:T(8,128)(2,1)S(1)}, bf16[768,256]{1,0:T(8,128)(2,1)S(1)}, u32[]{:S(2)}, u32[]{:S(2)}) %collective-permute-start.14) | collective-permute-done | bytes 393248 | tf_op jit(solution)/shard_map/ppermute | solution.py:438
  63.7 0.9 %product_last.2 = (f32[512,1024]{1,0:T(8,128)S(1)}, f32[1,1024]{1,0:T(1,128)S(1)}) custom-call(f32[16,1024]{1,0:T(8,128)S(1)} %keep_rows.1.keep_ref, bf16[512,512]{1,0:T(8,128)(2,1)S(1)} %get-tuple-element.63.left_ref, bf16[784,256]{1,0:T(8,128)(2,1)S(1)} %collective-permute-done.13.refs_0_, bf16[768,256]{1,0:T(8,128)(2,1)S(1)} %collective-permute-done.14.refs_1_, ...), custom_call_target="tpu_custom_call" | custom-call | flops 536870912 | tf_op jit(solution)/shard_map/product_last/pallas_call | solution.py:354
  64.6 1.6 %collective-permute-start.19 = (f32[1,1024]{1,0:T(1,128)S(1)}, f32[1,1024]{1,0:T(1,128)S(1)}, u32[]{:S(2)}, u32[]{:S(2)}) collective-permute-start(f32[1,1024]{1,0:T(1,128)S(1)} %get-tuple-element.72), channel_id=1, source_target_pairs={{0,4},{4,0},{8,12},{12,8},{16,20},{20,16},{24,28},{28,24},{1,5},{5... | collective-permute-start | bytes 12296 | tf_op jit(solution)/shard_map/ppermute | solution.py:409
  66.3 2.1 %collective-permute-done.19 = f32[1,1024]{1,0:T(1,128)S(1)} collective-permute-done((f32[1,1024]{1,0:T(1,128)S(1)}, f32[1,1024]{1,0:T(1,128)S(1)}, u32[]{:S(2)}, u32[]{:S(2)}) %collective-permute-start.19) | collective-permute-done | bytes 4128 | tf_op jit(solution)/shard_map/ppermute | solution.py:409
  68.4 1.0 %collective-permute-start.20 = (f32[1,1024]{1,0:T(1,128)S(1)}, f32[1,1024]{1,0:T(1,128)S(1)}, u32[]{:S(2)}, u32[]{:S(2)}) collective-permute-start(f32[1,1024]{1,0:T(1,128)S(1)} %add.12), channel_id=1, source_target_pairs={{0,8},{4,12},{8,16},{12,20},{16,24},{20,28},{24,0},{28,4},{1,9},{5... | collective-permute-start | bytes 12296 | tf_op jit(solution)/shard_map/ppermute | solution.py:411
  69.4 1.9 %collective-permute-start.21 = (f32[1,1024]{1,0:T(1,128)S(1)}, f32[1,1024]{1,0:T(1,128)S(1)}, u32[]{:S(2)}, u32[]{:S(2)}) collective-permute-start(f32[1,1024]{1,0:T(1,128)S(1)} %add.12), channel_id=1, source_target_pairs={{0,16},{4,20},{8,24},{12,28},{16,0},{20,4},{24,8},{28,12},{1,17},{... | collective-permute-start | bytes 12296 | tf_op jit(solution)/shard_map/ppermute | solution.py:411
  71.4 1.3 %collective-permute-start.22 = (f32[1,1024]{1,0:T(1,128)S(1)}, f32[1,1024]{1,0:T(1,128)S(1)}, u32[]{:S(2)}, u32[]{:S(2)}) collective-permute-start(f32[1,1024]{1,0:T(1,128)S(1)} %add.12), channel_id=1, source_target_pairs={{0,24},{4,28},{8,0},{12,4},{16,8},{20,12},{24,16},{28,20},{1,25},{... | collective-permute-start | bytes 12296 | tf_op jit(solution)/shard_map/ppermute | solution.py:411
  72.7 1.1 %collective-permute-done.20 = f32[1,1024]{1,0:T(1,128)S(1)} collective-permute-done((f32[1,1024]{1,0:T(1,128)S(1)}, f32[1,1024]{1,0:T(1,128)S(1)}, u32[]{:S(2)}, u32[]{:S(2)}) %collective-permute-start.20) | collective-permute-done | bytes 4128 | tf_op jit(solution)/shard_map/ppermute | solution.py:411
  73.8 0.2 collective-permute-done.21
  73.9 1.0 %collective-permute-done.22 = f32[1,1024]{1,0:T(1,128)S(1)} collective-permute-done((f32[1,1024]{1,0:T(1,128)S(1)}, f32[1,1024]{1,0:T(1,128)S(1)}, u32[]{:S(2)}, u32[]{:S(2)}) %collective-permute-start.22) | collective-permute-done | bytes 4128 | tf_op jit(solution)/shard_map/ppermute | solution.py:411
  75.0 1.4 %scale.1 = f32[512,1024]{1,0:T(8,128)} custom-call(f32[512,1024]{1,0:T(8,128)S(1)} %get-tuple-element.67.first_ref, f32[512,1024]{1,0:T(8,128)S(1)} %get-tuple-element.71.second_ref, f32[1,1024]{1,0:T(1,128)S(1)} %add_add_fusion.totals_ref), custom_call_target="tpu_custom_call" | custom-call | flops 536870912 | tf_op jit(solution)/shard_map/scale/pallas_call | solution.py:391
  (13 shorter events, 0.1 us)
Async XLA Ops:
  1.4 3.2 %collective-permute-start.4 = (bf16[1552,256]{1,0:T(8,128)(2,1)S(1)}, bf16[1552,256]{1,0:T(8,128)(2,1)S(1)}, u32[]{:S(2)}, u32[]{:S(2)}) collective-permute-start(bf16[1552,256]{1,0:T(8,128)(2,1)S(1)} %get-tuple-element.49.refs_0_), channel_id=1, source_target_pairs={{0,1},{1,0},{2,3},{3,2},{4,5},{5,4},{6,7},{7,6},{8,9},{9,8},{10,11... | collective-permute-start | bytes 2383880 | tf_op jit(solution)/shard_map/ppermute | solution.py:441
  1.9 14.5 %collective-permute-start.2 = (bf16[784,256]{1,0:T(8,128)(2,1)S(1)}, bf16[784,256]{1,0:T(8,128)(2,1)S(1)}, u32[]{:S(2)}, u32[]{:S(2)}) collective-permute-start(bf16[784,256]{1,0:T(8,128)(2,1)S(1)} %get-tuple-element.59.refs_4_), channel_id=1, source_target_pairs={{0,4},{4,12},{12,20},{20,28},{28,24},{24,16},{16,8},{8,0},{1,5},{5... | collective-permute-start | bytes 1204232 | tf_op jit(solution)/shard_map/ppermute | solution.py:430
  4.5 12.0 %collective-permute-start.3 = (bf16[768,256]{1,0:T(8,128)(2,1)S(1)}, bf16[768,256]{1,0:T(8,128)(2,1)S(1)}, u32[]{:S(2)}, u32[]{:S(2)}) collective-permute-start(bf16[768,256]{1,0:T(8,128)(2,1)S(1)} %get-tuple-element.39.refs_5_), channel_id=1, source_target_pairs={{0,8},{4,0},{12,4},{20,12},{28,20},{24,28},{16,24},{8,16},{1,9},{5... | collective-permute-start | bytes 1179656 | tf_op jit(solution)/shard_map/ppermute | solution.py:430
  4.6 22.4 %collective-permute-start.5 = (bf16[1552,256]{1,0:T(8,128)(2,1)S(1)}, bf16[1552,256]{1,0:T(8,128)(2,1)S(1)}, u32[]{:S(2)}, u32[]{:S(2)}) collective-permute-start(bf16[1552,256]{1,0:T(8,128)(2,1)S(1)} %get-tuple-element.49.refs_0_), channel_id=1, source_target_pairs={{0,2},{1,3},{2,0},{3,1},{4,6},{5,7},{6,4},{7,5},{8,10},{9,11},{10,... | collective-permute-start | bytes 2383880 | tf_op jit(solution)/shard_map/ppermute | solution.py:441
  6.7 18.4 %collective-permute-start.1 = (bf16[784,256]{1,0:T(8,128)(2,1)S(1)}, bf16[784,256]{1,0:T(8,128)(2,1)S(1)}, u32[]{:S(2)}, u32[]{:S(2)}) collective-permute-start(bf16[784,256]{1,0:T(8,128)(2,1)S(1)} %get-tuple-element.59.refs_4_), channel_id=1, source_target_pairs={{0,8},{4,0},{12,4},{20,12},{28,20},{24,28},{16,24},{8,16},{1,9},{5... | collective-permute-start | bytes 1204232 | tf_op jit(solution)/shard_map/ppermute | solution.py:430
  8.3 14.8 %collective-permute-start = (bf16[768,256]{1,0:T(8,128)(2,1)S(1)}, bf16[768,256]{1,0:T(8,128)(2,1)S(1)}, u32[]{:S(2)}, u32[]{:S(2)}) collective-permute-start(bf16[768,256]{1,0:T(8,128)(2,1)S(1)} %get-tuple-element.39.refs_5_), channel_id=1, source_target_pairs={{0,4},{4,12},{12,20},{20,28},{28,24},{24,16},{16,8},{8,0},{1,5},{5... | collective-permute-start | bytes 1179656 | tf_op jit(solution)/shard_map/ppermute | solution.py:430
  16.5 17.0 %collective-permute-start.9 = (bf16[784,256]{1,0:T(8,128)(2,1)S(1)}, bf16[784,256]{1,0:T(8,128)(2,1)S(1)}, u32[]{:S(2)}, u32[]{:S(2)}) collective-permute-start(bf16[784,256]{1,0:T(8,128)(2,1)S(1)} %collective-permute-done.2.refs_6_.refs_8_), channel_id=1, source_target_pairs={{0,4},{4,12},{12,20},{20,28},{28,24},{24,16},{16,8},{8,0},{1,5},{5... | collective-permute-start | bytes 1204232 | tf_op jit(solution)/shard_map/ppermute | solution.py:430
  18.0 15.4 %collective-permute-start.10 = (bf16[768,256]{1,0:T(8,128)(2,1)S(1)}, bf16[768,256]{1,0:T(8,128)(2,1)S(1)}, u32[]{:S(2)}, u32[]{:S(2)}) collective-permute-start(bf16[768,256]{1,0:T(8,128)(2,1)S(1)} %collective-permute-done.3.refs_9_.refs_11_), channel_id=1, source_target_pairs={{0,8},{4,0},{12,4},{20,12},{28,20},{24,28},{16,24},{8,16},{1,9},{5... | collective-permute-start | bytes 1179656 | tf_op jit(solution)/shard_map/ppermute | solution.py:430
  18.8 8.6 %copy-start = (s32[2,4]{1,0:T(2,128)S(1)}, s32[2,4]{1,0:T(2,128)}, u32[]{:S(2)}) copy-start(s32[2,4]{1,0:T(2,128)} %out_mask_ref) | copy-start | bytes 100
  25.1 17.0 %collective-permute-start.8 = (bf16[784,256]{1,0:T(8,128)(2,1)S(1)}, bf16[784,256]{1,0:T(8,128)(2,1)S(1)}, u32[]{:S(2)}, u32[]{:S(2)}) collective-permute-start(bf16[784,256]{1,0:T(8,128)(2,1)S(1)} %collective-permute-done.1.refs_8_.refs_10_), channel_id=1, source_target_pairs={{0,8},{4,0},{12,4},{20,12},{28,20},{24,28},{16,24},{8,16},{1,9},{5... | collective-permute-start | bytes 1204232 | tf_op jit(solution)/shard_map/ppermute | solution.py:430
  25.2 15.0 %collective-permute-start.7 = (bf16[768,256]{1,0:T(8,128)(2,1)S(1)}, bf16[768,256]{1,0:T(8,128)(2,1)S(1)}, u32[]{:S(2)}, u32[]{:S(2)}) collective-permute-start(bf16[768,256]{1,0:T(8,128)(2,1)S(1)} %collective-permute-done.refs_7_.refs_9_), channel_id=1, source_target_pairs={{0,4},{4,12},{12,20},{20,28},{28,24},{24,16},{16,8},{8,0},{1,5},{5... | collective-permute-start | bytes 1179656 | tf_op jit(solution)/shard_map/ppermute | solution.py:430
  27.1 17.0 %collective-permute-start.6 = (bf16[1552,256]{1,0:T(8,128)(2,1)S(1)}, bf16[1552,256]{1,0:T(8,128)(2,1)S(1)}, u32[]{:S(2)}, u32[]{:S(2)}) collective-permute-start(bf16[1552,256]{1,0:T(8,128)(2,1)S(1)} %collective-permute-done.5.refs_0_), channel_id=1, source_target_pairs={{0,1},{1,0},{2,3},{3,2},{4,5},{5,4},{6,7},{7,6},{8,9},{9,8},{10,11... | collective-permute-start | bytes 2383880 | tf_op jit(solution)/shard_map/ppermute | solution.py:441
  33.5 17.0 %collective-permute-start.11 = (bf16[784,256]{1,0:T(8,128)(2,1)S(1)}, bf16[784,256]{1,0:T(8,128)(2,1)S(1)}, u32[]{:S(2)}, u32[]{:S(2)}) collective-permute-start(bf16[784,256]{1,0:T(8,128)(2,1)S(1)} %collective-permute-done.9.refs_4_), channel_id=1, source_target_pairs={{0,4},{4,12},{12,20},{20,28},{28,24},{24,16},{16,8},{8,0},{1,5},{5... | collective-permute-start | bytes 1204232 | tf_op jit(solution)/shard_map/ppermute | solution.py:430
  35.1 15.4 %collective-permute-start.12 = (bf16[768,256]{1,0:T(8,128)(2,1)S(1)}, bf16[768,256]{1,0:T(8,128)(2,1)S(1)}, u32[]{:S(2)}, u32[]{:S(2)}) collective-permute-start(bf16[768,256]{1,0:T(8,128)(2,1)S(1)} %collective-permute-done.10.refs_7_), channel_id=1, source_target_pairs={{0,8},{4,0},{12,4},{20,12},{28,20},{24,28},{16,24},{8,16},{1,9},{5... | collective-permute-start | bytes 1179656 | tf_op jit(solution)/shard_map/ppermute | solution.py:430
  42.1 18.2 %collective-permute-start.15 = (bf16[768,256]{1,0:T(8,128)(2,1)S(1)}, bf16[768,256]{1,0:T(8,128)(2,1)S(1)}, u32[]{:S(2)}, u32[]{:S(2)}) collective-permute-start(bf16[768,256]{1,0:T(8,128)(2,1)S(1)} %collective-permute-done.7.refs_5_), channel_id=1, source_target_pairs={{0,4},{4,12},{12,20},{20,28},{28,24},{24,16},{16,8},{8,0},{1,5},{5... | collective-permute-start | bytes 1179656 | tf_op jit(solution)/shard_map/ppermute | solution.py:430
  43.7 17.3 %collective-permute-start.16 = (bf16[784,256]{1,0:T(8,128)(2,1)S(1)}, bf16[784,256]{1,0:T(8,128)(2,1)S(1)}, u32[]{:S(2)}, u32[]{:S(2)}) collective-permute-start(bf16[784,256]{1,0:T(8,128)(2,1)S(1)} %collective-permute-done.8.refs_6_), channel_id=1, source_target_pairs={{0,8},{4,0},{12,4},{20,12},{28,20},{24,28},{16,24},{8,16},{1,9},{5... | collective-permute-start | bytes 1204232 | tf_op jit(solution)/shard_map/ppermute | solution.py:430
  50.5 13.2 %collective-permute-start.13 = (bf16[784,256]{1,0:T(8,128)(2,1)S(1)}, bf16[784,256]{1,0:T(8,128)(2,1)S(1)}, u32[]{:S(2)}, u32[]{:S(2)}) collective-permute-start(bf16[784,256]{1,0:T(8,128)(2,1)S(1)} %collective-permute-done.11.refs_2_), channel_id=1, source_target_pairs={{0,4},{1,1},{2,6},{3,3},{4,12},{5,5},{6,14},{7,7},{12,20},{13,13},... | collective-permute-start | bytes 1204232 | tf_op jit(solution)/shard_map/ppermute | solution.py:438
  54.0 9.7 %collective-permute-start.14 = (bf16[768,256]{1,0:T(8,128)(2,1)S(1)}, bf16[768,256]{1,0:T(8,128)(2,1)S(1)}, u32[]{:S(2)}, u32[]{:S(2)}) collective-permute-start(bf16[768,256]{1,0:T(8,128)(2,1)S(1)} %collective-permute-done.12.refs_5_), channel_id=1, source_target_pairs={{0,8},{1,1},{2,10},{3,3},{4,0},{5,5},{6,2},{7,7},{12,4},{13,13},{1... | collective-permute-start | bytes 1179656 | tf_op jit(solution)/shard_map/ppermute | solution.py:438
  59.5 5.0 %collective-permute-start.17 = (bf16[784,256]{1,0:T(8,128)(2,1)S(1)}, bf16[784,256]{1,0:T(8,128)(2,1)S(1)}, u32[]{:S(2)}, u32[]{:S(2)}) collective-permute-start(bf16[784,256]{1,0:T(8,128)(2,1)S(1)} %collective-permute-done.11.refs_2_), channel_id=1, source_target_pairs={{0,0},{1,5},{2,2},{3,7},{4,4},{5,13},{6,6},{7,15},{12,12},{13,21},... | collective-permute-start | bytes 1204232 | tf_op jit(solution)/shard_map/ppermute | solution.py:438
  60.3 4.3 %collective-permute-start.18 = (bf16[768,256]{1,0:T(8,128)(2,1)S(1)}, bf16[768,256]{1,0:T(8,128)(2,1)S(1)}, u32[]{:S(2)}, u32[]{:S(2)}) collective-permute-start(bf16[768,256]{1,0:T(8,128)(2,1)S(1)} %collective-permute-done.12.refs_5_), channel_id=1, source_target_pairs={{0,0},{1,9},{2,2},{3,11},{4,4},{5,1},{6,6},{7,3},{12,12},{13,5},{1... | collective-permute-start | bytes 1179656 | tf_op jit(solution)/shard_map/ppermute | solution.py:438
  64.6 3.8 %collective-permute-start.19 = (f32[1,1024]{1,0:T(1,128)S(1)}, f32[1,1024]{1,0:T(1,128)S(1)}, u32[]{:S(2)}, u32[]{:S(2)}) collective-permute-start(f32[1,1024]{1,0:T(1,128)S(1)} %get-tuple-element.72), channel_id=1, source_target_pairs={{0,4},{4,0},{8,12},{12,8},{16,20},{20,16},{24,28},{28,24},{1,5},{5... | collective-permute-start | bytes 12296 | tf_op jit(solution)/shard_map/ppermute | solution.py:409
  68.4 5.4 %collective-permute-start.20 = (f32[1,1024]{1,0:T(1,128)S(1)}, f32[1,1024]{1,0:T(1,128)S(1)}, u32[]{:S(2)}, u32[]{:S(2)}) collective-permute-start(f32[1,1024]{1,0:T(1,128)S(1)} %add.12), channel_id=1, source_target_pairs={{0,8},{4,12},{8,16},{12,20},{16,24},{20,28},{24,0},{28,4},{1,9},{5... | collective-permute-start | bytes 12296 | tf_op jit(solution)/shard_map/ppermute | solution.py:411
  69.4 4.5 %collective-permute-start.21 = (f32[1,1024]{1,0:T(1,128)S(1)}, f32[1,1024]{1,0:T(1,128)S(1)}, u32[]{:S(2)}, u32[]{:S(2)}) collective-permute-start(f32[1,1024]{1,0:T(1,128)S(1)} %add.12), channel_id=1, source_target_pairs={{0,16},{4,20},{8,24},{12,28},{16,0},{20,4},{24,8},{28,12},{1,17},{... | collective-permute-start | bytes 12296 | tf_op jit(solution)/shard_map/ppermute | solution.py:411
  71.4 3.6 %collective-permute-start.22 = (f32[1,1024]{1,0:T(1,128)S(1)}, f32[1,1024]{1,0:T(1,128)S(1)}, u32[]{:S(2)}, u32[]{:S(2)}) collective-permute-start(f32[1,1024]{1,0:T(1,128)S(1)} %add.12), channel_id=1, source_target_pairs={{0,24},{4,28},{8,0},{12,4},{16,8},{20,12},{24,16},{28,20},{1,25},{... | collective-permute-start | bytes 12296 | tf_op jit(solution)/shard_map/ppermute | solution.py:411

commit v3 on v2

--- a/solution.py
+++ b/solution.py
@@ -369,7 +369,7 @@
 def scale_kernel(sz, steps, first_ref, second_ref, totals_ref, flow_ref, buf, sems):
     total_rows = float(sz.rows * sz.n_row)
     size = sz.rows // steps
-    share = 1.0 / totals_ref[...]
+    totals = totals_ref[...]
     copies = []
     for s in range(steps):
         rows = pl.ds(s * size, size)
@@ -377,7 +377,7 @@
 
             @pl.when(lax.axis_index("col") % 2 == core)
             def _():
-                buf[rows, :] = (total_rows * ref[rows, :]) * share
+                buf[rows, :] = total_rows * ref[rows, :] / totals
 
         copies.append(pltpu.make_async_copy(buf.at[rows], flow_ref.at[rows], sems.at[s]))
         copies[-1].start()
@@ -504,8 +504,9 @@
             if keys[0][0] == half - 1:
                 acc = near_product(sz, acc, lefts[:2], chunks)
             else:
-                then = (half - 1, 1 - half, half) if keys[0][0] == half - 2 else ()
-                acc, *lefts = product(sz, acc, dist, [dense[d] for d in dist], chunks, keys, then)
+                then = () if lefts else (half - 1, 1 - half, half)
+                acc, *more = product(sz, acc, dist, [dense[d] for d in dist], chunks, keys, then)
+                lefts = lefts or more
             gate.append(acc)
         if i + 3 == len(arrivals):
             final = after(final, acc)

time: 77.6 us -> 77.2 us (level)
  no operation moved by 1% of the time
where the time goes in v3:
time: 77.2 us; the launch traced here: 76.7 us
  waiting for transfers between devices  33.1 us (43%)
  starting transfers between devices  29 us (38%)
  Pallas kernels  14.4 us (19%)
    ppermute x12, waiting for transfers between devices, hop(): return lax.ppermute(chunk, 'row', pairs)  27.2 us
    ppermute x12, starting transfers between devices, hop(): return lax.ppermute(chunk, 'row', pairs)  12.9 us
    pallas_call x2, Pallas kernels, product(): pl.pallas_call(functools.partial(product_kernel, sz, dist, keys, first, t...  7.38 us
    ppermute x4, starting transfers between devices, last_hop(): return lax.ppermute(chunk, ('row', 'col'), pairs)  7.2 us
    ppermute x3, starting transfers between devices, column_sums(): lax.ppermute(pair, 'row', [(q, (q + 2 * t) % sz.n_row) for q in range(sz....  4.77 us
    ppermute x3, starting transfers between devices, apart(): return lax.ppermute(value, 'col', [(q, q ^ far) for q in range(n_col)])  2.58 us
    ppermute x3, waiting for transfers between devices, column_sums(): lax.ppermute(pair, 'row', [(q, (q + 2 * t) % sz.n_row) for q in range(sz....  2.25 us
    ppermute x1, waiting for transfers between devices, column_sums(): lax.ppermute(sums, 'row', [(q, q ^ 1) for q in range(sz.n_row)])  2.03 us
  transfers between devices with their start and end apart: 23, of which 12 were waited for; matrix products, arithmetic and copies ran while one was open for 0% of the time, Pallas kernels for 15%

profile of v3, /device:TPU:0, one launch (start us, length us, event | category | flops | bytes accessed | tf_op | source)
XLA Modules:
  0.0 76.7 jit_solution(2475995859417247490)
XLA Ops:
  0.0 1.4 %pack_tiles.1 = (bf16[1552,256]{1,0:T(8,128)(2,1)S(1)}, bf16[784,256]{1,0:T(8,128)(2,1)S(1)}, bf16[768,256]{1,0:T(8,128)(2,1)S(1)}) custom-call(s32[2,4]{1,0:T(2,128)} %mask_ref.1, bf16[512,1024]{1,0:T(8,128)(2,1)} %matrix_ref.1), custom_call_target="tpu_custom_call" | custom-call | tf_op jit(solution)/shard_map/pack_tiles/pallas_call | solution.py:87
  1.4 0.5 collective-permute-start.4
  1.9 2.6 %collective-permute-start.2 = (bf16[784,256]{1,0:T(8,128)(2,1)S(1)}, bf16[784,256]{1,0:T(8,128)(2,1)S(1)}, u32[]{:S(2)}, u32[]{:S(2)}) collective-permute-start(bf16[784,256]{1,0:T(8,128)(2,1)S(1)} %get-tuple-element.59.refs_4_), channel_id=1, source_target_pairs={{0,4},{4,12},{12,20},{20,28},{28,24},{24,16},{16,8},{8,0},{1,5},{5... | collective-permute-start | bytes 1204232 | tf_op jit(solution)/shard_map/ppermute | solution.py:430
  4.5 0.1 collective-permute-start.3
  4.6 0.0 collective-permute-done.4.refs_0_
  4.6 2.1 %collective-permute-start.5 = (bf16[1552,256]{1,0:T(8,128)(2,1)S(1)}, bf16[1552,256]{1,0:T(8,128)(2,1)S(1)}, u32[]{:S(2)}, u32[]{:S(2)}) collective-permute-start(bf16[1552,256]{1,0:T(8,128)(2,1)S(1)} %get-tuple-element.49.refs_0_), channel_id=1, source_target_pairs={{0,2},{1,3},{2,0},{3,1},{4,6},{5,7},{6,4},{7,5},{8,10},{9,11},{10,... | collective-permute-start | bytes 2383880 | tf_op jit(solution)/shard_map/ppermute | solution.py:441
  6.7 1.6 %collective-permute-start.1 = (bf16[784,256]{1,0:T(8,128)(2,1)S(1)}, bf16[784,256]{1,0:T(8,128)(2,1)S(1)}, u32[]{:S(2)}, u32[]{:S(2)}) collective-permute-start(bf16[784,256]{1,0:T(8,128)(2,1)S(1)} %get-tuple-element.59.refs_4_), channel_id=1, source_target_pairs={{0,8},{4,0},{12,4},{20,12},{28,20},{24,28},{16,24},{8,16},{1,9},{5... | collective-permute-start | bytes 1204232 | tf_op jit(solution)/shard_map/ppermute | solution.py:430
  8.3 0.4 collective-permute-start
  8.7 7.7 %collective-permute-done.3.refs_9_.refs_11_ = bf16[768,256]{1,0:T(8,128)(2,1)S(1)} collective-permute-done((bf16[768,256]{1,0:T(8,128)(2,1)S(1)}, bf16[768,256]{1,0:T(8,128)(2,1)S(1)}, u32[]{:S(2)}, u32[]{:S(2)}) %collective-permute-start.3) | collective-permute-done | bytes 393248 | tf_op jit(solution)/shard_map/ppermute | solution.py:430
  16.5 1.6 %collective-permute-start.9 = (bf16[784,256]{1,0:T(8,128)(2,1)S(1)}, bf16[784,256]{1,0:T(8,128)(2,1)S(1)}, u32[]{:S(2)}, u32[]{:S(2)}) collective-permute-start(bf16[784,256]{1,0:T(8,128)(2,1)S(1)} %collective-permute-done.2.refs_6_.refs_8_), channel_id=1, source_target_pairs={{0,4},{4,12},{12,20},{20,28},{28,24},{24,16},{16,8},{8,0},{1,5},{5... | collective-permute-start | bytes 1204232 | tf_op jit(solution)/shard_map/ppermute | solution.py:430
  18.0 0.4 collective-permute-start.10
  18.5 0.3 expand_tiles.3.refs_0_
  18.8 0.0 copy-start
  18.8 4.3 %collective-permute-done.refs_7_.refs_9_ = bf16[768,256]{1,0:T(8,128)(2,1)S(1)} collective-permute-done((bf16[768,256]{1,0:T(8,128)(2,1)S(1)}, bf16[768,256]{1,0:T(8,128)(2,1)S(1)}, u32[]{:S(2)}, u32[]{:S(2)}) %collective-permute-start) | collective-permute-done | bytes 393248 | tf_op jit(solution)/shard_map/ppermute | solution.py:430
  23.1 1.9 %collective-permute-done.1.refs_8_.refs_10_ = bf16[784,256]{1,0:T(8,128)(2,1)S(1)} collective-permute-done((bf16[784,256]{1,0:T(8,128)(2,1)S(1)}, bf16[784,256]{1,0:T(8,128)(2,1)S(1)}, u32[]{:S(2)}, u32[]{:S(2)}) %collective-permute-start.1) | collective-permute-done | bytes 401440 | tf_op jit(solution)/shard_map/ppermute | solution.py:430
  25.1 0.1 collective-permute-start.8
  25.2 1.9 %collective-permute-start.7 = (bf16[768,256]{1,0:T(8,128)(2,1)S(1)}, bf16[768,256]{1,0:T(8,128)(2,1)S(1)}, u32[]{:S(2)}, u32[]{:S(2)}) collective-permute-start(bf16[768,256]{1,0:T(8,128)(2,1)S(1)} %collective-permute-done.refs_7_.refs_9_), channel_id=1, source_target_pairs={{0,4},{4,12},{12,20},{20,28},{28,24},{24,16},{16,8},{8,0},{1,5},{5... | collective-permute-start | bytes 1179656 | tf_op jit(solution)/shard_map/ppermute | solution.py:430
  27.1 0.0 collective-permute-done.5.refs_0_
  27.1 0.0 collective-permute-start.6
  27.1 0.3 expand_tiles.4.refs_1_
  27.4 0.6 keep_rows.1.keep_ref
  28.0 5.5 %collective-permute-done.10.refs_7_ = bf16[768,256]{1,0:T(8,128)(2,1)S(1)} collective-permute-done((bf16[768,256]{1,0:T(8,128)(2,1)S(1)}, bf16[768,256]{1,0:T(8,128)(2,1)S(1)}, u32[]{:S(2)}, u32[]{:S(2)}) %collective-permute-start.10) | collective-permute-done | bytes 393248 | tf_op jit(solution)/shard_map/ppermute | solution.py:430
  33.5 1.6 %collective-permute-start.11 = (bf16[784,256]{1,0:T(8,128)(2,1)S(1)}, bf16[784,256]{1,0:T(8,128)(2,1)S(1)}, u32[]{:S(2)}, u32[]{:S(2)}) collective-permute-start(bf16[784,256]{1,0:T(8,128)(2,1)S(1)} %collective-permute-done.9.refs_4_), channel_id=1, source_target_pairs={{0,4},{4,12},{12,20},{20,28},{28,24},{24,16},{16,8},{8,0},{1,5},{5... | collective-permute-start | bytes 1204232 | tf_op jit(solution)/shard_map/ppermute | solution.py:430
  35.1 0.4 collective-permute-start.12
  35.5 4.6 %collective-permute-done.7.refs_5_ = bf16[768,256]{1,0:T(8,128)(2,1)S(1)} collective-permute-done((bf16[768,256]{1,0:T(8,128)(2,1)S(1)}, bf16[768,256]{1,0:T(8,128)(2,1)S(1)}, u32[]{:S(2)}, u32[]{:S(2)}) %collective-permute-start.7) | collective-permute-done | bytes 393248 | tf_op jit(solution)/shard_map/ppermute | solution.py:430
  40.1 1.9 %collective-permute-done.8.refs_6_ = bf16[784,256]{1,0:T(8,128)(2,1)S(1)} collective-permute-done((bf16[784,256]{1,0:T(8,128)(2,1)S(1)}, bf16[784,256]{1,0:T(8,128)(2,1)S(1)}, u32[]{:S(2)}, u32[]{:S(2)}) %collective-permute-start.8) | collective-permute-done | bytes 401440 | tf_op jit(solution)/shard_map/ppermute | solution.py:430
  42.1 1.6 %collective-permute-start.15 = (bf16[768,256]{1,0:T(8,128)(2,1)S(1)}, bf16[768,256]{1,0:T(8,128)(2,1)S(1)}, u32[]{:S(2)}, u32[]{:S(2)}) collective-permute-start(bf16[768,256]{1,0:T(8,128)(2,1)S(1)} %collective-permute-done.7.refs_5_), channel_id=1, source_target_pairs={{0,4},{4,12},{12,20},{20,28},{28,24},{24,16},{16,8},{8,0},{1,5},{5... | collective-permute-start | bytes 1179656 | tf_op jit(solution)/shard_map/ppermute | solution.py:430
  43.7 0.4 collective-permute-start.16
  44.1 0.7 expand_tiles.5
  44.8 4.5 %product.2 = (f32[512,1024]{1,0:T(8,128)S(1)}, bf16[512,512]{1,0:T(8,128)(2,1)S(1)}, bf16[512,512]{1,0:T(8,128)(2,1)S(1)}, bf16[512,512]{1,0:T(8,128)(2,1)S(1)}) custom-call(bf16[512,1024]{1,0:T(8,128)(2,1)S(1)} %expand_tiles.3.refs_0_, bf16[512,1024]{1,0:T(8,128)(2,1)S(1)} %expand_tiles.4.refs_1_, bf16[512,1024]{1,0:T(8,128)(2,1)S(1)} %get-tuple-element.57.refs_2_, ...), custom_call_target="tpu_custom_call" | custom-call | flops 536870912 | tf_op jit(solution)/shard_map/product/pallas_call | solution.py:242
  49.3 1.2 %collective-permute-done.12.refs_5_ = bf16[768,256]{1,0:T(8,128)(2,1)S(1)} collective-permute-done((bf16[768,256]{1,0:T(8,128)(2,1)S(1)}, bf16[768,256]{1,0:T(8,128)(2,1)S(1)}, u32[]{:S(2)}, u32[]{:S(2)}) %collective-permute-start.12) | collective-permute-done | bytes 393248 | tf_op jit(solution)/shard_map/ppermute | solution.py:430
  50.5 3.5 %collective-permute-start.13 = (bf16[784,256]{1,0:T(8,128)(2,1)S(1)}, bf16[784,256]{1,0:T(8,128)(2,1)S(1)}, u32[]{:S(2)}, u32[]{:S(2)}) collective-permute-start(bf16[784,256]{1,0:T(8,128)(2,1)S(1)} %collective-permute-done.11.refs_2_), channel_id=1, source_target_pairs={{0,4},{1,1},{2,6},{3,3},{4,12},{5,5},{6,14},{7,7},{12,20},{13,13},... | collective-permute-start | bytes 1204232 | tf_op jit(solution)/shard_map/ppermute | solution.py:438
  54.0 2.4 %collective-permute-start.14 = (bf16[768,256]{1,0:T(8,128)(2,1)S(1)}, bf16[768,256]{1,0:T(8,128)(2,1)S(1)}, u32[]{:S(2)}, u32[]{:S(2)}) collective-permute-start(bf16[768,256]{1,0:T(8,128)(2,1)S(1)} %collective-permute-done.12.refs_5_), channel_id=1, source_target_pairs={{0,8},{1,1},{2,10},{3,3},{4,0},{5,5},{6,2},{7,7},{12,4},{13,13},{1... | collective-permute-start | bytes 1179656 | tf_op jit(solution)/shard_map/ppermute | solution.py:438
  56.4 2.9 %product.3.refs_6_ = f32[512,1024]{1,0:T(8,128)S(1)} custom-call(bf16[512,1024]{1,0:T(8,128)(2,1)S(1)} %expand_tiles.3.refs_0_, bf16[512,1024]{1,0:T(8,128)(2,1)S(1)} %expand_tiles.4.refs_1_, bf16[512,1024]{1,0:T(8,128)(2,1)S(1)} %get-tuple-element.57.refs_2_, bf16[512,1024]{1,0:T(8,128)(2,1)S(1)} %get-tuple-element.58.refs_3_, ...), custom_call_target="tpu_custom_call" | custom-call | flops 536870912 | tf_op jit(solution)/shard_map/product/pallas_call | solution.py:242
  59.2 0.7 collective-permute-start.17
  59.9 0.7 collective-permute-start.18
  60.6 1.4 %product_near.1.refs_2_ = f32[512,1024]{1,0:T(8,128)S(1)} custom-call(bf16[512,512]{1,0:T(8,128)(2,1)S(1)} %get-tuple-element.64.refs_0_, bf16[512,512]{1,0:T(8,128)(2,1)S(1)} %get-tuple-element.65.refs_1_, bf16[784,256]{1,0:T(8,128)(2,1)S(1)} %collective-permute-done.11.refs_2_, bf16[768,256]{1,0:T(8,128)(2,1)S(1)} %collective-permute-done.15.refs_3_, ...), custom_call_target="tpu_custom_call" | custom-call | flops 536870912 | tf_op jit(solution)/shard_map/product_near/pallas_call | solution.py:285
  62.1 1.6 %collective-permute-done.14.refs_1_ = bf16[768,256]{1,0:T(8,128)(2,1)S(1)} collective-permute-done((bf16[768,256]{1,0:T(8,128)(2,1)S(1)}, bf16[768,256]{1,0:T(8,128)(2,1)S(1)}, u32[]{:S(2)}, u32[]{:S(2)}) %collective-permute-start.14) | collective-permute-done | bytes 393248 | tf_op jit(solution)/shard_map/ppermute | solution.py:438
  63.7 0.9 %product_last.2 = (f32[512,1024]{1,0:T(8,128)S(1)}, f32[1,1024]{1,0:T(1,128)S(1)}) custom-call(f32[16,1024]{1,0:T(8,128)S(1)} %keep_rows.1.keep_ref, bf16[512,512]{1,0:T(8,128)(2,1)S(1)} %get-tuple-element.60.left_ref, bf16[784,256]{1,0:T(8,128)(2,1)S(1)} %collective-permute-done.13.refs_0_, bf16[768,256]{1,0:T(8,128)(2,1)S(1)} %collective-permute-done.14.refs_1_, ...), custom_call_target="tpu_custom_call" | custom-call | flops 536870912 | tf_op jit(solution)/shard_map/product_last/pallas_call | solution.py:354
  64.6 1.6 %collective-permute-start.19 = (f32[1,1024]{1,0:T(1,128)S(1)}, f32[1,1024]{1,0:T(1,128)S(1)}, u32[]{:S(2)}, u32[]{:S(2)}) collective-permute-start(f32[1,1024]{1,0:T(1,128)S(1)} %get-tuple-element.72), channel_id=1, source_target_pairs={{0,4},{4,0},{8,12},{12,8},{16,20},{20,16},{24,28},{28,24},{1,5},{5... | collective-permute-start | bytes 12296 | tf_op jit(solution)/shard_map/ppermute | solution.py:409
  66.3 2.0 %collective-permute-done.19 = f32[1,1024]{1,0:T(1,128)S(1)} collective-permute-done((f32[1,1024]{1,0:T(1,128)S(1)}, f32[1,1024]{1,0:T(1,128)S(1)}, u32[]{:S(2)}, u32[]{:S(2)}) %collective-permute-start.19) | collective-permute-done | bytes 4128 | tf_op jit(solution)/shard_map/ppermute | solution.py:409
  68.3 1.1 %collective-permute-start.20 = (f32[1,1024]{1,0:T(1,128)S(1)}, f32[1,1024]{1,0:T(1,128)S(1)}, u32[]{:S(2)}, u32[]{:S(2)}) collective-permute-start(f32[1,1024]{1,0:T(1,128)S(1)} %add.12), channel_id=1, source_target_pairs={{0,8},{4,12},{8,16},{12,20},{16,24},{20,28},{24,0},{28,4},{1,9},{5... | collective-permute-start | bytes 12296 | tf_op jit(solution)/shard_map/ppermute | solution.py:411
  69.4 2.3 %collective-permute-start.21 = (f32[1,1024]{1,0:T(1,128)S(1)}, f32[1,1024]{1,0:T(1,128)S(1)}, u32[]{:S(2)}, u32[]{:S(2)}) collective-permute-start(f32[1,1024]{1,0:T(1,128)S(1)} %add.12), channel_id=1, source_target_pairs={{0,16},{4,20},{8,24},{12,28},{16,0},{20,4},{24,8},{28,12},{1,17},{... | collective-permute-start | bytes 12296 | tf_op jit(solution)/shard_map/ppermute | solution.py:411
  71.7 1.4 %collective-permute-start.22 = (f32[1,1024]{1,0:T(1,128)S(1)}, f32[1,1024]{1,0:T(1,128)S(1)}, u32[]{:S(2)}, u32[]{:S(2)}) collective-permute-start(f32[1,1024]{1,0:T(1,128)S(1)} %add.12), channel_id=1, source_target_pairs={{0,24},{4,28},{8,0},{12,4},{16,8},{20,12},{24,16},{28,20},{1,25},{... | collective-permute-start | bytes 12296 | tf_op jit(solution)/shard_map/ppermute | solution.py:411
  73.1 0.6 collective-permute-done.20
  73.7 0.2 collective-permute-done.21
  73.9 1.4 %collective-permute-done.22 = f32[1,1024]{1,0:T(1,128)S(1)} collective-permute-done((f32[1,1024]{1,0:T(1,128)S(1)}, f32[1,1024]{1,0:T(1,128)S(1)}, u32[]{:S(2)}, u32[]{:S(2)}) %collective-permute-start.22) | collective-permute-done | bytes 4128 | tf_op jit(solution)/shard_map/ppermute | solution.py:411
  75.3 1.4 %scale.1 = f32[512,1024]{1,0:T(8,128)} custom-call(f32[512,1024]{1,0:T(8,128)S(1)} %get-tuple-element.67.first_ref, f32[512,1024]{1,0:T(8,128)S(1)} %get-tuple-element.71.second_ref, f32[1,1024]{1,0:T(1,128)S(1)} %add_add_fusion.totals_ref), custom_call_target="tpu_custom_call" | custom-call | flops 536870912 | tf_op jit(solution)/shard_map/scale/pallas_call | solution.py:391
  (13 shorter events, 0.1 us)
Async XLA Ops:
  1.4 3.2 %collective-permute-start.4 = (bf16[1552,256]{1,0:T(8,128)(2,1)S(1)}, bf16[1552,256]{1,0:T(8,128)(2,1)S(1)}, u32[]{:S(2)}, u32[]{:S(2)}) collective-permute-start(bf16[1552,256]{1,0:T(8,128)(2,1)S(1)} %get-tuple-element.49.refs_0_), channel_id=1, source_target_pairs={{0,1},{1,0},{2,3},{3,2},{4,5},{5,4},{6,7},{7,6},{8,9},{9,8},{10,11... | collective-permute-start | bytes 2383880 | tf_op jit(solution)/shard_map/ppermute | solution.py:441
  1.9 14.5 %collective-permute-start.2 = (bf16[784,256]{1,0:T(8,128)(2,1)S(1)}, bf16[784,256]{1,0:T(8,128)(2,1)S(1)}, u32[]{:S(2)}, u32[]{:S(2)}) collective-permute-start(bf16[784,256]{1,0:T(8,128)(2,1)S(1)} %get-tuple-element.59.refs_4_), channel_id=1, source_target_pairs={{0,4},{4,12},{12,20},{20,28},{28,24},{24,16},{16,8},{8,0},{1,5},{5... | collective-permute-start | bytes 1204232 | tf_op jit(solution)/shard_map/ppermute | solution.py:430
  4.5 12.0 %collective-permute-start.3 = (bf16[768,256]{1,0:T(8,128)(2,1)S(1)}, bf16[768,256]{1,0:T(8,128)(2,1)S(1)}, u32[]{:S(2)}, u32[]{:S(2)}) collective-permute-start(bf16[768,256]{1,0:T(8,128)(2,1)S(1)} %get-tuple-element.39.refs_5_), channel_id=1, source_target_pairs={{0,8},{4,0},{12,4},{20,12},{28,20},{24,28},{16,24},{8,16},{1,9},{5... | collective-permute-start | bytes 1179656 | tf_op jit(solution)/shard_map/ppermute | solution.py:430
  4.6 22.4 %collective-permute-start.5 = (bf16[1552,256]{1,0:T(8,128)(2,1)S(1)}, bf16[1552,256]{1,0:T(8,128)(2,1)S(1)}, u32[]{:S(2)}, u32[]{:S(2)}) collective-permute-start(bf16[1552,256]{1,0:T(8,128)(2,1)S(1)} %get-tuple-element.49.refs_0_), channel_id=1, source_target_pairs={{0,2},{1,3},{2,0},{3,1},{4,6},{5,7},{6,4},{7,5},{8,10},{9,11},{10,... | collective-permute-start | bytes 2383880 | tf_op jit(solution)/shard_map/ppermute | solution.py:441
  6.7 18.4 %collective-permute-start.1 = (bf16[784,256]{1,0:T(8,128)(2,1)S(1)}, bf16[784,256]{1,0:T(8,128)(2,1)S(1)}, u32[]{:S(2)}, u32[]{:S(2)}) collective-permute-start(bf16[784,256]{1,0:T(8,128)(2,1)S(1)} %get-tuple-element.59.refs_4_), channel_id=1, source_target_pairs={{0,8},{4,0},{12,4},{20,12},{28,20},{24,28},{16,24},{8,16},{1,9},{5... | collective-permute-start | bytes 1204232 | tf_op jit(solution)/shard_map/ppermute | solution.py:430
  8.3 14.8 %collective-permute-start = (bf16[768,256]{1,0:T(8,128)(2,1)S(1)}, bf16[768,256]{1,0:T(8,128)(2,1)S(1)}, u32[]{:S(2)}, u32[]{:S(2)}) collective-permute-start(bf16[768,256]{1,0:T(8,128)(2,1)S(1)} %get-tuple-element.39.refs_5_), channel_id=1, source_target_pairs={{0,4},{4,12},{12,20},{20,28},{28,24},{24,16},{16,8},{8,0},{1,5},{5... | collective-permute-start | bytes 1179656 | tf_op jit(solution)/shard_map/ppermute | solution.py:430
  16.5 17.0 %collective-permute-start.9 = (bf16[784,256]{1,0:T(8,128)(2,1)S(1)}, bf16[784,256]{1,0:T(8,128)(2,1)S(1)}, u32[]{:S(2)}, u32[]{:S(2)}) collective-permute-start(bf16[784,256]{1,0:T(8,128)(2,1)S(1)} %collective-permute-done.2.refs_6_.refs_8_), channel_id=1, source_target_pairs={{0,4},{4,12},{12,20},{20,28},{28,24},{24,16},{16,8},{8,0},{1,5},{5... | collective-permute-start | bytes 1204232 | tf_op jit(solution)/shard_map/ppermute | solution.py:430
  18.0 15.4 %collective-permute-start.10 = (bf16[768,256]{1,0:T(8,128)(2,1)S(1)}, bf16[768,256]{1,0:T(8,128)(2,1)S(1)}, u32[]{:S(2)}, u32[]{:S(2)}) collective-permute-start(bf16[768,256]{1,0:T(8,128)(2,1)S(1)} %collective-permute-done.3.refs_9_.refs_11_), channel_id=1, source_target_pairs={{0,8},{4,0},{12,4},{20,12},{28,20},{24,28},{16,24},{8,16},{1,9},{5... | collective-permute-start | bytes 1179656 | tf_op jit(solution)/shard_map/ppermute | solution.py:430
  18.8 8.6 %copy-start = (s32[2,4]{1,0:T(2,128)S(1)}, s32[2,4]{1,0:T(2,128)}, u32[]{:S(2)}) copy-start(s32[2,4]{1,0:T(2,128)} %out_mask_ref) | copy-start | bytes 100
  25.1 17.0 %collective-permute-start.8 = (bf16[784,256]{1,0:T(8,128)(2,1)S(1)}, bf16[784,256]{1,0:T(8,128)(2,1)S(1)}, u32[]{:S(2)}, u32[]{:S(2)}) collective-permute-start(bf16[784,256]{1,0:T(8,128)(2,1)S(1)} %collective-permute-done.1.refs_8_.refs_10_), channel_id=1, source_target_pairs={{0,8},{4,0},{12,4},{20,12},{28,20},{24,28},{16,24},{8,16},{1,9},{5... | collective-permute-start | bytes 1204232 | tf_op jit(solution)/shard_map/ppermute | solution.py:430
  25.2 15.0 %collective-permute-start.7 = (bf16[768,256]{1,0:T(8,128)(2,1)S(1)}, bf16[768,256]{1,0:T(8,128)(2,1)S(1)}, u32[]{:S(2)}, u32[]{:S(2)}) collective-permute-start(bf16[768,256]{1,0:T(8,128)(2,1)S(1)} %collective-permute-done.refs_7_.refs_9_), channel_id=1, source_target_pairs={{0,4},{4,12},{12,20},{20,28},{28,24},{24,16},{16,8},{8,0},{1,5},{5... | collective-permute-start | bytes 1179656 | tf_op jit(solution)/shard_map/ppermute | solution.py:430
  27.1 17.0 %collective-permute-start.6 = (bf16[1552,256]{1,0:T(8,128)(2,1)S(1)}, bf16[1552,256]{1,0:T(8,128)(2,1)S(1)}, u32[]{:S(2)}, u32[]{:S(2)}) collective-permute-start(bf16[1552,256]{1,0:T(8,128)(2,1)S(1)} %collective-permute-done.5.refs_0_), channel_id=1, source_target_pairs={{0,1},{1,0},{2,3},{3,2},{4,5},{5,4},{6,7},{7,6},{8,9},{9,8},{10,11... | collective-permute-start | bytes 2383880 | tf_op jit(solution)/shard_map/ppermute | solution.py:441
  33.5 17.0 %collective-permute-start.11 = (bf16[784,256]{1,0:T(8,128)(2,1)S(1)}, bf16[784,256]{1,0:T(8,128)(2,1)S(1)}, u32[]{:S(2)}, u32[]{:S(2)}) collective-permute-start(bf16[784,256]{1,0:T(8,128)(2,1)S(1)} %collective-permute-done.9.refs_4_), channel_id=1, source_target_pairs={{0,4},{4,12},{12,20},{20,28},{28,24},{24,16},{16,8},{8,0},{1,5},{5... | collective-permute-start | bytes 1204232 | tf_op jit(solution)/shard_map/ppermute | solution.py:430
  35.1 15.4 %collective-permute-start.12 = (bf16[768,256]{1,0:T(8,128)(2,1)S(1)}, bf16[768,256]{1,0:T(8,128)(2,1)S(1)}, u32[]{:S(2)}, u32[]{:S(2)}) collective-permute-start(bf16[768,256]{1,0:T(8,128)(2,1)S(1)} %collective-permute-done.10.refs_7_), channel_id=1, source_target_pairs={{0,8},{4,0},{12,4},{20,12},{28,20},{24,28},{16,24},{8,16},{1,9},{5... | collective-permute-start | bytes 1179656 | tf_op jit(solution)/shard_map/ppermute | solution.py:430
  42.1 17.9 %collective-permute-start.15 = (bf16[768,256]{1,0:T(8,128)(2,1)S(1)}, bf16[768,256]{1,0:T(8,128)(2,1)S(1)}, u32[]{:S(2)}, u32[]{:S(2)}) collective-permute-start(bf16[768,256]{1,0:T(8,128)(2,1)S(1)} %collective-permute-done.7.refs_5_), channel_id=1, source_target_pairs={{0,4},{4,12},{12,20},{20,28},{28,24},{24,16},{16,8},{8,0},{1,5},{5... | collective-permute-start | bytes 1179656 | tf_op jit(solution)/shard_map/ppermute | solution.py:430
  43.7 17.0 %collective-permute-start.16 = (bf16[784,256]{1,0:T(8,128)(2,1)S(1)}, bf16[784,256]{1,0:T(8,128)(2,1)S(1)}, u32[]{:S(2)}, u32[]{:S(2)}) collective-permute-start(bf16[784,256]{1,0:T(8,128)(2,1)S(1)} %collective-permute-done.8.refs_6_), channel_id=1, source_target_pairs={{0,8},{4,0},{12,4},{20,12},{28,20},{24,28},{16,24},{8,16},{1,9},{5... | collective-permute-start | bytes 1204232 | tf_op jit(solution)/shard_map/ppermute | solution.py:430
  50.5 13.2 %collective-permute-start.13 = (bf16[784,256]{1,0:T(8,128)(2,1)S(1)}, bf16[784,256]{1,0:T(8,128)(2,1)S(1)}, u32[]{:S(2)}, u32[]{:S(2)}) collective-permute-start(bf16[784,256]{1,0:T(8,128)(2,1)S(1)} %collective-permute-done.11.refs_2_), channel_id=1, source_target_pairs={{0,4},{1,1},{2,6},{3,3},{4,12},{5,5},{6,14},{7,7},{12,20},{13,13},... | collective-permute-start | bytes 1204232 | tf_op jit(solution)/shard_map/ppermute | solution.py:438
  54.0 9.7 %collective-permute-start.14 = (bf16[768,256]{1,0:T(8,128)(2,1)S(1)}, bf16[768,256]{1,0:T(8,128)(2,1)S(1)}, u32[]{:S(2)}, u32[]{:S(2)}) collective-permute-start(bf16[768,256]{1,0:T(8,128)(2,1)S(1)} %collective-permute-done.12.refs_5_), channel_id=1, source_target_pairs={{0,8},{1,1},{2,10},{3,3},{4,0},{5,5},{6,2},{7,7},{12,4},{13,13},{1... | collective-permute-start | bytes 1179656 | tf_op jit(solution)/shard_map/ppermute | solution.py:438
  59.2 5.3 %collective-permute-start.17 = (bf16[784,256]{1,0:T(8,128)(2,1)S(1)}, bf16[784,256]{1,0:T(8,128)(2,1)S(1)}, u32[]{:S(2)}, u32[]{:S(2)}) collective-permute-start(bf16[784,256]{1,0:T(8,128)(2,1)S(1)} %collective-permute-done.11.refs_2_), channel_id=1, source_target_pairs={{0,0},{1,5},{2,2},{3,7},{4,4},{5,13},{6,6},{7,15},{12,12},{13,21},... | collective-permute-start | bytes 1204232 | tf_op jit(solution)/shard_map/ppermute | solution.py:438
  59.9 4.6 %collective-permute-start.18 = (bf16[768,256]{1,0:T(8,128)(2,1)S(1)}, bf16[768,256]{1,0:T(8,128)(2,1)S(1)}, u32[]{:S(2)}, u32[]{:S(2)}) collective-permute-start(bf16[768,256]{1,0:T(8,128)(2,1)S(1)} %collective-permute-done.12.refs_5_), channel_id=1, source_target_pairs={{0,0},{1,9},{2,2},{3,11},{4,4},{5,1},{6,6},{7,3},{12,12},{13,5},{1... | collective-permute-start | bytes 1179656 | tf_op jit(solution)/shard_map/ppermute | solution.py:438
  64.6 3.7 %collective-permute-start.19 = (f32[1,1024]{1,0:T(1,128)S(1)}, f32[1,1024]{1,0:T(1,128)S(1)}, u32[]{:S(2)}, u32[]{:S(2)}) collective-permute-start(f32[1,1024]{1,0:T(1,128)S(1)} %get-tuple-element.72), channel_id=1, source_target_pairs={{0,4},{4,0},{8,12},{12,8},{16,20},{20,16},{24,28},{28,24},{1,5},{5... | collective-permute-start | bytes 12296 | tf_op jit(solution)/shard_map/ppermute | solution.py:409
  68.3 5.4 %collective-permute-start.20 = (f32[1,1024]{1,0:T(1,128)S(1)}, f32[1,1024]{1,0:T(1,128)S(1)}, u32[]{:S(2)}, u32[]{:S(2)}) collective-permute-start(f32[1,1024]{1,0:T(1,128)S(1)} %add.12), channel_id=1, source_target_pairs={{0,8},{4,12},{8,16},{12,20},{16,24},{20,28},{24,0},{28,4},{1,9},{5... | collective-permute-start | bytes 12296 | tf_op jit(solution)/shard_map/ppermute | solution.py:411
  69.4 4.5 %collective-permute-start.21 = (f32[1,1024]{1,0:T(1,128)S(1)}, f32[1,1024]{1,0:T(1,128)S(1)}, u32[]{:S(2)}, u32[]{:S(2)}) collective-permute-start(f32[1,1024]{1,0:T(1,128)S(1)} %add.12), channel_id=1, source_target_pairs={{0,16},{4,20},{8,24},{12,28},{16,0},{20,4},{24,8},{28,12},{1,17},{... | collective-permute-start | bytes 12296 | tf_op jit(solution)/shard_map/ppermute | solution.py:411
  71.7 3.6 %collective-permute-start.22 = (f32[1,1024]{1,0:T(1,128)S(1)}, f32[1,1024]{1,0:T(1,128)S(1)}, u32[]{:S(2)}, u32[]{:S(2)}) collective-permute-start(f32[1,1024]{1,0:T(1,128)S(1)} %add.12), channel_id=1, source_target_pairs={{0,24},{4,28},{8,0},{12,4},{16,8},{20,12},{24,16},{28,20},{1,25},{... | collective-permute-start | bytes 12296 | tf_op jit(solution)/shard_map/ppermute | solution.py:411

commit v4 on v3

--- a/solution.py
+++ b/solution.py
@@ -21,9 +21,12 @@
         self.tr, self.tc = in_mask.shape
         self.tile = self.rows // self.tr
         self.cap = self.tr * self.tc * 3 // 4
-        self.pay_rows = CODE_ROWS + self.cap * self.tile
-        self.buf_rows = self.pay_rows + self.tile
-        self.cut = CODE_ROWS + (self.cap + 1) // 2 * self.tile
+        self.wide = min(self.tile, 128)
+        self.parts = self.tile // self.wide
+        self.slot = self.parts * self.tile
+        self.pay_rows = CODE_ROWS + self.cap * self.slot
+        self.buf_rows = self.pay_rows + self.slot
+        self.cut = CODE_ROWS + (self.cap + 1) // 2 * self.slot
         self.chunks = ((0, self.cut), (self.cut, self.pay_rows - self.cut))
         self.n_row, self.n_col = n_row, n_col
 
@@ -63,7 +66,7 @@
     code = jnp.int32(0)
     for t, flag in enumerate(flags):
         code = code + flag * (1 << t)
-    codes = jnp.full((CODE_ROWS, sz.tile), code.astype(jnp.float32), jnp.float32)
+    codes = jnp.full((CODE_ROWS, sz.wide), code.astype(jnp.float32), jnp.float32)
     codes = codes.astype(jnp.bfloat16)
     whole_ref[0:CODE_ROWS, :] = codes
     chunk_refs[0][0:CODE_ROWS, :] = codes
@@ -74,11 +77,13 @@
         row = pl.multiple_of(which // sz.tc * sz.tile, sz.tile)
         col = pl.multiple_of(which % sz.tc * sz.tile, sz.tile)
         values = matrix_ref[pl.ds(row, sz.tile), pl.ds(col, sz.tile)]
-        at = CODE_ROWS + s * sz.tile
-        whole_ref[at : at + sz.tile, :] = values
-        for ref, (start, size) in zip(chunk_refs, sz.chunks):
-            if start <= at < start + size:
-                ref[at - start : at - start + sz.tile, :] = values
+        for j in range(sz.parts):
+            part = values[:, j * sz.wide : (j + 1) * sz.wide]
+            at = CODE_ROWS + s * sz.slot + j * sz.tile
+            whole_ref[at : at + sz.tile, :] = part
+            for ref, (start, size) in zip(chunk_refs, sz.chunks):
+                if start <= at < start + size:
+                    ref[at - start : at - start + sz.tile, :] = part
 
 
 def pack(sz, matrix, in_mask):
@@ -86,7 +91,7 @@
     sizes = [sz.pay_rows] + [size for _, size in sz.chunks]
     return pl.pallas_call(
         functools.partial(pack_kernel, sz),
-        out_shape=[pltpu.VMEM((size, sz.tile), jnp.bfloat16) for size in sizes],
+        out_shape=[pltpu.VMEM((size, sz.wide), jnp.bfloat16) for size in sizes],
         in_specs=[pl.BlockSpec(memory_space=pltpu.SMEM), vmem],
         out_specs=[vmem] * len(sizes),
         compiler_params=pltpu.CompilerParams(vmem_limit_bytes=VMEM_LIMIT),
@@ -104,8 +109,16 @@
     return slots
 
 
-def slot_rows(sz, slot):
-    return pl.ds(pl.multiple_of(CODE_ROWS + slot * sz.tile, 16), sz.tile)
+def load_tile(sz, buf, slot):
+    at = CODE_ROWS + slot * sz.slot
+    parts = [
+        buf[pl.ds(pl.multiple_of(at + j * sz.tile, 16), sz.tile), :] for j in range(sz.parts)
+    ]
+    return jnp.concatenate(parts, axis=1)
+
+
+def clear_spare(sz, buf):
+    buf[sz.pay_rows :, :] = jnp.zeros((sz.slot, sz.wide), jnp.bfloat16)
 
 
 def expand_kernel(sz, n, *refs):
@@ -115,15 +128,14 @@
         copy = pltpu.make_async_copy(pays[p], buf.at[p, pl.ds(0, sz.pay_rows)], sems.at[p])
         copy.start()
         copies.append(copy)
-        buf[p, sz.pay_rows :, :] = jnp.zeros((sz.tile, sz.tile), jnp.bfloat16)
+        clear_spare(sz, buf.at[p])
     for p in range(n):
         copies[p].wait()
-        slots = slots_of(sz, buf[p, 0:CODE_ROWS, 0:128])
+        slots = slots_of(sz, buf[p, 0:CODE_ROWS, :])
         for t in range(sz.tr * sz.tc):
             a, k = t // sz.tc, t % sz.tc
-            dense[p][a * sz.tile : (a + 1) * sz.tile, k * sz.tile : (k + 1) * sz.tile] = buf[
-                p, slot_rows(sz, slots[t]), :
-            ]
+            rows, cols = slice(a * sz.tile, (a + 1) * sz.tile), slice(k * sz.tile, (k + 1) * sz.tile)
+            dense[p][rows, cols] = load_tile(sz, buf.at[p], slots[t])
 
 
 def expand(sz, pays, weight=1):
@@ -134,7 +146,7 @@
         in_specs=[pl.BlockSpec(memory_space=pltpu.HBM)] * n,
         out_specs=[pl.BlockSpec(memory_space=pltpu.VMEM)] * n,
         scratch_shapes=[
-            pltpu.VMEM((n, sz.buf_rows, sz.tile), jnp.bfloat16),
+            pltpu.VMEM((n, sz.buf_rows, sz.wide), jnp.bfloat16),
             pltpu.SemaphoreType.DMA((n,)),
         ],
         compiler_params=pltpu.CompilerParams(vmem_limit_bytes=2 * VMEM_LIMIT),
@@ -144,7 +156,7 @@
 
 
 def load_right(sz, buf, slots, b):
-    tiles = [buf[slot_rows(sz, slots[k * sz.tc + b]), :] for k in range(sz.tr)]
+    tiles = [load_tile(sz, buf, slots[k * sz.tc + b]) for k in range(sz.tr)]
     return jnp.concatenate(tiles, axis=0)
 
 
@@ -194,11 +206,11 @@
             copy.start()
 
     def add(p):
-        buf[p, sz.pay_rows :, :] = jnp.zeros((sz.tile, sz.tile), jnp.bfloat16)
+        clear_spare(sz, buf.at[p])
         wait_left(sz, blocks, left.at[p], sems.at[p * per_piece])
         for copy in copies(p):
             copy.wait()
-        slots = slots_of(sz, buf[p, 0:CODE_ROWS, 0:128])
+        slots = slots_of(sz, buf[p, 0:CODE_ROWS, :])
         for b in range(sz.tc):
             cols = slice(b * sz.tile, (b + 1) * sz.tile)
             term = jnp.dot(
@@ -245,7 +257,7 @@
         in_specs=in_specs,
         out_specs=[vmem] * len(out_shape),
         scratch_shapes=[
-            pltpu.VMEM((n, sz.buf_rows, sz.tile), jnp.bfloat16),
+            pltpu.VMEM((n, sz.buf_rows, sz.wide), jnp.bfloat16),
             pltpu.VMEM((n, sz.rows, sz.rows), jnp.bfloat16),
             pltpu.SemaphoreType.DMA((n * (len(sz.chunks) + 1) + max(1, len(then)),)),
         ],
@@ -264,8 +276,8 @@
     for p in range(n):
         for ref, chunk in zip(pays[p], sz.chunks):
             buf[p, pl.ds(*chunk), :] = ref[...]
-        buf[p, sz.pay_rows :, :] = jnp.zeros((sz.tile, sz.tile), jnp.bfloat16)
-        slots.append(slots_of(sz, buf[p, 0:CODE_ROWS, 0:128]))
+        clear_spare(sz, buf.at[p])
+        slots.append(slots_of(sz, buf[p, 0:CODE_ROWS, :]))
     for b in range(sz.tc):
         cols = slice(b * sz.tile, (b + 1) * sz.tile)
         total = before_ref[:, cols]
@@ -287,7 +299,7 @@
         out_shape=jax.ShapeDtypeStruct((sz.rows, sz.cols), jnp.float32),
         in_specs=[vmem] * len(args),
         out_specs=vmem,
-        scratch_shapes=[pltpu.VMEM((n, sz.buf_rows, sz.tile), jnp.bfloat16)],
+        scratch_shapes=[pltpu.VMEM((n, sz.buf_rows, sz.wide), jnp.bfloat16)],
         compiler_params=pltpu.CompilerParams(vmem_limit_bytes=VMEM_LIMIT),
         cost_estimate=cost(),
         name="product_near",
@@ -326,8 +338,8 @@
     def _():
         for ref, chunk in zip(pays, sz.chunks):
             buf[pl.ds(*chunk), :] = ref[...]
-        buf[sz.pay_rows :, :] = jnp.zeros((sz.tile, sz.tile), jnp.bfloat16)
-        slots = slots_of(sz, buf[0:CODE_ROWS, 0:128])
+        clear_spare(sz, buf)
+        slots = slots_of(sz, buf[0:CODE_ROWS, :])
         for b in range(sz.tc):
             cols = slice(b * sz.tile, (b + 1) * sz.tile)
             block = before_ref[:, cols] + jnp.dot(
@@ -359,7 +371,7 @@
         ],
         in_specs=[vmem] * len(args),
         out_specs=[vmem] * 2,
-        scratch_shapes=[pltpu.VMEM((sz.buf_rows, sz.tile), jnp.bfloat16)],
+        scratch_shapes=[pltpu.VMEM((sz.buf_rows, sz.wide), jnp.bfloat16)],
         compiler_params=pltpu.CompilerParams(vmem_limit_bytes=VMEM_LIMIT),
         cost_estimate=cost(),
         name="product_last",

time: 77.2 us -> 76.9 us (level)
  no operation moved by 1% of the time
where the time goes in v4:
time: 76.9 us; the launch traced here: 76.5 us
  waiting for transfers between devices  32.6 us (42%)
  starting transfers between devices  28.9 us (38%)
  Pallas kernels  14.7 us (19%)
    ppermute x12, waiting for transfers between devices, hop(): return lax.ppermute(chunk, 'row', pairs)  26.8 us
    ppermute x12, starting transfers between devices, hop(): return lax.ppermute(chunk, 'row', pairs)  12.9 us
    pallas_call x2, Pallas kernels, product(): pl.pallas_call(functools.partial(product_kernel, sz, dist, keys, first, t...  7.4 us
    ppermute x4, starting transfers between devices, last_hop(): return lax.ppermute(chunk, ('row', 'col'), pairs)  7.2 us
    ppermute x3, starting transfers between devices, column_sums(): lax.ppermute(pair, 'row', [(q, (q + 2 * t) % sz.n_row) for q in range(sz....  4.57 us
    ppermute x3, starting transfers between devices, apart(): return lax.ppermute(value, 'col', [(q, q ^ far) for q in range(n_col)])  2.63 us
    ppermute x3, waiting for transfers between devices, column_sums(): lax.ppermute(pair, 'row', [(q, (q + 2 * t) % sz.n_row) for q in range(sz....  2.26 us
    ppermute x1, waiting for transfers between devices, column_sums(): lax.ppermute(sums, 'row', [(q, q ^ 1) for q in range(sz.n_row)])  2.03 us
  transfers between devices with their start and end apart: 23, of which 12 were waited for; matrix products, arithmetic and copies ran while one was open for 0% of the time, Pallas kernels for 15%

profile of v4, /device:TPU:0, one launch (start us, length us, event | category | flops | bytes accessed | tf_op | source)
XLA Modules:
  0.0 76.5 jit_solution(12394931813596591442)
XLA Ops:
  0.0 1.5 %pack_tiles.1 = (bf16[3088,128]{1,0:T(8,128)(2,1)S(1)}, bf16[1552,128]{1,0:T(8,128)(2,1)S(1)}, bf16[1536,128]{1,0:T(8,128)(2,1)S(1)}) custom-call(s32[2,4]{1,0:T(2,128)} %mask_ref.1, bf16[512,1024]{1,0:T(8,128)(2,1)} %matrix_ref.1), custom_call_target="tpu_custom_call" | custom-call | tf_op jit(solution)/shard_map/pack_tiles/pallas_call | solution.py:92
  1.5 0.5 collective-permute-start.4
  2.0 2.6 %collective-permute-start.2 = (bf16[1552,128]{1,0:T(8,128)(2,1)S(1)}, bf16[1552,128]{1,0:T(8,128)(2,1)S(1)}, u32[]{:S(2)}, u32[]{:S(2)}) collective-permute-start(bf16[1552,128]{1,0:T(8,128)(2,1)S(1)} %get-tuple-element.59.refs_4_), channel_id=1, source_target_pairs={{0,4},{4,12},{12,20},{20,28},{28,24},{24,16},{16,8},{8,0},{1,5},{5... | collective-permute-start | bytes 1191944 | tf_op jit(solution)/shard_map/ppermute | solution.py:442
  4.6 0.1 collective-permute-start.3
  4.7 0.0 collective-permute-done.4.refs_0_
  4.7 2.0 %collective-permute-start.5 = (bf16[3088,128]{1,0:T(8,128)(2,1)S(1)}, bf16[3088,128]{1,0:T(8,128)(2,1)S(1)}, u32[]{:S(2)}, u32[]{:S(2)}) collective-permute-start(bf16[3088,128]{1,0:T(8,128)(2,1)S(1)} %get-tuple-element.49.refs_0_), channel_id=1, source_target_pairs={{0,2},{1,3},{2,0},{3,1},{4,6},{5,7},{6,4},{7,5},{8,10},{9,11},{10,... | collective-permute-start | bytes 2371592 | tf_op jit(solution)/shard_map/ppermute | solution.py:453
  6.8 1.6 %collective-permute-start.1 = (bf16[1552,128]{1,0:T(8,128)(2,1)S(1)}, bf16[1552,128]{1,0:T(8,128)(2,1)S(1)}, u32[]{:S(2)}, u32[]{:S(2)}) collective-permute-start(bf16[1552,128]{1,0:T(8,128)(2,1)S(1)} %get-tuple-element.59.refs_4_), channel_id=1, source_target_pairs={{0,8},{4,0},{12,4},{20,12},{28,20},{24,28},{16,24},{8,16},{1,9},{5... | collective-permute-start | bytes 1191944 | tf_op jit(solution)/shard_map/ppermute | solution.py:442
  8.4 0.4 collective-permute-start
  8.8 7.7 %collective-permute-done.3.refs_9_.refs_11_ = bf16[1536,128]{1,0:T(8,128)(2,1)S(1)} collective-permute-done((bf16[1536,128]{1,0:T(8,128)(2,1)S(1)}, bf16[1536,128]{1,0:T(8,128)(2,1)S(1)}, u32[]{:S(2)}, u32[]{:S(2)}) %collective-permute-start.3) | collective-permute-done | bytes 393248 | tf_op jit(solution)/shard_map/ppermute | solution.py:442
  16.5 1.6 %collective-permute-start.9 = (bf16[1552,128]{1,0:T(8,128)(2,1)S(1)}, bf16[1552,128]{1,0:T(8,128)(2,1)S(1)}, u32[]{:S(2)}, u32[]{:S(2)}) collective-permute-start(bf16[1552,128]{1,0:T(8,128)(2,1)S(1)} %collective-permute-done.2.refs_6_.refs_8_), channel_id=1, source_target_pairs={{0,4},{4,12},{12,20},{20,28},{28,24},{24,16},{16,8},{8,0},{1,5},{5... | collective-permute-start | bytes 1191944 | tf_op jit(solution)/shard_map/ppermute | solution.py:442
  18.1 0.4 collective-permute-start.10
  18.6 0.4 expand_tiles.3.refs_0_
  19.0 4.2 %collective-permute-done.refs_7_.refs_9_ = bf16[1536,128]{1,0:T(8,128)(2,1)S(1)} collective-permute-done((bf16[1536,128]{1,0:T(8,128)(2,1)S(1)}, bf16[1536,128]{1,0:T(8,128)(2,1)S(1)}, u32[]{:S(2)}, u32[]{:S(2)}) %collective-permute-start) | collective-permute-done | bytes 393248 | tf_op jit(solution)/shard_map/ppermute | solution.py:442
  23.1 1.9 %collective-permute-done.1.refs_8_.refs_10_ = bf16[1552,128]{1,0:T(8,128)(2,1)S(1)} collective-permute-done((bf16[1552,128]{1,0:T(8,128)(2,1)S(1)}, bf16[1552,128]{1,0:T(8,128)(2,1)S(1)}, u32[]{:S(2)}, u32[]{:S(2)}) %collective-permute-start.1) | collective-permute-done | bytes 397344 | tf_op jit(solution)/shard_map/ppermute | solution.py:442
  25.1 0.1 collective-permute-start.8
  25.2 1.9 %collective-permute-start.7 = (bf16[1536,128]{1,0:T(8,128)(2,1)S(1)}, bf16[1536,128]{1,0:T(8,128)(2,1)S(1)}, u32[]{:S(2)}, u32[]{:S(2)}) collective-permute-start(bf16[1536,128]{1,0:T(8,128)(2,1)S(1)} %collective-permute-done.refs_7_.refs_9_), channel_id=1, source_target_pairs={{0,4},{4,12},{12,20},{20,28},{28,24},{24,16},{16,8},{8,0},{1,5},{5... | collective-permute-start | bytes 1179656 | tf_op jit(solution)/shard_map/ppermute | solution.py:442
  27.1 0.6 keep_rows.1.keep_ref
  27.7 0.0 collective-permute-done.5.refs_0_
  27.7 0.1 collective-permute-start.6
  27.7 0.4 expand_tiles.4.refs_1_
  28.1 5.3 %collective-permute-done.10.refs_7_ = bf16[1536,128]{1,0:T(8,128)(2,1)S(1)} collective-permute-done((bf16[1536,128]{1,0:T(8,128)(2,1)S(1)}, bf16[1536,128]{1,0:T(8,128)(2,1)S(1)}, u32[]{:S(2)}, u32[]{:S(2)}) %collective-permute-start.10) | collective-permute-done | bytes 393248 | tf_op jit(solution)/shard_map/ppermute | solution.py:442
  33.5 1.6 %collective-permute-start.11 = (bf16[1552,128]{1,0:T(8,128)(2,1)S(1)}, bf16[1552,128]{1,0:T(8,128)(2,1)S(1)}, u32[]{:S(2)}, u32[]{:S(2)}) collective-permute-start(bf16[1552,128]{1,0:T(8,128)(2,1)S(1)} %collective-permute-done.9.refs_4_), channel_id=1, source_target_pairs={{0,4},{4,12},{12,20},{20,28},{28,24},{24,16},{16,8},{8,0},{1,5},{5... | collective-permute-start | bytes 1191944 | tf_op jit(solution)/shard_map/ppermute | solution.py:442
  35.1 0.4 collective-permute-start.12
  35.5 4.5 %collective-permute-done.7.refs_5_ = bf16[1536,128]{1,0:T(8,128)(2,1)S(1)} collective-permute-done((bf16[1536,128]{1,0:T(8,128)(2,1)S(1)}, bf16[1536,128]{1,0:T(8,128)(2,1)S(1)}, u32[]{:S(2)}, u32[]{:S(2)}) %collective-permute-start.7) | collective-permute-done | bytes 393248 | tf_op jit(solution)/shard_map/ppermute | solution.py:442
  40.1 1.9 %collective-permute-done.8.refs_6_ = bf16[1552,128]{1,0:T(8,128)(2,1)S(1)} collective-permute-done((bf16[1552,128]{1,0:T(8,128)(2,1)S(1)}, bf16[1552,128]{1,0:T(8,128)(2,1)S(1)}, u32[]{:S(2)}, u32[]{:S(2)}) %collective-permute-start.8) | collective-permute-done | bytes 397344 | tf_op jit(solution)/shard_map/ppermute | solution.py:442
  42.0 1.6 %collective-permute-start.15 = (bf16[1536,128]{1,0:T(8,128)(2,1)S(1)}, bf16[1536,128]{1,0:T(8,128)(2,1)S(1)}, u32[]{:S(2)}, u32[]{:S(2)}) collective-permute-start(bf16[1536,128]{1,0:T(8,128)(2,1)S(1)} %collective-permute-done.7.refs_5_), channel_id=1, source_target_pairs={{0,4},{4,12},{12,20},{20,28},{28,24},{24,16},{16,8},{8,0},{1,5},{5... | collective-permute-start | bytes 1179656 | tf_op jit(solution)/shard_map/ppermute | solution.py:442
  43.6 0.4 collective-permute-start.16
  44.0 0.0 collective-permute-done.6.refs_1_
  44.0 0.8 %expand_tiles.5 = (bf16[512,1024]{1,0:T(8,128)(2,1)S(1)}, bf16[512,1024]{1,0:T(8,128)(2,1)S(1)}) custom-call(bf16[3088,128]{1,0:T(8,128)(2,1)S(1)} %collective-permute-done.5.refs_0_, bf16[3088,128]{1,0:T(8,128)(2,1)S(1)} %collective-permute-done.6.refs_1_), custom_call_target="tpu_custom_call" | custom-call | flops 536870912 | tf_op jit(solution)/shard_map/expand_tiles/pallas_call | solution.py:143
  44.8 4.5 %product.2 = (f32[512,1024]{1,0:T(8,128)S(1)}, bf16[512,512]{1,0:T(8,128)(2,1)S(1)}, bf16[512,512]{1,0:T(8,128)(2,1)S(1)}, bf16[512,512]{1,0:T(8,128)(2,1)S(1)}) custom-call(bf16[512,1024]{1,0:T(8,128)(2,1)S(1)} %expand_tiles.3.refs_0_, bf16[512,1024]{1,0:T(8,128)(2,1)S(1)} %expand_tiles.4.refs_1_, bf16[512,1024]{1,0:T(8,128)(2,1)S(1)} %get-tuple-element.57.refs_2_, ...), custom_call_target="tpu_custom_call" | custom-call | flops 536870912 | tf_op jit(solution)/shard_map/product/pallas_call | solution.py:254
  49.3 1.1 %collective-permute-done.12.refs_5_ = bf16[1536,128]{1,0:T(8,128)(2,1)S(1)} collective-permute-done((bf16[1536,128]{1,0:T(8,128)(2,1)S(1)}, bf16[1536,128]{1,0:T(8,128)(2,1)S(1)}, u32[]{:S(2)}, u32[]{:S(2)}) %collective-permute-start.12) | collective-permute-done | bytes 393248 | tf_op jit(solution)/shard_map/ppermute | solution.py:442
  50.4 3.5 %collective-permute-start.13 = (bf16[1552,128]{1,0:T(8,128)(2,1)S(1)}, bf16[1552,128]{1,0:T(8,128)(2,1)S(1)}, u32[]{:S(2)}, u32[]{:S(2)}) collective-permute-start(bf16[1552,128]{1,0:T(8,128)(2,1)S(1)} %collective-permute-done.11.refs_2_), channel_id=1, source_target_pairs={{0,4},{1,1},{2,6},{3,3},{4,12},{5,5},{6,14},{7,7},{12,20},{13,13},... | collective-permute-start | bytes 1191944 | tf_op jit(solution)/shard_map/ppermute | solution.py:450
  53.9 2.4 %collective-permute-start.14 = (bf16[1536,128]{1,0:T(8,128)(2,1)S(1)}, bf16[1536,128]{1,0:T(8,128)(2,1)S(1)}, u32[]{:S(2)}, u32[]{:S(2)}) collective-permute-start(bf16[1536,128]{1,0:T(8,128)(2,1)S(1)} %collective-permute-done.12.refs_5_), channel_id=1, source_target_pairs={{0,8},{1,1},{2,10},{3,3},{4,0},{5,5},{6,2},{7,7},{12,4},{13,13},{1... | collective-permute-start | bytes 1179656 | tf_op jit(solution)/shard_map/ppermute | solution.py:450
  56.3 2.9 %product.3.refs_6_ = f32[512,1024]{1,0:T(8,128)S(1)} custom-call(bf16[512,1024]{1,0:T(8,128)(2,1)S(1)} %expand_tiles.3.refs_0_, bf16[512,1024]{1,0:T(8,128)(2,1)S(1)} %expand_tiles.4.refs_1_, bf16[512,1024]{1,0:T(8,128)(2,1)S(1)} %get-tuple-element.57.refs_2_, bf16[512,1024]{1,0:T(8,128)(2,1)S(1)} %get-tuple-element.58.refs_3_, ...), custom_call_target="tpu_custom_call" | custom-call | flops 536870912 | tf_op jit(solution)/shard_map/product/pallas_call | solution.py:254
  59.2 0.7 collective-permute-start.17
  59.9 0.7 collective-permute-start.18
  60.6 1.4 %product_near.1.refs_2_ = f32[512,1024]{1,0:T(8,128)S(1)} custom-call(bf16[512,512]{1,0:T(8,128)(2,1)S(1)} %get-tuple-element.64.refs_0_, bf16[512,512]{1,0:T(8,128)(2,1)S(1)} %get-tuple-element.65.refs_1_, bf16[1552,128]{1,0:T(8,128)(2,1)S(1)} %collective-permute-done.11.refs_2_, bf16[1536,128]{1,0:T(8,128)(2,1)S(1)} %collective-permute-done.15.refs_3_, ...), custom_call_target="tpu_custom_call" | custom-call | flops 536870912 | tf_op jit(solution)/shard_map/product_near/pallas_call | solution.py:297
  62.0 1.6 %collective-permute-done.14.refs_1_ = bf16[1536,128]{1,0:T(8,128)(2,1)S(1)} collective-permute-done((bf16[1536,128]{1,0:T(8,128)(2,1)S(1)}, bf16[1536,128]{1,0:T(8,128)(2,1)S(1)}, u32[]{:S(2)}, u32[]{:S(2)}) %collective-permute-start.14) | collective-permute-done | bytes 393248 | tf_op jit(solution)/shard_map/ppermute | solution.py:450
  63.6 0.9 %product_last.2 = (f32[512,1024]{1,0:T(8,128)S(1)}, f32[1,1024]{1,0:T(1,128)S(1)}) custom-call(f32[16,1024]{1,0:T(8,128)S(1)} %keep_rows.1.keep_ref, bf16[512,512]{1,0:T(8,128)(2,1)S(1)} %get-tuple-element.60.left_ref, bf16[1552,128]{1,0:T(8,128)(2,1)S(1)} %collective-permute-done.13.refs_0_, bf16[1536,128]{1,0:T(8,128)(2,1)S(1)} %collective-permute-done.14.refs_1_, ...), custom_call_target="tpu_custom_call" | custom-call | flops 536870912 | tf_op jit(solution)/shard_map/product_last/pallas_call | solution.py:366
  64.5 1.6 %collective-permute-start.19 = (f32[1,1024]{1,0:T(1,128)S(1)}, f32[1,1024]{1,0:T(1,128)S(1)}, u32[]{:S(2)}, u32[]{:S(2)}) collective-permute-start(f32[1,1024]{1,0:T(1,128)S(1)} %get-tuple-element.72), channel_id=1, source_target_pairs={{0,4},{4,0},{8,12},{12,8},{16,20},{20,16},{24,28},{28,24},{1,5},{5... | collective-permute-start | bytes 12296 | tf_op jit(solution)/shard_map/ppermute | solution.py:421
  66.2 2.0 %collective-permute-done.19 = f32[1,1024]{1,0:T(1,128)S(1)} collective-permute-done((f32[1,1024]{1,0:T(1,128)S(1)}, f32[1,1024]{1,0:T(1,128)S(1)}, u32[]{:S(2)}, u32[]{:S(2)}) %collective-permute-start.19) | collective-permute-done | bytes 4128 | tf_op jit(solution)/shard_map/ppermute | solution.py:421
  68.2 1.1 %collective-permute-start.20 = (f32[1,1024]{1,0:T(1,128)S(1)}, f32[1,1024]{1,0:T(1,128)S(1)}, u32[]{:S(2)}, u32[]{:S(2)}) collective-permute-start(f32[1,1024]{1,0:T(1,128)S(1)} %add.12), channel_id=1, source_target_pairs={{0,8},{4,12},{8,16},{12,20},{16,24},{20,28},{24,0},{28,4},{1,9},{5... | collective-permute-start | bytes 12296 | tf_op jit(solution)/shard_map/ppermute | solution.py:423
  69.4 2.1 %collective-permute-start.21 = (f32[1,1024]{1,0:T(1,128)S(1)}, f32[1,1024]{1,0:T(1,128)S(1)}, u32[]{:S(2)}, u32[]{:S(2)}) collective-permute-start(f32[1,1024]{1,0:T(1,128)S(1)} %add.12), channel_id=1, source_target_pairs={{0,16},{4,20},{8,24},{12,28},{16,0},{20,4},{24,8},{28,12},{1,17},{... | collective-permute-start | bytes 12296 | tf_op jit(solution)/shard_map/ppermute | solution.py:423
  71.4 1.3 %collective-permute-start.22 = (f32[1,1024]{1,0:T(1,128)S(1)}, f32[1,1024]{1,0:T(1,128)S(1)}, u32[]{:S(2)}, u32[]{:S(2)}) collective-permute-start(f32[1,1024]{1,0:T(1,128)S(1)} %add.12), channel_id=1, source_target_pairs={{0,24},{4,28},{8,0},{12,4},{16,8},{20,12},{24,16},{28,20},{1,25},{... | collective-permute-start | bytes 12296 | tf_op jit(solution)/shard_map/ppermute | solution.py:423
  72.8 0.8 %collective-permute-done.20 = f32[1,1024]{1,0:T(1,128)S(1)} collective-permute-done((f32[1,1024]{1,0:T(1,128)S(1)}, f32[1,1024]{1,0:T(1,128)S(1)}, u32[]{:S(2)}, u32[]{:S(2)}) %collective-permute-start.20) | collective-permute-done | bytes 4128 | tf_op jit(solution)/shard_map/ppermute | solution.py:423
  73.6 0.2 collective-permute-done.21
  73.9 1.2 %collective-permute-done.22 = f32[1,1024]{1,0:T(1,128)S(1)} collective-permute-done((f32[1,1024]{1,0:T(1,128)S(1)}, f32[1,1024]{1,0:T(1,128)S(1)}, u32[]{:S(2)}, u32[]{:S(2)}) %collective-permute-start.22) | collective-permute-done | bytes 4128 | tf_op jit(solution)/shard_map/ppermute | solution.py:423
  75.1 1.4 %scale.1 = f32[512,1024]{1,0:T(8,128)} custom-call(f32[512,1024]{1,0:T(8,128)S(1)} %get-tuple-element.67.first_ref, f32[512,1024]{1,0:T(8,128)S(1)} %get-tuple-element.71.second_ref, f32[1,1024]{1,0:T(1,128)S(1)} %add_add_fusion.totals_ref), custom_call_target="tpu_custom_call" | custom-call | flops 536870912 | tf_op jit(solution)/shard_map/scale/pallas_call | solution.py:403
  (13 shorter events, 0.1 us)
Async XLA Ops:
  1.5 3.2 %collective-permute-start.4 = (bf16[3088,128]{1,0:T(8,128)(2,1)S(1)}, bf16[3088,128]{1,0:T(8,128)(2,1)S(1)}, u32[]{:S(2)}, u32[]{:S(2)}) collective-permute-start(bf16[3088,128]{1,0:T(8,128)(2,1)S(1)} %get-tuple-element.49.refs_0_), channel_id=1, source_target_pairs={{0,1},{1,0},{2,3},{3,2},{4,5},{5,4},{6,7},{7,6},{8,9},{9,8},{10,11... | collective-permute-start | bytes 2371592 | tf_op jit(solution)/shard_map/ppermute | solution.py:453
  2.0 14.5 %collective-permute-start.2 = (bf16[1552,128]{1,0:T(8,128)(2,1)S(1)}, bf16[1552,128]{1,0:T(8,128)(2,1)S(1)}, u32[]{:S(2)}, u32[]{:S(2)}) collective-permute-start(bf16[1552,128]{1,0:T(8,128)(2,1)S(1)} %get-tuple-element.59.refs_4_), channel_id=1, source_target_pairs={{0,4},{4,12},{12,20},{20,28},{28,24},{24,16},{16,8},{8,0},{1,5},{5... | collective-permute-start | bytes 1191944 | tf_op jit(solution)/shard_map/ppermute | solution.py:442
  4.6 22.5 %copy-start = (s32[2,4]{1,0:T(2,128)S(1)}, s32[2,4]{1,0:T(2,128)}, u32[]{:S(2)}) copy-start(s32[2,4]{1,0:T(2,128)} %out_mask_ref) | copy-start | bytes 100
  4.6 12.0 %collective-permute-start.3 = (bf16[1536,128]{1,0:T(8,128)(2,1)S(1)}, bf16[1536,128]{1,0:T(8,128)(2,1)S(1)}, u32[]{:S(2)}, u32[]{:S(2)}) collective-permute-start(bf16[1536,128]{1,0:T(8,128)(2,1)S(1)} %get-tuple-element.39.refs_5_), channel_id=1, source_target_pairs={{0,8},{4,0},{12,4},{20,12},{28,20},{24,28},{16,24},{8,16},{1,9},{5... | collective-permute-start | bytes 1179656 | tf_op jit(solution)/shard_map/ppermute | solution.py:442
  4.7 22.9 %collective-permute-start.5 = (bf16[3088,128]{1,0:T(8,128)(2,1)S(1)}, bf16[3088,128]{1,0:T(8,128)(2,1)S(1)}, u32[]{:S(2)}, u32[]{:S(2)}) collective-permute-start(bf16[3088,128]{1,0:T(8,128)(2,1)S(1)} %get-tuple-element.49.refs_0_), channel_id=1, source_target_pairs={{0,2},{1,3},{2,0},{3,1},{4,6},{5,7},{6,4},{7,5},{8,10},{9,11},{10,... | collective-permute-start | bytes 2371592 | tf_op jit(solution)/shard_map/ppermute | solution.py:453
  6.8 18.3 %collective-permute-start.1 = (bf16[1552,128]{1,0:T(8,128)(2,1)S(1)}, bf16[1552,128]{1,0:T(8,128)(2,1)S(1)}, u32[]{:S(2)}, u32[]{:S(2)}) collective-permute-start(bf16[1552,128]{1,0:T(8,128)(2,1)S(1)} %get-tuple-element.59.refs_4_), channel_id=1, source_target_pairs={{0,8},{4,0},{12,4},{20,12},{28,20},{24,28},{16,24},{8,16},{1,9},{5... | collective-permute-start | bytes 1191944 | tf_op jit(solution)/shard_map/ppermute | solution.py:442
  8.4 14.8 %collective-permute-start = (bf16[1536,128]{1,0:T(8,128)(2,1)S(1)}, bf16[1536,128]{1,0:T(8,128)(2,1)S(1)}, u32[]{:S(2)}, u32[]{:S(2)}) collective-permute-start(bf16[1536,128]{1,0:T(8,128)(2,1)S(1)} %get-tuple-element.39.refs_5_), channel_id=1, source_target_pairs={{0,4},{4,12},{12,20},{20,28},{28,24},{24,16},{16,8},{8,0},{1,5},{5... | collective-permute-start | bytes 1179656 | tf_op jit(solution)/shard_map/ppermute | solution.py:442
  16.5 16.9 %collective-permute-start.9 = (bf16[1552,128]{1,0:T(8,128)(2,1)S(1)}, bf16[1552,128]{1,0:T(8,128)(2,1)S(1)}, u32[]{:S(2)}, u32[]{:S(2)}) collective-permute-start(bf16[1552,128]{1,0:T(8,128)(2,1)S(1)} %collective-permute-done.2.refs_6_.refs_8_), channel_id=1, source_target_pairs={{0,4},{4,12},{12,20},{20,28},{28,24},{24,16},{16,8},{8,0},{1,5},{5... | collective-permute-start | bytes 1191944 | tf_op jit(solution)/shard_map/ppermute | solution.py:442
  18.1 15.4 %collective-permute-start.10 = (bf16[1536,128]{1,0:T(8,128)(2,1)S(1)}, bf16[1536,128]{1,0:T(8,128)(2,1)S(1)}, u32[]{:S(2)}, u32[]{:S(2)}) collective-permute-start(bf16[1536,128]{1,0:T(8,128)(2,1)S(1)} %collective-permute-done.3.refs_9_.refs_11_), channel_id=1, source_target_pairs={{0,8},{4,0},{12,4},{20,12},{28,20},{24,28},{16,24},{8,16},{1,9},{5... | collective-permute-start | bytes 1179656 | tf_op jit(solution)/shard_map/ppermute | solution.py:442
  25.1 16.9 %collective-permute-start.8 = (bf16[1552,128]{1,0:T(8,128)(2,1)S(1)}, bf16[1552,128]{1,0:T(8,128)(2,1)S(1)}, u32[]{:S(2)}, u32[]{:S(2)}) collective-permute-start(bf16[1552,128]{1,0:T(8,128)(2,1)S(1)} %collective-permute-done.1.refs_8_.refs_10_), channel_id=1, source_target_pairs={{0,8},{4,0},{12,4},{20,12},{28,20},{24,28},{16,24},{8,16},{1,9},{5... | collective-permute-start | bytes 1191944 | tf_op jit(solution)/shard_map/ppermute | solution.py:442
  25.2 14.9 %collective-permute-start.7 = (bf16[1536,128]{1,0:T(8,128)(2,1)S(1)}, bf16[1536,128]{1,0:T(8,128)(2,1)S(1)}, u32[]{:S(2)}, u32[]{:S(2)}) collective-permute-start(bf16[1536,128]{1,0:T(8,128)(2,1)S(1)} %collective-permute-done.refs_7_.refs_9_), channel_id=1, source_target_pairs={{0,4},{4,12},{12,20},{20,28},{28,24},{24,16},{16,8},{8,0},{1,5},{5... | collective-permute-start | bytes 1179656 | tf_op jit(solution)/shard_map/ppermute | solution.py:442
  27.7 16.4 %collective-permute-start.6 = (bf16[3088,128]{1,0:T(8,128)(2,1)S(1)}, bf16[3088,128]{1,0:T(8,128)(2,1)S(1)}, u32[]{:S(2)}, u32[]{:S(2)}) collective-permute-start(bf16[3088,128]{1,0:T(8,128)(2,1)S(1)} %collective-permute-done.5.refs_0_), channel_id=1, source_target_pairs={{0,1},{1,0},{2,3},{3,2},{4,5},{5,4},{6,7},{7,6},{8,9},{9,8},{10,11... | collective-permute-start | bytes 2371592 | tf_op jit(solution)/shard_map/ppermute | solution.py:453
  33.5 16.9 %collective-permute-start.11 = (bf16[1552,128]{1,0:T(8,128)(2,1)S(1)}, bf16[1552,128]{1,0:T(8,128)(2,1)S(1)}, u32[]{:S(2)}, u32[]{:S(2)}) collective-permute-start(bf16[1552,128]{1,0:T(8,128)(2,1)S(1)} %collective-permute-done.9.refs_4_), channel_id=1, source_target_pairs={{0,4},{4,12},{12,20},{20,28},{28,24},{24,16},{16,8},{8,0},{1,5},{5... | collective-permute-start | bytes 1191944 | tf_op jit(solution)/shard_map/ppermute | solution.py:442
  35.1 15.4 %collective-permute-start.12 = (bf16[1536,128]{1,0:T(8,128)(2,1)S(1)}, bf16[1536,128]{1,0:T(8,128)(2,1)S(1)}, u32[]{:S(2)}, u32[]{:S(2)}) collective-permute-start(bf16[1536,128]{1,0:T(8,128)(2,1)S(1)} %collective-permute-done.10.refs_7_), channel_id=1, source_target_pairs={{0,8},{4,0},{12,4},{20,12},{28,20},{24,28},{16,24},{8,16},{1,9},{5... | collective-permute-start | bytes 1179656 | tf_op jit(solution)/shard_map/ppermute | solution.py:442
  42.0 17.9 %collective-permute-start.15 = (bf16[1536,128]{1,0:T(8,128)(2,1)S(1)}, bf16[1536,128]{1,0:T(8,128)(2,1)S(1)}, u32[]{:S(2)}, u32[]{:S(2)}) collective-permute-start(bf16[1536,128]{1,0:T(8,128)(2,1)S(1)} %collective-permute-done.7.refs_5_), channel_id=1, source_target_pairs={{0,4},{4,12},{12,20},{20,28},{28,24},{24,16},{16,8},{8,0},{1,5},{5... | collective-permute-start | bytes 1179656 | tf_op jit(solution)/shard_map/ppermute | solution.py:442
  43.6 17.0 %collective-permute-start.16 = (bf16[1552,128]{1,0:T(8,128)(2,1)S(1)}, bf16[1552,128]{1,0:T(8,128)(2,1)S(1)}, u32[]{:S(2)}, u32[]{:S(2)}) collective-permute-start(bf16[1552,128]{1,0:T(8,128)(2,1)S(1)} %collective-permute-done.8.refs_6_), channel_id=1, source_target_pairs={{0,8},{4,0},{12,4},{20,12},{28,20},{24,28},{16,24},{8,16},{1,9},{5... | collective-permute-start | bytes 1191944 | tf_op jit(solution)/shard_map/ppermute | solution.py:442
  50.4 13.2 %collective-permute-start.13 = (bf16[1552,128]{1,0:T(8,128)(2,1)S(1)}, bf16[1552,128]{1,0:T(8,128)(2,1)S(1)}, u32[]{:S(2)}, u32[]{:S(2)}) collective-permute-start(bf16[1552,128]{1,0:T(8,128)(2,1)S(1)} %collective-permute-done.11.refs_2_), channel_id=1, source_target_pairs={{0,4},{1,1},{2,6},{3,3},{4,12},{5,5},{6,14},{7,7},{12,20},{13,13},... | collective-permute-start | bytes 1191944 | tf_op jit(solution)/shard_map/ppermute | solution.py:450
  53.9 9.7 %collective-permute-start.14 = (bf16[1536,128]{1,0:T(8,128)(2,1)S(1)}, bf16[1536,128]{1,0:T(8,128)(2,1)S(1)}, u32[]{:S(2)}, u32[]{:S(2)}) collective-permute-start(bf16[1536,128]{1,0:T(8,128)(2,1)S(1)} %collective-permute-done.12.refs_5_), channel_id=1, source_target_pairs={{0,8},{1,1},{2,10},{3,3},{4,0},{5,5},{6,2},{7,7},{12,4},{13,13},{1... | collective-permute-start | bytes 1179656 | tf_op jit(solution)/shard_map/ppermute | solution.py:450
  59.2 5.3 %collective-permute-start.17 = (bf16[1552,128]{1,0:T(8,128)(2,1)S(1)}, bf16[1552,128]{1,0:T(8,128)(2,1)S(1)}, u32[]{:S(2)}, u32[]{:S(2)}) collective-permute-start(bf16[1552,128]{1,0:T(8,128)(2,1)S(1)} %collective-permute-done.11.refs_2_), channel_id=1, source_target_pairs={{0,0},{1,5},{2,2},{3,7},{4,4},{5,13},{6,6},{7,15},{12,12},{13,21},... | collective-permute-start | bytes 1191944 | tf_op jit(solution)/shard_map/ppermute | solution.py:450
  59.9 4.6 %collective-permute-start.18 = (bf16[1536,128]{1,0:T(8,128)(2,1)S(1)}, bf16[1536,128]{1,0:T(8,128)(2,1)S(1)}, u32[]{:S(2)}, u32[]{:S(2)}) collective-permute-start(bf16[1536,128]{1,0:T(8,128)(2,1)S(1)} %collective-permute-done.12.refs_5_), channel_id=1, source_target_pairs={{0,0},{1,9},{2,2},{3,11},{4,4},{5,1},{6,6},{7,3},{12,12},{13,5},{1... | collective-permute-start | bytes 1179656 | tf_op jit(solution)/shard_map/ppermute | solution.py:450
  64.5 3.7 %collective-permute-start.19 = (f32[1,1024]{1,0:T(1,128)S(1)}, f32[1,1024]{1,0:T(1,128)S(1)}, u32[]{:S(2)}, u32[]{:S(2)}) collective-permute-start(f32[1,1024]{1,0:T(1,128)S(1)} %get-tuple-element.72), channel_id=1, source_target_pairs={{0,4},{4,0},{8,12},{12,8},{16,20},{20,16},{24,28},{28,24},{1,5},{5... | collective-permute-start | bytes 12296 | tf_op jit(solution)/shard_map/ppermute | solution.py:421
  68.2 5.4 %collective-permute-start.20 = (f32[1,1024]{1,0:T(1,128)S(1)}, f32[1,1024]{1,0:T(1,128)S(1)}, u32[]{:S(2)}, u32[]{:S(2)}) collective-permute-start(f32[1,1024]{1,0:T(1,128)S(1)} %add.12), channel_id=1, source_target_pairs={{0,8},{4,12},{8,16},{12,20},{16,24},{20,28},{24,0},{28,4},{1,9},{5... | collective-permute-start | bytes 12296 | tf_op jit(solution)/shard_map/ppermute | solution.py:423
  69.4 4.5 %collective-permute-start.21 = (f32[1,1024]{1,0:T(1,128)S(1)}, f32[1,1024]{1,0:T(1,128)S(1)}, u32[]{:S(2)}, u32[]{:S(2)}) collective-permute-start(f32[1,1024]{1,0:T(1,128)S(1)} %add.12), channel_id=1, source_target_pairs={{0,16},{4,20},{8,24},{12,28},{16,0},{20,4},{24,8},{28,12},{1,17},{... | collective-permute-start | bytes 12296 | tf_op jit(solution)/shard_map/ppermute | solution.py:423
  71.4 3.6 %collective-permute-start.22 = (f32[1,1024]{1,0:T(1,128)S(1)}, f32[1,1024]{1,0:T(1,128)S(1)}, u32[]{:S(2)}, u32[]{:S(2)}) collective-permute-start(f32[1,1024]{1,0:T(1,128)S(1)} %add.12), channel_id=1, source_target_pairs={{0,24},{4,28},{8,0},{12,4},{16,8},{20,12},{24,16},{28,20},{1,25},{... | collective-permute-start | bytes 12296 | tf_op jit(solution)/shard_map/ppermute | solution.py:423

commit v5 on v4

--- a/solution.py
+++ b/solution.py
@@ -441,12 +441,14 @@
         pairs = [(ring[p], ring[(p + way) % n_row]) for p in range(n_row)]
         return lax.ppermute(chunk, "row", pairs)
 
-    def last_hop(chunk, way, core):
-        pairs = [
-            (ring[p] * n_col + c, (ring[(p + way) % n_row] if c % 2 == core else ring[p]) * n_col + c)
-            for p in range(n_row)
-            for c in range(n_col)
-        ]
+    def last_hop(chunk, way, core, keep=False):
+        aside = 2 if n_col % 4 == 0 and not keep else 0
+        pairs = []
+        for p in range(n_row):
+            for c in range(n_col):
+                mine = c % 2 == core
+                to = (ring[(p + way) % n_row], c) if mine else (ring[p], c ^ aside)
+                pairs.append((ring[p] * n_col + c, to[0] * n_col + to[1]))
         return lax.ppermute(chunk, ("row", "col"), pairs)
 
     def apart(value, far):
@@ -521,8 +523,8 @@
                 lefts = lefts or more
             gate.append(acc)
         if i + 3 == len(arrivals):
-            final = after(final, acc)
-            second = [last_hop(chunk, way, 1) for chunk, way in zip(final, (1, -1))]
+            early = last_hop(after(final[:1], acc)[0], 1, 1, keep=True)
+    second = [early, last_hop(after(final[1:], *here)[0], -1, 1)]
     left = lefts[2]
     mine, sums = last_product(sz, 0, acc, left, first, keep)
     other, sums = last_product(sz, 1, acc, left, second, keep, sums)

time: 76.9 us -> 77.9 us (1.013)
  waiting for transfers between devices: 32.6 us -> 36.5 us
  starting transfers between devices: 28.9 us -> 26.3 us
    ppermute x4, starting transfers between devices: 7.2 us -> 4.2 us  [last_hop(): return lax.ppermute(chunk, ('row', 'col'), pairs)]
    ppermute x4, waiting for transfers between devices: 1.56 us -> 3.93 us  [last_hop(): return lax.ppermute(chunk, ('row', 'col'), pairs)]
    ppermute x12, waiting for transfers between devices: 26.8 us -> 28.9 us  [hop(): return lax.ppermute(chunk, 'row', pairs)]
  transfers between devices with their start and end apart: 23 -> 23, of which waited for: 12 -> 15; matrix products, arithmetic and copies ran while one was open for 0% -> 0% of each run, Pallas kernels for 15% -> 15%
where the time goes in v5:
time: 77.9 us; the launch traced here: 77.7 us
  waiting for transfers between devices  36.5 us (47%)
  starting transfers between devices  26.3 us (34%)
  Pallas kernels  14.7 us (19%)
    ppermute x12, waiting for transfers between devices, hop(): return lax.ppermute(chunk, 'row', pairs)  28.9 us
    ppermute x12, starting transfers between devices, hop(): return lax.ppermute(chunk, 'row', pairs)  12.9 us
    pallas_call x2, Pallas kernels, product(): pl.pallas_call(functools.partial(product_kernel, sz, dist, keys, first, t...  7.36 us
    ppermute x3, starting transfers between devices, column_sums(): lax.ppermute(pair, 'row', [(q, (q + 2 * t) % sz.n_row) for q in range(sz....  5.07 us
    ppermute x4, starting transfers between devices, last_hop(): return lax.ppermute(chunk, ('row', 'col'), pairs)  4.2 us
    ppermute x4, waiting for transfers between devices, last_hop(): return lax.ppermute(chunk, ('row', 'col'), pairs)  3.93 us
    ppermute x3, starting transfers between devices, apart(): return lax.ppermute(value, 'col', [(q, q ^ far) for q in range(n_col)])  2.63 us
    ppermute x1, waiting for transfers between devices, column_sums(): lax.ppermute(sums, 'row', [(q, q ^ 1) for q in range(sz.n_row)])  2.03 us
  transfers between devices with their start and end apart: 23, of which 15 were waited for; matrix products, arithmetic and copies ran while one was open for 0% of the time, Pallas kernels for 15%

profile of v5, /device:TPU:0, one launch (start us, length us, event | category | flops | bytes accessed | tf_op | source)
XLA Modules:
  0.0 77.7 jit_solution(12021692670211994320)
XLA Ops:
  0.0 1.5 %pack_tiles.1 = (bf16[3088,128]{1,0:T(8,128)(2,1)S(1)}, bf16[1552,128]{1,0:T(8,128)(2,1)S(1)}, bf16[1536,128]{1,0:T(8,128)(2,1)S(1)}) custom-call(s32[2,4]{1,0:T(2,128)} %mask_ref.1, bf16[512,1024]{1,0:T(8,128)(2,1)} %matrix_ref.1), custom_call_target="tpu_custom_call" | custom-call | tf_op jit(solution)/shard_map/pack_tiles/pallas_call | solution.py:92
  1.5 0.5 collective-permute-start.4
  2.0 2.6 %collective-permute-start.2 = (bf16[1552,128]{1,0:T(8,128)(2,1)S(1)}, bf16[1552,128]{1,0:T(8,128)(2,1)S(1)}, u32[]{:S(2)}, u32[]{:S(2)}) collective-permute-start(bf16[1552,128]{1,0:T(8,128)(2,1)S(1)} %get-tuple-element.62.refs_4_), channel_id=1, source_target_pairs={{0,4},{4,12},{12,20},{20,28},{28,24},{24,16},{16,8},{8,0},{1,5},{5... | collective-permute-start | bytes 1191944 | tf_op jit(solution)/shard_map/ppermute | solution.py:442
  4.6 0.1 collective-permute-start.3
  4.7 2.0 %collective-permute-start.5 = (bf16[3088,128]{1,0:T(8,128)(2,1)S(1)}, bf16[3088,128]{1,0:T(8,128)(2,1)S(1)}, u32[]{:S(2)}, u32[]{:S(2)}) collective-permute-start(bf16[3088,128]{1,0:T(8,128)(2,1)S(1)} %get-tuple-element.52.refs_0_), channel_id=1, source_target_pairs={{0,2},{1,3},{2,0},{3,1},{4,6},{5,7},{6,4},{7,5},{8,10},{9,11},{10,... | collective-permute-start | bytes 2371592 | tf_op jit(solution)/shard_map/ppermute | solution.py:455
  6.8 1.6 %collective-permute-start.1 = (bf16[1552,128]{1,0:T(8,128)(2,1)S(1)}, bf16[1552,128]{1,0:T(8,128)(2,1)S(1)}, u32[]{:S(2)}, u32[]{:S(2)}) collective-permute-start(bf16[1552,128]{1,0:T(8,128)(2,1)S(1)} %get-tuple-element.62.refs_4_), channel_id=1, source_target_pairs={{0,8},{4,0},{12,4},{20,12},{28,20},{24,28},{16,24},{8,16},{1,9},{5... | collective-permute-start | bytes 1191944 | tf_op jit(solution)/shard_map/ppermute | solution.py:442
  8.4 0.4 collective-permute-start
  8.8 7.7 %collective-permute-done.3.refs_9_.refs_11_ = bf16[1536,128]{1,0:T(8,128)(2,1)S(1)} collective-permute-done((bf16[1536,128]{1,0:T(8,128)(2,1)S(1)}, bf16[1536,128]{1,0:T(8,128)(2,1)S(1)}, u32[]{:S(2)}, u32[]{:S(2)}) %collective-permute-start.3) | collective-permute-done | bytes 393248 | tf_op jit(solution)/shard_map/ppermute | solution.py:442
  16.5 1.6 %collective-permute-start.9 = (bf16[1552,128]{1,0:T(8,128)(2,1)S(1)}, bf16[1552,128]{1,0:T(8,128)(2,1)S(1)}, u32[]{:S(2)}, u32[]{:S(2)}) collective-permute-start(bf16[1552,128]{1,0:T(8,128)(2,1)S(1)} %collective-permute-done.2.refs_6_.refs_8_), channel_id=1, source_target_pairs={{0,4},{4,12},{12,20},{20,28},{28,24},{24,16},{16,8},{8,0},{1,5},{5... | collective-permute-start | bytes 1191944 | tf_op jit(solution)/shard_map/ppermute | solution.py:442
  18.1 0.4 collective-permute-start.10
  18.6 0.4 expand_tiles.3.refs_0_
  19.0 4.2 %collective-permute-done.refs_7_.refs_9_ = bf16[1536,128]{1,0:T(8,128)(2,1)S(1)} collective-permute-done((bf16[1536,128]{1,0:T(8,128)(2,1)S(1)}, bf16[1536,128]{1,0:T(8,128)(2,1)S(1)}, u32[]{:S(2)}, u32[]{:S(2)}) %collective-permute-start) | collective-permute-done | bytes 393248 | tf_op jit(solution)/shard_map/ppermute | solution.py:442
  23.1 1.9 %collective-permute-done.1.refs_8_.refs_10_ = bf16[1552,128]{1,0:T(8,128)(2,1)S(1)} collective-permute-done((bf16[1552,128]{1,0:T(8,128)(2,1)S(1)}, bf16[1552,128]{1,0:T(8,128)(2,1)S(1)}, u32[]{:S(2)}, u32[]{:S(2)}) %collective-permute-start.1) | collective-permute-done | bytes 397344 | tf_op jit(solution)/shard_map/ppermute | solution.py:442
  25.1 0.1 collective-permute-start.8
  25.2 1.9 %collective-permute-start.7 = (bf16[1536,128]{1,0:T(8,128)(2,1)S(1)}, bf16[1536,128]{1,0:T(8,128)(2,1)S(1)}, u32[]{:S(2)}, u32[]{:S(2)}) collective-permute-start(bf16[1536,128]{1,0:T(8,128)(2,1)S(1)} %collective-permute-done.refs_7_.refs_9_), channel_id=1, source_target_pairs={{0,4},{4,12},{12,20},{20,28},{28,24},{24,16},{16,8},{8,0},{1,5},{5... | collective-permute-start | bytes 1179656 | tf_op jit(solution)/shard_map/ppermute | solution.py:442
  27.1 0.6 keep_rows.1.keep_ref
  27.7 0.1 collective-permute-start.6
  27.7 0.4 expand_tiles.4.refs_1_
  28.1 5.3 %collective-permute-done.10.refs_7_ = bf16[1536,128]{1,0:T(8,128)(2,1)S(1)} collective-permute-done((bf16[1536,128]{1,0:T(8,128)(2,1)S(1)}, bf16[1536,128]{1,0:T(8,128)(2,1)S(1)}, u32[]{:S(2)}, u32[]{:S(2)}) %collective-permute-start.10) | collective-permute-done | bytes 393248 | tf_op jit(solution)/shard_map/ppermute | solution.py:442
  33.5 1.6 %collective-permute-start.11 = (bf16[1552,128]{1,0:T(8,128)(2,1)S(1)}, bf16[1552,128]{1,0:T(8,128)(2,1)S(1)}, u32[]{:S(2)}, u32[]{:S(2)}) collective-permute-start(bf16[1552,128]{1,0:T(8,128)(2,1)S(1)} %collective-permute-done.9.refs_4_), channel_id=1, source_target_pairs={{0,4},{4,12},{12,20},{20,28},{28,24},{24,16},{16,8},{8,0},{1,5},{5... | collective-permute-start | bytes 1191944 | tf_op jit(solution)/shard_map/ppermute | solution.py:442
  35.1 0.4 collective-permute-start.12
  35.5 4.5 %collective-permute-done.7.refs_5_ = bf16[1536,128]{1,0:T(8,128)(2,1)S(1)} collective-permute-done((bf16[1536,128]{1,0:T(8,128)(2,1)S(1)}, bf16[1536,128]{1,0:T(8,128)(2,1)S(1)}, u32[]{:S(2)}, u32[]{:S(2)}) %collective-permute-start.7) | collective-permute-done | bytes 393248 | tf_op jit(solution)/shard_map/ppermute | solution.py:442
  40.1 1.9 %collective-permute-done.8.refs_6_ = bf16[1552,128]{1,0:T(8,128)(2,1)S(1)} collective-permute-done((bf16[1552,128]{1,0:T(8,128)(2,1)S(1)}, bf16[1552,128]{1,0:T(8,128)(2,1)S(1)}, u32[]{:S(2)}, u32[]{:S(2)}) %collective-permute-start.8) | collective-permute-done | bytes 397344 | tf_op jit(solution)/shard_map/ppermute | solution.py:442
  42.0 0.1 collective-permute-start.16
  42.1 1.9 %collective-permute-start.15 = (bf16[1536,128]{1,0:T(8,128)(2,1)S(1)}, bf16[1536,128]{1,0:T(8,128)(2,1)S(1)}, u32[]{:S(2)}, u32[]{:S(2)}) collective-permute-start(bf16[1536,128]{1,0:T(8,128)(2,1)S(1)} %collective-permute-done.7.refs_5_), channel_id=1, source_target_pairs={{0,4},{4,12},{12,20},{20,28},{28,24},{24,16},{16,8},{8,0},{1,5},{5... | collective-permute-start | bytes 1179656 | tf_op jit(solution)/shard_map/ppermute | solution.py:442
  44.0 0.8 expand_tiles.5
  44.8 4.5 %product.2 = (f32[512,1024]{1,0:T(8,128)S(1)}, bf16[512,512]{1,0:T(8,128)(2,1)S(1)}, bf16[512,512]{1,0:T(8,128)(2,1)S(1)}, bf16[512,512]{1,0:T(8,128)(2,1)S(1)}) custom-call(bf16[512,1024]{1,0:T(8,128)(2,1)S(1)} %expand_tiles.3.refs_0_, bf16[512,1024]{1,0:T(8,128)(2,1)S(1)} %expand_tiles.4.refs_1_, bf16[512,1024]{1,0:T(8,128)(2,1)S(1)} %get-tuple-element.60.refs_2_, ...), custom_call_target="tpu_custom_call" | custom-call | flops 536870912 | tf_op jit(solution)/shard_map/product/pallas_call | solution.py:254
  49.3 1.1 %collective-permute-done.12.refs_5_ = bf16[1536,128]{1,0:T(8,128)(2,1)S(1)} collective-permute-done((bf16[1536,128]{1,0:T(8,128)(2,1)S(1)}, bf16[1536,128]{1,0:T(8,128)(2,1)S(1)}, u32[]{:S(2)}, u32[]{:S(2)}) %collective-permute-start.12) | collective-permute-done | bytes 393248 | tf_op jit(solution)/shard_map/ppermute | solution.py:442
  50.4 1.6 %collective-permute-start.13 = (bf16[1552,128]{1,0:T(8,128)(2,1)S(1)}, bf16[1552,128]{1,0:T(8,128)(2,1)S(1)}, u32[]{:S(2)}, u32[]{:S(2)}) collective-permute-start(bf16[1552,128]{1,0:T(8,128)(2,1)S(1)} %collective-permute-done.11.refs_2_), channel_id=1, source_target_pairs={{0,4},{1,3},{2,6},{3,1},{4,12},{5,7},{6,14},{7,5},{12,20},{13,15},... | collective-permute-start | bytes 1191944 | tf_op jit(solution)/shard_map/ppermute | solution.py:452
  52.0 0.4 collective-permute-start.14
  52.5 2.8 %product.3.refs_6_ = f32[512,1024]{1,0:T(8,128)S(1)} custom-call(bf16[512,1024]{1,0:T(8,128)(2,1)S(1)} %expand_tiles.3.refs_0_, bf16[512,1024]{1,0:T(8,128)(2,1)S(1)} %expand_tiles.4.refs_1_, bf16[512,1024]{1,0:T(8,128)(2,1)S(1)} %get-tuple-element.60.refs_2_, bf16[512,1024]{1,0:T(8,128)(2,1)S(1)} %get-tuple-element.61.refs_3_, ...), custom_call_target="tpu_custom_call" | custom-call | flops 536870912 | tf_op jit(solution)/shard_map/product/pallas_call | solution.py:254
  55.3 0.7 collective-permute-start.17
  56.0 0.8 collective-permute-done.15.refs_3_
  56.8 1.4 %collective-permute-done.16.refs_4_ = bf16[1552,128]{1,0:T(8,128)(2,1)S(1)} collective-permute-done((bf16[1552,128]{1,0:T(8,128)(2,1)S(1)}, bf16[1552,128]{1,0:T(8,128)(2,1)S(1)}, u32[]{:S(2)}, u32[]{:S(2)}) %collective-permute-start.16) | collective-permute-done | bytes 397344 | tf_op jit(solution)/shard_map/ppermute | solution.py:442
  58.2 1.5 %collective-permute-start.18 = (bf16[1536,128]{1,0:T(8,128)(2,1)S(1)}, bf16[1536,128]{1,0:T(8,128)(2,1)S(1)}, u32[]{:S(2)}, u32[]{:S(2)}) collective-permute-start(bf16[1536,128]{1,0:T(8,128)(2,1)S(1)} %collective-permute-done.12.refs_5_), channel_id=1, source_target_pairs={{0,2},{1,9},{2,0},{3,11},{4,6},{5,1},{6,4},{7,3},{12,14},{13,5},{1... | collective-permute-start | bytes 1179656 | tf_op jit(solution)/shard_map/ppermute | solution.py:452
  59.7 1.4 %product_near.1.refs_2_ = f32[512,1024]{1,0:T(8,128)S(1)} custom-call(bf16[512,512]{1,0:T(8,128)(2,1)S(1)} %get-tuple-element.67.refs_0_, bf16[512,512]{1,0:T(8,128)(2,1)S(1)} %get-tuple-element.68.refs_1_, bf16[1552,128]{1,0:T(8,128)(2,1)S(1)} %collective-permute-done.11.refs_2_, bf16[1536,128]{1,0:T(8,128)(2,1)S(1)} %collective-permute-done.15.refs_3_, ...), custom_call_target="tpu_custom_call" | custom-call | flops 536870912 | tf_op jit(solution)/shard_map/product_near/pallas_call | solution.py:297
  61.1 1.6 %collective-permute-done.14.refs_1_ = bf16[1536,128]{1,0:T(8,128)(2,1)S(1)} collective-permute-done((bf16[1536,128]{1,0:T(8,128)(2,1)S(1)}, bf16[1536,128]{1,0:T(8,128)(2,1)S(1)}, u32[]{:S(2)}, u32[]{:S(2)}) %collective-permute-start.14) | collective-permute-done | bytes 393248 | tf_op jit(solution)/shard_map/ppermute | solution.py:452
  62.8 0.9 %product_last.2 = (f32[512,1024]{1,0:T(8,128)S(1)}, f32[1,1024]{1,0:T(1,128)S(1)}) custom-call(f32[16,1024]{1,0:T(8,128)S(1)} %keep_rows.1.keep_ref, bf16[512,512]{1,0:T(8,128)(2,1)S(1)} %get-tuple-element.63.left_ref, bf16[1552,128]{1,0:T(8,128)(2,1)S(1)} %collective-permute-done.13.refs_0_, bf16[1536,128]{1,0:T(8,128)(2,1)S(1)} %collective-permute-done.14.refs_1_, ...), custom_call_target="tpu_custom_call" | custom-call | flops 536870912 | tf_op jit(solution)/shard_map/product_last/pallas_call | solution.py:366
  63.7 2.3 %collective-permute-done.18.refs_1_ = bf16[1536,128]{1,0:T(8,128)(2,1)S(1)} collective-permute-done((bf16[1536,128]{1,0:T(8,128)(2,1)S(1)}, bf16[1536,128]{1,0:T(8,128)(2,1)S(1)}, u32[]{:S(2)}, u32[]{:S(2)}) %collective-permute-start.18) | collective-permute-done | bytes 393248 | tf_op jit(solution)/shard_map/ppermute | solution.py:452
  65.9 1.6 %collective-permute-start.19 = (f32[1,1024]{1,0:T(1,128)S(1)}, f32[1,1024]{1,0:T(1,128)S(1)}, u32[]{:S(2)}, u32[]{:S(2)}) collective-permute-start(f32[1,1024]{1,0:T(1,128)S(1)} %get-tuple-element.78), channel_id=1, source_target_pairs={{0,4},{4,0},{8,12},{12,8},{16,20},{20,16},{24,28},{28,24},{1,5},{5... | collective-permute-start | bytes 12296 | tf_op jit(solution)/shard_map/ppermute | solution.py:421
  67.5 2.0 %collective-permute-done.19 = f32[1,1024]{1,0:T(1,128)S(1)} collective-permute-done((f32[1,1024]{1,0:T(1,128)S(1)}, f32[1,1024]{1,0:T(1,128)S(1)}, u32[]{:S(2)}, u32[]{:S(2)}) %collective-permute-start.19) | collective-permute-done | bytes 4128 | tf_op jit(solution)/shard_map/ppermute | solution.py:421
  69.6 1.1 %collective-permute-start.20 = (f32[1,1024]{1,0:T(1,128)S(1)}, f32[1,1024]{1,0:T(1,128)S(1)}, u32[]{:S(2)}, u32[]{:S(2)}) collective-permute-start(f32[1,1024]{1,0:T(1,128)S(1)} %add.12), channel_id=1, source_target_pairs={{0,8},{4,12},{8,16},{12,20},{16,24},{20,28},{24,0},{28,4},{1,9},{5... | collective-permute-start | bytes 12296 | tf_op jit(solution)/shard_map/ppermute | solution.py:423
  70.7 2.0 %collective-permute-start.21 = (f32[1,1024]{1,0:T(1,128)S(1)}, f32[1,1024]{1,0:T(1,128)S(1)}, u32[]{:S(2)}, u32[]{:S(2)}) collective-permute-start(f32[1,1024]{1,0:T(1,128)S(1)} %add.12), channel_id=1, source_target_pairs={{0,16},{4,20},{8,24},{12,28},{16,0},{20,4},{24,8},{28,12},{1,17},{... | collective-permute-start | bytes 12296 | tf_op jit(solution)/shard_map/ppermute | solution.py:423
  72.7 2.0 %collective-permute-start.22 = (f32[1,1024]{1,0:T(1,128)S(1)}, f32[1,1024]{1,0:T(1,128)S(1)}, u32[]{:S(2)}, u32[]{:S(2)}) collective-permute-start(f32[1,1024]{1,0:T(1,128)S(1)} %add.12), channel_id=1, source_target_pairs={{0,24},{4,28},{8,0},{12,4},{16,8},{20,12},{24,16},{28,20},{1,25},{... | collective-permute-start | bytes 12296 | tf_op jit(solution)/shard_map/ppermute | solution.py:423
  74.6 0.3 collective-permute-done.20
  75.0 0.2 collective-permute-done.21
  75.2 1.1 %collective-permute-done.22 = f32[1,1024]{1,0:T(1,128)S(1)} collective-permute-done((f32[1,1024]{1,0:T(1,128)S(1)}, f32[1,1024]{1,0:T(1,128)S(1)}, u32[]{:S(2)}, u32[]{:S(2)}) %collective-permute-start.22) | collective-permute-done | bytes 4128 | tf_op jit(solution)/shard_map/ppermute | solution.py:423
  76.3 1.4 %scale.1 = f32[512,1024]{1,0:T(8,128)} custom-call(f32[512,1024]{1,0:T(8,128)S(1)} %get-tuple-element.73.first_ref, f32[512,1024]{1,0:T(8,128)S(1)} %get-tuple-element.77.second_ref, f32[1,1024]{1,0:T(1,128)S(1)} %add_add_fusion.totals_ref), custom_call_target="tpu_custom_call" | custom-call | flops 536870912 | tf_op jit(solution)/shard_map/scale/pallas_call | solution.py:403
  (13 shorter events, 0.0 us)
Async XLA Ops:
  1.5 3.2 %collective-permute-start.4 = (bf16[3088,128]{1,0:T(8,128)(2,1)S(1)}, bf16[3088,128]{1,0:T(8,128)(2,1)S(1)}, u32[]{:S(2)}, u32[]{:S(2)}) collective-permute-start(bf16[3088,128]{1,0:T(8,128)(2,1)S(1)} %get-tuple-element.52.refs_0_), channel_id=1, source_target_pairs={{0,1},{1,0},{2,3},{3,2},{4,5},{5,4},{6,7},{7,6},{8,9},{9,8},{10,11... | collective-permute-start | bytes 2371592 | tf_op jit(solution)/shard_map/ppermute | solution.py:455
  2.0 14.5 %collective-permute-start.2 = (bf16[1552,128]{1,0:T(8,128)(2,1)S(1)}, bf16[1552,128]{1,0:T(8,128)(2,1)S(1)}, u32[]{:S(2)}, u32[]{:S(2)}) collective-permute-start(bf16[1552,128]{1,0:T(8,128)(2,1)S(1)} %get-tuple-element.62.refs_4_), channel_id=1, source_target_pairs={{0,4},{4,12},{12,20},{20,28},{28,24},{24,16},{16,8},{8,0},{1,5},{5... | collective-permute-start | bytes 1191944 | tf_op jit(solution)/shard_map/ppermute | solution.py:442
  4.6 22.5 %copy-start = (s32[2,4]{1,0:T(2,128)S(1)}, s32[2,4]{1,0:T(2,128)}, u32[]{:S(2)}) copy-start(s32[2,4]{1,0:T(2,128)} %out_mask_ref) | copy-start | bytes 100
  4.6 12.0 %collective-permute-start.3 = (bf16[1536,128]{1,0:T(8,128)(2,1)S(1)}, bf16[1536,128]{1,0:T(8,128)(2,1)S(1)}, u32[]{:S(2)}, u32[]{:S(2)}) collective-permute-start(bf16[1536,128]{1,0:T(8,128)(2,1)S(1)} %get-tuple-element.42.refs_5_), channel_id=1, source_target_pairs={{0,8},{4,0},{12,4},{20,12},{28,20},{24,28},{16,24},{8,16},{1,9},{5... | collective-permute-start | bytes 1179656 | tf_op jit(solution)/shard_map/ppermute | solution.py:442
  4.7 22.9 %collective-permute-start.5 = (bf16[3088,128]{1,0:T(8,128)(2,1)S(1)}, bf16[3088,128]{1,0:T(8,128)(2,1)S(1)}, u32[]{:S(2)}, u32[]{:S(2)}) collective-permute-start(bf16[3088,128]{1,0:T(8,128)(2,1)S(1)} %get-tuple-element.52.refs_0_), channel_id=1, source_target_pairs={{0,2},{1,3},{2,0},{3,1},{4,6},{5,7},{6,4},{7,5},{8,10},{9,11},{10,... | collective-permute-start | bytes 2371592 | tf_op jit(solution)/shard_map/ppermute | solution.py:455
  6.8 18.3 %collective-permute-start.1 = (bf16[1552,128]{1,0:T(8,128)(2,1)S(1)}, bf16[1552,128]{1,0:T(8,128)(2,1)S(1)}, u32[]{:S(2)}, u32[]{:S(2)}) collective-permute-start(bf16[1552,128]{1,0:T(8,128)(2,1)S(1)} %get-tuple-element.62.refs_4_), channel_id=1, source_target_pairs={{0,8},{4,0},{12,4},{20,12},{28,20},{24,28},{16,24},{8,16},{1,9},{5... | collective-permute-start | bytes 1191944 | tf_op jit(solution)/shard_map/ppermute | solution.py:442
  8.4 14.8 %collective-permute-start = (bf16[1536,128]{1,0:T(8,128)(2,1)S(1)}, bf16[1536,128]{1,0:T(8,128)(2,1)S(1)}, u32[]{:S(2)}, u32[]{:S(2)}) collective-permute-start(bf16[1536,128]{1,0:T(8,128)(2,1)S(1)} %get-tuple-element.42.refs_5_), channel_id=1, source_target_pairs={{0,4},{4,12},{12,20},{20,28},{28,24},{24,16},{16,8},{8,0},{1,5},{5... | collective-permute-start | bytes 1179656 | tf_op jit(solution)/shard_map/ppermute | solution.py:442
  16.5 16.9 %collective-permute-start.9 = (bf16[1552,128]{1,0:T(8,128)(2,1)S(1)}, bf16[1552,128]{1,0:T(8,128)(2,1)S(1)}, u32[]{:S(2)}, u32[]{:S(2)}) collective-permute-start(bf16[1552,128]{1,0:T(8,128)(2,1)S(1)} %collective-permute-done.2.refs_6_.refs_8_), channel_id=1, source_target_pairs={{0,4},{4,12},{12,20},{20,28},{28,24},{24,16},{16,8},{8,0},{1,5},{5... | collective-permute-start | bytes 1191944 | tf_op jit(solution)/shard_map/ppermute | solution.py:442
  18.1 15.4 %collective-permute-start.10 = (bf16[1536,128]{1,0:T(8,128)(2,1)S(1)}, bf16[1536,128]{1,0:T(8,128)(2,1)S(1)}, u32[]{:S(2)}, u32[]{:S(2)}) collective-permute-start(bf16[1536,128]{1,0:T(8,128)(2,1)S(1)} %collective-permute-done.3.refs_9_.refs_11_), channel_id=1, source_target_pairs={{0,8},{4,0},{12,4},{20,12},{28,20},{24,28},{16,24},{8,16},{1,9},{5... | collective-permute-start | bytes 1179656 | tf_op jit(solution)/shard_map/ppermute | solution.py:442
  25.1 16.9 %collective-permute-start.8 = (bf16[1552,128]{1,0:T(8,128)(2,1)S(1)}, bf16[1552,128]{1,0:T(8,128)(2,1)S(1)}, u32[]{:S(2)}, u32[]{:S(2)}) collective-permute-start(bf16[1552,128]{1,0:T(8,128)(2,1)S(1)} %collective-permute-done.1.refs_8_.refs_10_), channel_id=1, source_target_pairs={{0,8},{4,0},{12,4},{20,12},{28,20},{24,28},{16,24},{8,16},{1,9},{5... | collective-permute-start | bytes 1191944 | tf_op jit(solution)/shard_map/ppermute | solution.py:442
  25.2 14.9 %collective-permute-start.7 = (bf16[1536,128]{1,0:T(8,128)(2,1)S(1)}, bf16[1536,128]{1,0:T(8,128)(2,1)S(1)}, u32[]{:S(2)}, u32[]{:S(2)}) collective-permute-start(bf16[1536,128]{1,0:T(8,128)(2,1)S(1)} %collective-permute-done.refs_7_.refs_9_), channel_id=1, source_target_pairs={{0,4},{4,12},{12,20},{20,28},{28,24},{24,16},{16,8},{8,0},{1,5},{5... | collective-permute-start | bytes 1179656 | tf_op jit(solution)/shard_map/ppermute | solution.py:442
  27.7 16.4 %collective-permute-start.6 = (bf16[3088,128]{1,0:T(8,128)(2,1)S(1)}, bf16[3088,128]{1,0:T(8,128)(2,1)S(1)}, u32[]{:S(2)}, u32[]{:S(2)}) collective-permute-start(bf16[3088,128]{1,0:T(8,128)(2,1)S(1)} %collective-permute-done.5.refs_0_), channel_id=1, source_target_pairs={{0,1},{1,0},{2,3},{3,2},{4,5},{5,4},{6,7},{7,6},{8,9},{9,8},{10,11... | collective-permute-start | bytes 2371592 | tf_op jit(solution)/shard_map/ppermute | solution.py:455
  33.5 16.9 %collective-permute-start.11 = (bf16[1552,128]{1,0:T(8,128)(2,1)S(1)}, bf16[1552,128]{1,0:T(8,128)(2,1)S(1)}, u32[]{:S(2)}, u32[]{:S(2)}) collective-permute-start(bf16[1552,128]{1,0:T(8,128)(2,1)S(1)} %collective-permute-done.9.refs_4_), channel_id=1, source_target_pairs={{0,4},{4,12},{12,20},{20,28},{28,24},{24,16},{16,8},{8,0},{1,5},{5... | collective-permute-start | bytes 1191944 | tf_op jit(solution)/shard_map/ppermute | solution.py:442
  35.1 15.4 %collective-permute-start.12 = (bf16[1536,128]{1,0:T(8,128)(2,1)S(1)}, bf16[1536,128]{1,0:T(8,128)(2,1)S(1)}, u32[]{:S(2)}, u32[]{:S(2)}) collective-permute-start(bf16[1536,128]{1,0:T(8,128)(2,1)S(1)} %collective-permute-done.10.refs_7_), channel_id=1, source_target_pairs={{0,8},{4,0},{12,4},{20,12},{28,20},{24,28},{16,24},{8,16},{1,9},{5... | collective-permute-start | bytes 1179656 | tf_op jit(solution)/shard_map/ppermute | solution.py:442
  42.0 16.2 %collective-permute-start.16 = (bf16[1552,128]{1,0:T(8,128)(2,1)S(1)}, bf16[1552,128]{1,0:T(8,128)(2,1)S(1)}, u32[]{:S(2)}, u32[]{:S(2)}) collective-permute-start(bf16[1552,128]{1,0:T(8,128)(2,1)S(1)} %collective-permute-done.8.refs_6_), channel_id=1, source_target_pairs={{0,8},{4,0},{12,4},{20,12},{28,20},{24,28},{16,24},{8,16},{1,9},{5... | collective-permute-start | bytes 1191944 | tf_op jit(solution)/shard_map/ppermute | solution.py:442
  42.1 14.6 %collective-permute-start.15 = (bf16[1536,128]{1,0:T(8,128)(2,1)S(1)}, bf16[1536,128]{1,0:T(8,128)(2,1)S(1)}, u32[]{:S(2)}, u32[]{:S(2)}) collective-permute-start(bf16[1536,128]{1,0:T(8,128)(2,1)S(1)} %collective-permute-done.7.refs_5_), channel_id=1, source_target_pairs={{0,4},{4,12},{12,20},{20,28},{28,24},{24,16},{16,8},{8,0},{1,5},{5... | collective-permute-start | bytes 1179656 | tf_op jit(solution)/shard_map/ppermute | solution.py:442
  50.4 12.3 %collective-permute-start.13 = (bf16[1552,128]{1,0:T(8,128)(2,1)S(1)}, bf16[1552,128]{1,0:T(8,128)(2,1)S(1)}, u32[]{:S(2)}, u32[]{:S(2)}) collective-permute-start(bf16[1552,128]{1,0:T(8,128)(2,1)S(1)} %collective-permute-done.11.refs_2_), channel_id=1, source_target_pairs={{0,4},{1,3},{2,6},{3,1},{4,12},{5,7},{6,14},{7,5},{12,20},{13,15},... | collective-permute-start | bytes 1191944 | tf_op jit(solution)/shard_map/ppermute | solution.py:452
  52.0 10.7 %collective-permute-start.14 = (bf16[1536,128]{1,0:T(8,128)(2,1)S(1)}, bf16[1536,128]{1,0:T(8,128)(2,1)S(1)}, u32[]{:S(2)}, u32[]{:S(2)}) collective-permute-start(bf16[1536,128]{1,0:T(8,128)(2,1)S(1)} %collective-permute-done.12.refs_5_), channel_id=1, source_target_pairs={{0,8},{1,3},{2,10},{3,1},{4,0},{5,7},{6,2},{7,5},{12,4},{13,15},{1... | collective-permute-start | bytes 1179656 | tf_op jit(solution)/shard_map/ppermute | solution.py:452
  55.3 10.6 %collective-permute-start.17 = (bf16[1552,128]{1,0:T(8,128)(2,1)S(1)}, bf16[1552,128]{1,0:T(8,128)(2,1)S(1)}, u32[]{:S(2)}, u32[]{:S(2)}) collective-permute-start(bf16[1552,128]{1,0:T(8,128)(2,1)S(1)} %collective-permute-done.11.refs_2_), channel_id=1, source_target_pairs={{0,0},{1,5},{2,2},{3,7},{4,4},{5,13},{6,6},{7,15},{12,12},{13,21},... | collective-permute-start | bytes 1191944 | tf_op jit(solution)/shard_map/ppermute | solution.py:452
  58.2 7.8 %collective-permute-start.18 = (bf16[1536,128]{1,0:T(8,128)(2,1)S(1)}, bf16[1536,128]{1,0:T(8,128)(2,1)S(1)}, u32[]{:S(2)}, u32[]{:S(2)}) collective-permute-start(bf16[1536,128]{1,0:T(8,128)(2,1)S(1)} %collective-permute-done.12.refs_5_), channel_id=1, source_target_pairs={{0,2},{1,9},{2,0},{3,11},{4,6},{5,1},{6,4},{7,3},{12,14},{13,5},{1... | collective-permute-start | bytes 1179656 | tf_op jit(solution)/shard_map/ppermute | solution.py:452
  65.9 3.6 %collective-permute-start.19 = (f32[1,1024]{1,0:T(1,128)S(1)}, f32[1,1024]{1,0:T(1,128)S(1)}, u32[]{:S(2)}, u32[]{:S(2)}) collective-permute-start(f32[1,1024]{1,0:T(1,128)S(1)} %get-tuple-element.78), channel_id=1, source_target_pairs={{0,4},{4,0},{8,12},{12,8},{16,20},{20,16},{24,28},{28,24},{1,5},{5... | collective-permute-start | bytes 12296 | tf_op jit(solution)/shard_map/ppermute | solution.py:421
  69.6 5.4 %collective-permute-start.20 = (f32[1,1024]{1,0:T(1,128)S(1)}, f32[1,1024]{1,0:T(1,128)S(1)}, u32[]{:S(2)}, u32[]{:S(2)}) collective-permute-start(f32[1,1024]{1,0:T(1,128)S(1)} %add.12), channel_id=1, source_target_pairs={{0,8},{4,12},{8,16},{12,20},{16,24},{20,28},{24,0},{28,4},{1,9},{5... | collective-permute-start | bytes 12296 | tf_op jit(solution)/shard_map/ppermute | solution.py:423
  70.7 4.5 %collective-permute-start.21 = (f32[1,1024]{1,0:T(1,128)S(1)}, f32[1,1024]{1,0:T(1,128)S(1)}, u32[]{:S(2)}, u32[]{:S(2)}) collective-permute-start(f32[1,1024]{1,0:T(1,128)S(1)} %add.12), channel_id=1, source_target_pairs={{0,16},{4,20},{8,24},{12,28},{16,0},{20,4},{24,8},{28,12},{1,17},{... | collective-permute-start | bytes 12296 | tf_op jit(solution)/shard_map/ppermute | solution.py:423
  72.7 3.6 %collective-permute-start.22 = (f32[1,1024]{1,0:T(1,128)S(1)}, f32[1,1024]{1,0:T(1,128)S(1)}, u32[]{:S(2)}, u32[]{:S(2)}) collective-permute-start(f32[1,1024]{1,0:T(1,128)S(1)} %add.12), channel_id=1, source_target_pairs={{0,24},{4,28},{8,0},{12,4},{16,8},{20,12},{24,16},{28,20},{1,25},{... | collective-permute-start | bytes 12296 | tf_op jit(solution)/shard_map/ppermute | solution.py:423

commit v6 on v5

--- a/solution.py
+++ b/solution.py
@@ -506,9 +506,9 @@
             gate.append(keep)
         keys = None
         if i == 3:
-            keys = [(0, None), (1, 0), (-1, 0)]
+            keys = [(0, None), (1, None), (-1, 0)]
         elif i == 4:
-            keys = [(2, None), (-2, None), (1, 1), (-1, 1)]
+            keys = [(2, None), (-2, None), (-1, 1)]
         elif i > 4 and h == 1:
             keys = [(step, None), (-step, None)]
         if keys:
@@ -523,8 +523,8 @@
                 lefts = lefts or more
             gate.append(acc)
         if i + 3 == len(arrivals):
-            early = last_hop(after(final[:1], acc)[0], 1, 1, keep=True)
-    second = [early, last_hop(after(final[1:], *here)[0], -1, 1)]
+            final = after(final, acc)
+            second = [last_hop(chunk, way, 1, keep=True) for chunk, way in zip(final, (1, -1))]
     left = lefts[2]
     mine, sums = last_product(sz, 0, acc, left, first, keep)
     other, sums = last_product(sz, 1, acc, left, second, keep, sums)

time: 77.9 us -> 78 us (level)
  starting transfers between devices: 26.3 us -> 27.4 us
    ppermute x3, starting transfers between devices: 5.07 us -> 6.67 us  [column_sums(): lax.ppermute(pair, 'row', [(q, (q + 2 * t) % sz.n_row) for q in range(sz....]
    ppermute x4, starting transfers between devices: 4.2 us -> 3.39 us  [last_hop(): return lax.ppermute(chunk, ('row', 'col'), pairs)]
  transfers between devices with their start and end apart: 23 -> 23, of which waited for: 15 -> 14; matrix products, arithmetic and copies ran while one was open for 0% -> 0% of each run, Pallas kernels for 15% -> 15%
where the time goes in v6:
time: 78 us; the launch traced here: 77.8 us
  waiting for transfers between devices  35.8 us (46%)
  starting transfers between devices  27.4 us (35%)
  Pallas kernels  14.5 us (19%)
    ppermute x12, waiting for transfers between devices, hop(): return lax.ppermute(chunk, 'row', pairs)  28.5 us
    ppermute x12, starting transfers between devices, hop(): return lax.ppermute(chunk, 'row', pairs)  12.9 us
    pallas_call x2, Pallas kernels, product(): pl.pallas_call(functools.partial(product_kernel, sz, dist, keys, first, t...  7.15 us
    ppermute x3, starting transfers between devices, column_sums(): lax.ppermute(pair, 'row', [(q, (q + 2 * t) % sz.n_row) for q in range(sz....  6.67 us
    ppermute x4, starting transfers between devices, last_hop(): return lax.ppermute(chunk, ('row', 'col'), pairs)  3.39 us
    ppermute x4, waiting for transfers between devices, last_hop(): return lax.ppermute(chunk, ('row', 'col'), pairs)  3.25 us
    ppermute x3, starting transfers between devices, apart(): return lax.ppermute(value, 'col', [(q, q ^ far) for q in range(n_col)])  2.63 us
    ppermute x3, waiting for transfers between devices, column_sums(): lax.ppermute(pair, 'row', [(q, (q + 2 * t) % sz.n_row) for q in range(sz....  2.27 us
  transfers between devices with their start and end apart: 23, of which 14 were waited for; matrix products, arithmetic and copies ran while one was open for 0% of the time, Pallas kernels for 15%

profile of v6, /device:TPU:0, one launch (start us, length us, event | category | flops | bytes accessed | tf_op | source)
XLA Modules:
  0.0 77.8 jit_solution(5396524970435254952)
XLA Ops:
  0.0 1.5 %pack_tiles.1 = (bf16[3088,128]{1,0:T(8,128)(2,1)S(1)}, bf16[1552,128]{1,0:T(8,128)(2,1)S(1)}, bf16[1536,128]{1,0:T(8,128)(2,1)S(1)}) custom-call(s32[2,4]{1,0:T(2,128)} %mask_ref.1, bf16[512,1024]{1,0:T(8,128)(2,1)} %matrix_ref.1), custom_call_target="tpu_custom_call" | custom-call | tf_op jit(solution)/shard_map/pack_tiles/pallas_call | solution.py:92
  1.5 0.5 collective-permute-start.4
  2.0 2.6 %collective-permute-start.2 = (bf16[1552,128]{1,0:T(8,128)(2,1)S(1)}, bf16[1552,128]{1,0:T(8,128)(2,1)S(1)}, u32[]{:S(2)}, u32[]{:S(2)}) collective-permute-start(bf16[1552,128]{1,0:T(8,128)(2,1)S(1)} %get-tuple-element.59.refs_4_), channel_id=1, source_target_pairs={{0,4},{4,12},{12,20},{20,28},{28,24},{24,16},{16,8},{8,0},{1,5},{5... | collective-permute-start | bytes 1191944 | tf_op jit(solution)/shard_map/ppermute | solution.py:442
  4.6 0.1 collective-permute-start.3
  4.7 2.0 %collective-permute-start.5 = (bf16[3088,128]{1,0:T(8,128)(2,1)S(1)}, bf16[3088,128]{1,0:T(8,128)(2,1)S(1)}, u32[]{:S(2)}, u32[]{:S(2)}) collective-permute-start(bf16[3088,128]{1,0:T(8,128)(2,1)S(1)} %get-tuple-element.49.refs_0_), channel_id=1, source_target_pairs={{0,2},{1,3},{2,0},{3,1},{4,6},{5,7},{6,4},{7,5},{8,10},{9,11},{10,... | collective-permute-start | bytes 2371592 | tf_op jit(solution)/shard_map/ppermute | solution.py:455
  6.8 1.6 %collective-permute-start.1 = (bf16[1552,128]{1,0:T(8,128)(2,1)S(1)}, bf16[1552,128]{1,0:T(8,128)(2,1)S(1)}, u32[]{:S(2)}, u32[]{:S(2)}) collective-permute-start(bf16[1552,128]{1,0:T(8,128)(2,1)S(1)} %get-tuple-element.59.refs_4_), channel_id=1, source_target_pairs={{0,8},{4,0},{12,4},{20,12},{28,20},{24,28},{16,24},{8,16},{1,9},{5... | collective-permute-start | bytes 1191944 | tf_op jit(solution)/shard_map/ppermute | solution.py:442
  8.4 0.4 collective-permute-start
  8.8 7.7 %collective-permute-done.3.refs_9_ = bf16[1536,128]{1,0:T(8,128)(2,1)S(1)} collective-permute-done((bf16[1536,128]{1,0:T(8,128)(2,1)S(1)}, bf16[1536,128]{1,0:T(8,128)(2,1)S(1)}, u32[]{:S(2)}, u32[]{:S(2)}) %collective-permute-start.3) | collective-permute-done | bytes 393248 | tf_op jit(solution)/shard_map/ppermute | solution.py:442
  16.5 0.0 collective-permute-done.2.refs_6_
  16.5 1.6 %collective-permute-start.9 = (bf16[1552,128]{1,0:T(8,128)(2,1)S(1)}, bf16[1552,128]{1,0:T(8,128)(2,1)S(1)}, u32[]{:S(2)}, u32[]{:S(2)}) collective-permute-start(bf16[1552,128]{1,0:T(8,128)(2,1)S(1)} %collective-permute-done.2.refs_6_), channel_id=1, source_target_pairs={{0,4},{4,12},{12,20},{20,28},{28,24},{24,16},{16,8},{8,0},{1,5},{5... | collective-permute-start | bytes 1191944 | tf_op jit(solution)/shard_map/ppermute | solution.py:442
  18.1 0.4 collective-permute-start.10
  18.6 0.4 expand_tiles.3.refs_0_
  19.0 4.2 %collective-permute-done.refs_7_ = bf16[1536,128]{1,0:T(8,128)(2,1)S(1)} collective-permute-done((bf16[1536,128]{1,0:T(8,128)(2,1)S(1)}, bf16[1536,128]{1,0:T(8,128)(2,1)S(1)}, u32[]{:S(2)}, u32[]{:S(2)}) %collective-permute-start) | collective-permute-done | bytes 393248 | tf_op jit(solution)/shard_map/ppermute | solution.py:442
  23.1 1.9 %collective-permute-done.1.refs_8_ = bf16[1552,128]{1,0:T(8,128)(2,1)S(1)} collective-permute-done((bf16[1552,128]{1,0:T(8,128)(2,1)S(1)}, bf16[1552,128]{1,0:T(8,128)(2,1)S(1)}, u32[]{:S(2)}, u32[]{:S(2)}) %collective-permute-start.1) | collective-permute-done | bytes 397344 | tf_op jit(solution)/shard_map/ppermute | solution.py:442
  25.1 0.1 collective-permute-start.8
  25.2 1.9 %collective-permute-start.7 = (bf16[1536,128]{1,0:T(8,128)(2,1)S(1)}, bf16[1536,128]{1,0:T(8,128)(2,1)S(1)}, u32[]{:S(2)}, u32[]{:S(2)}) collective-permute-start(bf16[1536,128]{1,0:T(8,128)(2,1)S(1)} %collective-permute-done.refs_7_), channel_id=1, source_target_pairs={{0,4},{4,12},{12,20},{20,28},{28,24},{24,16},{16,8},{8,0},{1,5},{5... | collective-permute-start | bytes 1179656 | tf_op jit(solution)/shard_map/ppermute | solution.py:442
  27.1 0.6 keep_rows.1.keep_ref
  27.7 0.1 collective-permute-start.6
  27.7 0.4 expand_tiles.4.refs_1_
  28.1 5.3 %collective-permute-done.10.refs_7_ = bf16[1536,128]{1,0:T(8,128)(2,1)S(1)} collective-permute-done((bf16[1536,128]{1,0:T(8,128)(2,1)S(1)}, bf16[1536,128]{1,0:T(8,128)(2,1)S(1)}, u32[]{:S(2)}, u32[]{:S(2)}) %collective-permute-start.10) | collective-permute-done | bytes 393248 | tf_op jit(solution)/shard_map/ppermute | solution.py:442
  33.5 1.6 %collective-permute-start.11 = (bf16[1552,128]{1,0:T(8,128)(2,1)S(1)}, bf16[1552,128]{1,0:T(8,128)(2,1)S(1)}, u32[]{:S(2)}, u32[]{:S(2)}) collective-permute-start(bf16[1552,128]{1,0:T(8,128)(2,1)S(1)} %collective-permute-done.9.refs_4_), channel_id=1, source_target_pairs={{0,4},{4,12},{12,20},{20,28},{28,24},{24,16},{16,8},{8,0},{1,5},{5... | collective-permute-start | bytes 1191944 | tf_op jit(solution)/shard_map/ppermute | solution.py:442
  35.1 0.4 collective-permute-start.12
  35.5 4.5 %collective-permute-done.7.refs_5_ = bf16[1536,128]{1,0:T(8,128)(2,1)S(1)} collective-permute-done((bf16[1536,128]{1,0:T(8,128)(2,1)S(1)}, bf16[1536,128]{1,0:T(8,128)(2,1)S(1)}, u32[]{:S(2)}, u32[]{:S(2)}) %collective-permute-start.7) | collective-permute-done | bytes 393248 | tf_op jit(solution)/shard_map/ppermute | solution.py:442
  40.1 1.9 %collective-permute-done.8.refs_6_ = bf16[1552,128]{1,0:T(8,128)(2,1)S(1)} collective-permute-done((bf16[1552,128]{1,0:T(8,128)(2,1)S(1)}, bf16[1552,128]{1,0:T(8,128)(2,1)S(1)}, u32[]{:S(2)}, u32[]{:S(2)}) %collective-permute-start.8) | collective-permute-done | bytes 397344 | tf_op jit(solution)/shard_map/ppermute | solution.py:442
  42.0 1.6 %collective-permute-start.15 = (bf16[1536,128]{1,0:T(8,128)(2,1)S(1)}, bf16[1536,128]{1,0:T(8,128)(2,1)S(1)}, u32[]{:S(2)}, u32[]{:S(2)}) collective-permute-start(bf16[1536,128]{1,0:T(8,128)(2,1)S(1)} %collective-permute-done.7.refs_5_), channel_id=1, source_target_pairs={{0,4},{4,12},{12,20},{20,28},{28,24},{24,16},{16,8},{8,0},{1,5},{5... | collective-permute-start | bytes 1179656 | tf_op jit(solution)/shard_map/ppermute | solution.py:442
  43.6 0.4 collective-permute-start.16
  44.0 0.8 expand_tiles.5
  44.8 4.3 %product.2 = (f32[512,1024]{1,0:T(8,128)S(1)}, bf16[512,512]{1,0:T(8,128)(2,1)S(1)}, bf16[512,512]{1,0:T(8,128)(2,1)S(1)}, bf16[512,512]{1,0:T(8,128)(2,1)S(1)}) custom-call(bf16[512,1024]{1,0:T(8,128)(2,1)S(1)} %expand_tiles.3.refs_0_, bf16[512,1024]{1,0:T(8,128)(2,1)S(1)} %expand_tiles.4.refs_1_, bf16[512,1024]{1,0:T(8,128)(2,1)S(1)} %get-tuple-element.57.refs_2_, ...), custom_call_target="tpu_custom_call" | custom-call | flops 536870912 | tf_op jit(solution)/shard_map/product/pallas_call | solution.py:254
  49.1 1.3 %collective-permute-done.12.refs_5_ = bf16[1536,128]{1,0:T(8,128)(2,1)S(1)} collective-permute-done((bf16[1536,128]{1,0:T(8,128)(2,1)S(1)}, bf16[1536,128]{1,0:T(8,128)(2,1)S(1)}, u32[]{:S(2)}, u32[]{:S(2)}) %collective-permute-start.12) | collective-permute-done | bytes 393248 | tf_op jit(solution)/shard_map/ppermute | solution.py:442
  50.4 1.6 %collective-permute-start.13 = (bf16[1552,128]{1,0:T(8,128)(2,1)S(1)}, bf16[1552,128]{1,0:T(8,128)(2,1)S(1)}, u32[]{:S(2)}, u32[]{:S(2)}) collective-permute-start(bf16[1552,128]{1,0:T(8,128)(2,1)S(1)} %collective-permute-done.11.refs_2_), channel_id=1, source_target_pairs={{0,4},{1,3},{2,6},{3,1},{4,12},{5,7},{6,14},{7,5},{12,20},{13,15},... | collective-permute-start | bytes 1191944 | tf_op jit(solution)/shard_map/ppermute | solution.py:452
  52.0 0.4 collective-permute-start.14
  52.5 2.8 %product.3.refs_6_ = f32[512,1024]{1,0:T(8,128)S(1)} custom-call(bf16[512,1024]{1,0:T(8,128)(2,1)S(1)} %expand_tiles.3.refs_0_, bf16[512,1024]{1,0:T(8,128)(2,1)S(1)} %expand_tiles.4.refs_1_, bf16[512,1024]{1,0:T(8,128)(2,1)S(1)} %get-tuple-element.57.refs_2_, bf16[512,1024]{1,0:T(8,128)(2,1)S(1)} %get-tuple-element.58.refs_3_, ...), custom_call_target="tpu_custom_call" | custom-call | flops 536870912 | tf_op jit(solution)/shard_map/product/pallas_call | solution.py:254
  55.3 0.7 collective-permute-start.17
  56.0 0.8 collective-permute-done.15.refs_3_
  56.8 0.7 collective-permute-start.18
  57.4 0.7 collective-permute-done.16.refs_4_
  58.2 1.4 %product_near.1.refs_2_ = f32[512,1024]{1,0:T(8,128)S(1)} custom-call(bf16[512,512]{1,0:T(8,128)(2,1)S(1)} %get-tuple-element.64.refs_0_, bf16[512,512]{1,0:T(8,128)(2,1)S(1)} %get-tuple-element.65.refs_1_, bf16[1552,128]{1,0:T(8,128)(2,1)S(1)} %collective-permute-done.11.refs_2_, bf16[1536,128]{1,0:T(8,128)(2,1)S(1)} %collective-permute-done.15.refs_3_, ...), custom_call_target="tpu_custom_call" | custom-call | flops 536870912 | tf_op jit(solution)/shard_map/product_near/pallas_call | solution.py:297
  59.6 2.8 %collective-permute-done.14.refs_1_ = bf16[1536,128]{1,0:T(8,128)(2,1)S(1)} collective-permute-done((bf16[1536,128]{1,0:T(8,128)(2,1)S(1)}, bf16[1536,128]{1,0:T(8,128)(2,1)S(1)}, u32[]{:S(2)}, u32[]{:S(2)}) %collective-permute-start.14) | collective-permute-done | bytes 393248 | tf_op jit(solution)/shard_map/ppermute | solution.py:452
  62.4 0.5 collective-permute-done.13.refs_0_
  62.8 0.9 %product_last.2 = (f32[512,1024]{1,0:T(8,128)S(1)}, f32[1,1024]{1,0:T(1,128)S(1)}) custom-call(f32[16,1024]{1,0:T(8,128)S(1)} %keep_rows.1.keep_ref, bf16[512,512]{1,0:T(8,128)(2,1)S(1)} %get-tuple-element.60.left_ref, bf16[1552,128]{1,0:T(8,128)(2,1)S(1)} %collective-permute-done.13.refs_0_, bf16[1536,128]{1,0:T(8,128)(2,1)S(1)} %collective-permute-done.14.refs_1_, ...), custom_call_target="tpu_custom_call" | custom-call | flops 536870912 | tf_op jit(solution)/shard_map/product_last/pallas_call | solution.py:366
  63.8 1.8 %collective-permute-start.19 = (f32[1,1024]{1,0:T(1,128)S(1)}, f32[1,1024]{1,0:T(1,128)S(1)}, u32[]{:S(2)}, u32[]{:S(2)}) collective-permute-start(f32[1,1024]{1,0:T(1,128)S(1)} %get-tuple-element.72), channel_id=1, source_target_pairs={{0,4},{4,0},{8,12},{12,8},{16,20},{20,16},{24,28},{28,24},{1,5},{5... | collective-permute-start | bytes 12296 | tf_op jit(solution)/shard_map/ppermute | solution.py:421
  65.6 1.8 %collective-permute-done.19 = f32[1,1024]{1,0:T(1,128)S(1)} collective-permute-done((f32[1,1024]{1,0:T(1,128)S(1)}, f32[1,1024]{1,0:T(1,128)S(1)}, u32[]{:S(2)}, u32[]{:S(2)}) %collective-permute-start.19) | collective-permute-done | bytes 4128 | tf_op jit(solution)/shard_map/ppermute | solution.py:421
  67.5 2.7 %collective-permute-start.20 = (f32[1,1024]{1,0:T(1,128)S(1)}, f32[1,1024]{1,0:T(1,128)S(1)}, u32[]{:S(2)}, u32[]{:S(2)}) collective-permute-start(f32[1,1024]{1,0:T(1,128)S(1)} %add.12), channel_id=1, source_target_pairs={{0,8},{4,12},{8,16},{12,20},{16,24},{20,28},{24,0},{28,4},{1,9},{5... | collective-permute-start | bytes 12296 | tf_op jit(solution)/shard_map/ppermute | solution.py:423
  70.2 2.6 %collective-permute-start.21 = (f32[1,1024]{1,0:T(1,128)S(1)}, f32[1,1024]{1,0:T(1,128)S(1)}, u32[]{:S(2)}, u32[]{:S(2)}) collective-permute-start(f32[1,1024]{1,0:T(1,128)S(1)} %add.12), channel_id=1, source_target_pairs={{0,16},{4,20},{8,24},{12,28},{16,0},{20,4},{24,8},{28,12},{1,17},{... | collective-permute-start | bytes 12296 | tf_op jit(solution)/shard_map/ppermute | solution.py:423
  72.8 1.3 %collective-permute-start.22 = (f32[1,1024]{1,0:T(1,128)S(1)}, f32[1,1024]{1,0:T(1,128)S(1)}, u32[]{:S(2)}, u32[]{:S(2)}) collective-permute-start(f32[1,1024]{1,0:T(1,128)S(1)} %add.12), channel_id=1, source_target_pairs={{0,24},{4,28},{8,0},{12,4},{16,8},{20,12},{24,16},{28,20},{1,25},{... | collective-permute-start | bytes 12296 | tf_op jit(solution)/shard_map/ppermute | solution.py:423
  74.2 0.6 collective-permute-done.21
  74.7 1.7 %collective-permute-done.22 = f32[1,1024]{1,0:T(1,128)S(1)} collective-permute-done((f32[1,1024]{1,0:T(1,128)S(1)}, f32[1,1024]{1,0:T(1,128)S(1)}, u32[]{:S(2)}, u32[]{:S(2)}) %collective-permute-start.22) | collective-permute-done | bytes 4128 | tf_op jit(solution)/shard_map/ppermute | solution.py:423
  76.4 1.4 %scale.1 = f32[512,1024]{1,0:T(8,128)} custom-call(f32[512,1024]{1,0:T(8,128)S(1)} %get-tuple-element.67.first_ref, f32[512,1024]{1,0:T(8,128)S(1)} %get-tuple-element.71.second_ref, f32[1,1024]{1,0:T(1,128)S(1)} %add_add_fusion.totals_ref), custom_call_target="tpu_custom_call" | custom-call | flops 536870912 | tf_op jit(solution)/shard_map/scale/pallas_call | solution.py:403
  (13 shorter events, 0.1 us)
Async XLA Ops:
  1.5 3.2 %collective-permute-start.4 = (bf16[3088,128]{1,0:T(8,128)(2,1)S(1)}, bf16[3088,128]{1,0:T(8,128)(2,1)S(1)}, u32[]{:S(2)}, u32[]{:S(2)}) collective-permute-start(bf16[3088,128]{1,0:T(8,128)(2,1)S(1)} %get-tuple-element.49.refs_0_), channel_id=1, source_target_pairs={{0,1},{1,0},{2,3},{3,2},{4,5},{5,4},{6,7},{7,6},{8,9},{9,8},{10,11... | collective-permute-start | bytes 2371592 | tf_op jit(solution)/shard_map/ppermute | solution.py:455
  2.0 14.5 %collective-permute-start.2 = (bf16[1552,128]{1,0:T(8,128)(2,1)S(1)}, bf16[1552,128]{1,0:T(8,128)(2,1)S(1)}, u32[]{:S(2)}, u32[]{:S(2)}) collective-permute-start(bf16[1552,128]{1,0:T(8,128)(2,1)S(1)} %get-tuple-element.59.refs_4_), channel_id=1, source_target_pairs={{0,4},{4,12},{12,20},{20,28},{28,24},{24,16},{16,8},{8,0},{1,5},{5... | collective-permute-start | bytes 1191944 | tf_op jit(solution)/shard_map/ppermute | solution.py:442
  4.6 22.5 %copy-start = (s32[2,4]{1,0:T(2,128)S(1)}, s32[2,4]{1,0:T(2,128)}, u32[]{:S(2)}) copy-start(s32[2,4]{1,0:T(2,128)} %out_mask_ref) | copy-start | bytes 100
  4.6 12.0 %collective-permute-start.3 = (bf16[1536,128]{1,0:T(8,128)(2,1)S(1)}, bf16[1536,128]{1,0:T(8,128)(2,1)S(1)}, u32[]{:S(2)}, u32[]{:S(2)}) collective-permute-start(bf16[1536,128]{1,0:T(8,128)(2,1)S(1)} %get-tuple-element.39.refs_5_), channel_id=1, source_target_pairs={{0,8},{4,0},{12,4},{20,12},{28,20},{24,28},{16,24},{8,16},{1,9},{5... | collective-permute-start | bytes 1179656 | tf_op jit(solution)/shard_map/ppermute | solution.py:442
  4.7 22.9 %collective-permute-start.5 = (bf16[3088,128]{1,0:T(8,128)(2,1)S(1)}, bf16[3088,128]{1,0:T(8,128)(2,1)S(1)}, u32[]{:S(2)}, u32[]{:S(2)}) collective-permute-start(bf16[3088,128]{1,0:T(8,128)(2,1)S(1)} %get-tuple-element.49.refs_0_), channel_id=1, source_target_pairs={{0,2},{1,3},{2,0},{3,1},{4,6},{5,7},{6,4},{7,5},{8,10},{9,11},{10,... | collective-permute-start | bytes 2371592 | tf_op jit(solution)/shard_map/ppermute | solution.py:455
  6.8 18.3 %collective-permute-start.1 = (bf16[1552,128]{1,0:T(8,128)(2,1)S(1)}, bf16[1552,128]{1,0:T(8,128)(2,1)S(1)}, u32[]{:S(2)}, u32[]{:S(2)}) collective-permute-start(bf16[1552,128]{1,0:T(8,128)(2,1)S(1)} %get-tuple-element.59.refs_4_), channel_id=1, source_target_pairs={{0,8},{4,0},{12,4},{20,12},{28,20},{24,28},{16,24},{8,16},{1,9},{5... | collective-permute-start | bytes 1191944 | tf_op jit(solution)/shard_map/ppermute | solution.py:442
  8.4 14.8 %collective-permute-start = (bf16[1536,128]{1,0:T(8,128)(2,1)S(1)}, bf16[1536,128]{1,0:T(8,128)(2,1)S(1)}, u32[]{:S(2)}, u32[]{:S(2)}) collective-permute-start(bf16[1536,128]{1,0:T(8,128)(2,1)S(1)} %get-tuple-element.39.refs_5_), channel_id=1, source_target_pairs={{0,4},{4,12},{12,20},{20,28},{28,24},{24,16},{16,8},{8,0},{1,5},{5... | collective-permute-start | bytes 1179656 | tf_op jit(solution)/shard_map/ppermute | solution.py:442
  16.5 16.9 %collective-permute-start.9 = (bf16[1552,128]{1,0:T(8,128)(2,1)S(1)}, bf16[1552,128]{1,0:T(8,128)(2,1)S(1)}, u32[]{:S(2)}, u32[]{:S(2)}) collective-permute-start(bf16[1552,128]{1,0:T(8,128)(2,1)S(1)} %collective-permute-done.2.refs_6_), channel_id=1, source_target_pairs={{0,4},{4,12},{12,20},{20,28},{28,24},{24,16},{16,8},{8,0},{1,5},{5... | collective-permute-start | bytes 1191944 | tf_op jit(solution)/shard_map/ppermute | solution.py:442
  18.1 15.4 %collective-permute-start.10 = (bf16[1536,128]{1,0:T(8,128)(2,1)S(1)}, bf16[1536,128]{1,0:T(8,128)(2,1)S(1)}, u32[]{:S(2)}, u32[]{:S(2)}) collective-permute-start(bf16[1536,128]{1,0:T(8,128)(2,1)S(1)} %collective-permute-done.3.refs_9_), channel_id=1, source_target_pairs={{0,8},{4,0},{12,4},{20,12},{28,20},{24,28},{16,24},{8,16},{1,9},{5... | collective-permute-start | bytes 1179656 | tf_op jit(solution)/shard_map/ppermute | solution.py:442
  25.1 16.9 %collective-permute-start.8 = (bf16[1552,128]{1,0:T(8,128)(2,1)S(1)}, bf16[1552,128]{1,0:T(8,128)(2,1)S(1)}, u32[]{:S(2)}, u32[]{:S(2)}) collective-permute-start(bf16[1552,128]{1,0:T(8,128)(2,1)S(1)} %collective-permute-done.1.refs_8_), channel_id=1, source_target_pairs={{0,8},{4,0},{12,4},{20,12},{28,20},{24,28},{16,24},{8,16},{1,9},{5... | collective-permute-start | bytes 1191944 | tf_op jit(solution)/shard_map/ppermute | solution.py:442
  25.2 14.9 %collective-permute-start.7 = (bf16[1536,128]{1,0:T(8,128)(2,1)S(1)}, bf16[1536,128]{1,0:T(8,128)(2,1)S(1)}, u32[]{:S(2)}, u32[]{:S(2)}) collective-permute-start(bf16[1536,128]{1,0:T(8,128)(2,1)S(1)} %collective-permute-done.refs_7_), channel_id=1, source_target_pairs={{0,4},{4,12},{12,20},{20,28},{28,24},{24,16},{16,8},{8,0},{1,5},{5... | collective-permute-start | bytes 1179656 | tf_op jit(solution)/shard_map/ppermute | solution.py:442
  27.7 16.4 %collective-permute-start.6 = (bf16[3088,128]{1,0:T(8,128)(2,1)S(1)}, bf16[3088,128]{1,0:T(8,128)(2,1)S(1)}, u32[]{:S(2)}, u32[]{:S(2)}) collective-permute-start(bf16[3088,128]{1,0:T(8,128)(2,1)S(1)} %collective-permute-done.5.refs_0_), channel_id=1, source_target_pairs={{0,1},{1,0},{2,3},{3,2},{4,5},{5,4},{6,7},{7,6},{8,9},{9,8},{10,11... | collective-permute-start | bytes 2371592 | tf_op jit(solution)/shard_map/ppermute | solution.py:455
  33.5 16.9 %collective-permute-start.11 = (bf16[1552,128]{1,0:T(8,128)(2,1)S(1)}, bf16[1552,128]{1,0:T(8,128)(2,1)S(1)}, u32[]{:S(2)}, u32[]{:S(2)}) collective-permute-start(bf16[1552,128]{1,0:T(8,128)(2,1)S(1)} %collective-permute-done.9.refs_4_), channel_id=1, source_target_pairs={{0,4},{4,12},{12,20},{20,28},{28,24},{24,16},{16,8},{8,0},{1,5},{5... | collective-permute-start | bytes 1191944 | tf_op jit(solution)/shard_map/ppermute | solution.py:442
  35.1 15.4 %collective-permute-start.12 = (bf16[1536,128]{1,0:T(8,128)(2,1)S(1)}, bf16[1536,128]{1,0:T(8,128)(2,1)S(1)}, u32[]{:S(2)}, u32[]{:S(2)}) collective-permute-start(bf16[1536,128]{1,0:T(8,128)(2,1)S(1)} %collective-permute-done.10.refs_7_), channel_id=1, source_target_pairs={{0,8},{4,0},{12,4},{20,12},{28,20},{24,28},{16,24},{8,16},{1,9},{5... | collective-permute-start | bytes 1179656 | tf_op jit(solution)/shard_map/ppermute | solution.py:442
  42.0 14.8 %collective-permute-start.15 = (bf16[1536,128]{1,0:T(8,128)(2,1)S(1)}, bf16[1536,128]{1,0:T(8,128)(2,1)S(1)}, u32[]{:S(2)}, u32[]{:S(2)}) collective-permute-start(bf16[1536,128]{1,0:T(8,128)(2,1)S(1)} %collective-permute-done.7.refs_5_), channel_id=1, source_target_pairs={{0,4},{4,12},{12,20},{20,28},{28,24},{24,16},{16,8},{8,0},{1,5},{5... | collective-permute-start | bytes 1179656 | tf_op jit(solution)/shard_map/ppermute | solution.py:442
  43.6 14.6 %collective-permute-start.16 = (bf16[1552,128]{1,0:T(8,128)(2,1)S(1)}, bf16[1552,128]{1,0:T(8,128)(2,1)S(1)}, u32[]{:S(2)}, u32[]{:S(2)}) collective-permute-start(bf16[1552,128]{1,0:T(8,128)(2,1)S(1)} %collective-permute-done.8.refs_6_), channel_id=1, source_target_pairs={{0,8},{4,0},{12,4},{20,12},{28,20},{24,28},{16,24},{8,16},{1,9},{5... | collective-permute-start | bytes 1191944 | tf_op jit(solution)/shard_map/ppermute | solution.py:442
  50.4 12.4 %collective-permute-start.13 = (bf16[1552,128]{1,0:T(8,128)(2,1)S(1)}, bf16[1552,128]{1,0:T(8,128)(2,1)S(1)}, u32[]{:S(2)}, u32[]{:S(2)}) collective-permute-start(bf16[1552,128]{1,0:T(8,128)(2,1)S(1)} %collective-permute-done.11.refs_2_), channel_id=1, source_target_pairs={{0,4},{1,3},{2,6},{3,1},{4,12},{5,7},{6,14},{7,5},{12,20},{13,15},... | collective-permute-start | bytes 1191944 | tf_op jit(solution)/shard_map/ppermute | solution.py:452
  52.0 10.4 %collective-permute-start.14 = (bf16[1536,128]{1,0:T(8,128)(2,1)S(1)}, bf16[1536,128]{1,0:T(8,128)(2,1)S(1)}, u32[]{:S(2)}, u32[]{:S(2)}) collective-permute-start(bf16[1536,128]{1,0:T(8,128)(2,1)S(1)} %collective-permute-done.12.refs_5_), channel_id=1, source_target_pairs={{0,8},{1,3},{2,10},{3,1},{4,0},{5,7},{6,2},{7,5},{12,4},{13,15},{1... | collective-permute-start | bytes 1179656 | tf_op jit(solution)/shard_map/ppermute | solution.py:452
  55.3 8.5 %collective-permute-start.17 = (bf16[1552,128]{1,0:T(8,128)(2,1)S(1)}, bf16[1552,128]{1,0:T(8,128)(2,1)S(1)}, u32[]{:S(2)}, u32[]{:S(2)}) collective-permute-start(bf16[1552,128]{1,0:T(8,128)(2,1)S(1)} %collective-permute-done.11.refs_2_), channel_id=1, source_target_pairs={{0,0},{1,5},{2,2},{3,7},{4,4},{5,13},{6,6},{7,15},{12,12},{13,21},... | collective-permute-start | bytes 1191944 | tf_op jit(solution)/shard_map/ppermute | solution.py:452
  56.8 7.0 %collective-permute-start.18 = (bf16[1536,128]{1,0:T(8,128)(2,1)S(1)}, bf16[1536,128]{1,0:T(8,128)(2,1)S(1)}, u32[]{:S(2)}, u32[]{:S(2)}) collective-permute-start(bf16[1536,128]{1,0:T(8,128)(2,1)S(1)} %collective-permute-done.12.refs_5_), channel_id=1, source_target_pairs={{0,0},{1,9},{2,2},{3,11},{4,4},{5,1},{6,6},{7,3},{12,12},{13,5},{1... | collective-permute-start | bytes 1179656 | tf_op jit(solution)/shard_map/ppermute | solution.py:452
  63.8 3.7 %collective-permute-start.19 = (f32[1,1024]{1,0:T(1,128)S(1)}, f32[1,1024]{1,0:T(1,128)S(1)}, u32[]{:S(2)}, u32[]{:S(2)}) collective-permute-start(f32[1,1024]{1,0:T(1,128)S(1)} %get-tuple-element.72), channel_id=1, source_target_pairs={{0,4},{4,0},{8,12},{12,8},{16,20},{20,16},{24,28},{28,24},{1,5},{5... | collective-permute-start | bytes 12296 | tf_op jit(solution)/shard_map/ppermute | solution.py:421
  67.5 6.7 %collective-permute-start.20 = (f32[1,1024]{1,0:T(1,128)S(1)}, f32[1,1024]{1,0:T(1,128)S(1)}, u32[]{:S(2)}, u32[]{:S(2)}) collective-permute-start(f32[1,1024]{1,0:T(1,128)S(1)} %add.12), channel_id=1, source_target_pairs={{0,8},{4,12},{8,16},{12,20},{16,24},{20,28},{24,0},{28,4},{1,9},{5... | collective-permute-start | bytes 12296 | tf_op jit(solution)/shard_map/ppermute | solution.py:423
  70.2 4.5 %collective-permute-start.21 = (f32[1,1024]{1,0:T(1,128)S(1)}, f32[1,1024]{1,0:T(1,128)S(1)}, u32[]{:S(2)}, u32[]{:S(2)}) collective-permute-start(f32[1,1024]{1,0:T(1,128)S(1)} %add.12), channel_id=1, source_target_pairs={{0,16},{4,20},{8,24},{12,28},{16,0},{20,4},{24,8},{28,12},{1,17},{... | collective-permute-start | bytes 12296 | tf_op jit(solution)/shard_map/ppermute | solution.py:423
  72.8 3.6 %collective-permute-start.22 = (f32[1,1024]{1,0:T(1,128)S(1)}, f32[1,1024]{1,0:T(1,128)S(1)}, u32[]{:S(2)}, u32[]{:S(2)}) collective-permute-start(f32[1,1024]{1,0:T(1,128)S(1)} %add.12), channel_id=1, source_target_pairs={{0,24},{4,28},{8,0},{12,4},{16,8},{20,12},{24,16},{28,20},{1,25},{... | collective-permute-start | bytes 12296 | tf_op jit(solution)/shard_map/ppermute | solution.py:423

commit v7 on v6

--- a/solution.py
+++ b/solution.py
@@ -399,7 +399,7 @@
 
 def scale(sz, first, second, totals):
     vmem = pl.BlockSpec(memory_space=pltpu.VMEM)
-    steps = 4
+    steps = 8
     return pl.pallas_call(
         functools.partial(scale_kernel, sz, steps),
         out_shape=jax.ShapeDtypeStruct((sz.rows, sz.cols), jnp.float32),
@@ -506,9 +506,9 @@
             gate.append(keep)
         keys = None
         if i == 3:
-            keys = [(0, None), (1, None), (-1, 0)]
+            keys = [(0, None), (1, 0), (-1, 0)]
         elif i == 4:
-            keys = [(2, None), (-2, None), (-1, 1)]
+            keys = [(2, None), (-2, None), (1, 1), (-1, 1)]
         elif i > 4 and h == 1:
             keys = [(step, None), (-step, None)]
         if keys:

time: 78 us -> 77 us (0.987)
  starting transfers between devices: 27.4 us -> 26.1 us
    ppermute x3, starting transfers between devices: 6.67 us -> 5.62 us  [column_sums(): lax.ppermute(pair, 'row', [(q, (q + 2 * t) % sz.n_row) for q in range(sz....]
  transfers between devices with their start and end apart: 23 -> 23, of which waited for: 14 -> 13; matrix products, arithmetic and copies ran while one was open for 0% -> 0% of each run, Pallas kernels for 15% -> 15%
where the time goes in v7:
time: 77 us; the launch traced here: 76.4 us
  waiting for transfers between devices  35.4 us (46%)
  starting transfers between devices  26.1 us (34%)
  Pallas kernels  14.7 us (19%)
    ppermute x12, waiting for transfers between devices, hop(): return lax.ppermute(chunk, 'row', pairs)  28.2 us
    ppermute x12, starting transfers between devices, hop(): return lax.ppermute(chunk, 'row', pairs)  12.9 us
    pallas_call x2, Pallas kernels, product(): pl.pallas_call(functools.partial(product_kernel, sz, dist, keys, first, t...  7.36 us
    ppermute x3, starting transfers between devices, column_sums(): lax.ppermute(pair, 'row', [(q, (q + 2 * t) % sz.n_row) for q in range(sz....  5.62 us
    ppermute x4, starting transfers between devices, last_hop(): return lax.ppermute(chunk, ('row', 'col'), pairs)  3.39 us
    ppermute x4, waiting for transfers between devices, last_hop(): return lax.ppermute(chunk, ('row', 'col'), pairs)  2.77 us
    ppermute x3, starting transfers between devices, apart(): return lax.ppermute(value, 'col', [(q, q ^ far) for q in range(n_col)])  2.63 us
    ppermute x3, waiting for transfers between devices, column_sums(): lax.ppermute(pair, 'row', [(q, (q + 2 * t) % sz.n_row) for q in range(sz....  2.26 us
  transfers between devices with their start and end apart: 23, of which 13 were waited for; matrix products, arithmetic and copies ran while one was open for 0% of the time, Pallas kernels for 15%

profile of v7, /device:TPU:0, one launch (start us, length us, event | category | flops | bytes accessed | tf_op | source)
XLA Modules:
  0.0 76.4 jit_solution(9824638186647739102)
XLA Ops:
  0.0 1.5 %pack_tiles.1 = (bf16[3088,128]{1,0:T(8,128)(2,1)S(1)}, bf16[1552,128]{1,0:T(8,128)(2,1)S(1)}, bf16[1536,128]{1,0:T(8,128)(2,1)S(1)}) custom-call(s32[2,4]{1,0:T(2,128)} %mask_ref.1, bf16[512,1024]{1,0:T(8,128)(2,1)} %matrix_ref.1), custom_call_target="tpu_custom_call" | custom-call | tf_op jit(solution)/shard_map/pack_tiles/pallas_call | solution.py:92
  1.5 0.5 collective-permute-start.4
  2.0 2.6 %collective-permute-start.2 = (bf16[1552,128]{1,0:T(8,128)(2,1)S(1)}, bf16[1552,128]{1,0:T(8,128)(2,1)S(1)}, u32[]{:S(2)}, u32[]{:S(2)}) collective-permute-start(bf16[1552,128]{1,0:T(8,128)(2,1)S(1)} %get-tuple-element.59.refs_4_), channel_id=1, source_target_pairs={{0,4},{4,12},{12,20},{20,28},{28,24},{24,16},{16,8},{8,0},{1,5},{5... | collective-permute-start | bytes 1191944 | tf_op jit(solution)/shard_map/ppermute | solution.py:442
  4.6 0.1 collective-permute-start.3
  4.7 2.0 %collective-permute-start.5 = (bf16[3088,128]{1,0:T(8,128)(2,1)S(1)}, bf16[3088,128]{1,0:T(8,128)(2,1)S(1)}, u32[]{:S(2)}, u32[]{:S(2)}) collective-permute-start(bf16[3088,128]{1,0:T(8,128)(2,1)S(1)} %get-tuple-element.49.refs_0_), channel_id=1, source_target_pairs={{0,2},{1,3},{2,0},{3,1},{4,6},{5,7},{6,4},{7,5},{8,10},{9,11},{10,... | collective-permute-start | bytes 2371592 | tf_op jit(solution)/shard_map/ppermute | solution.py:455
  6.8 1.6 %collective-permute-start.1 = (bf16[1552,128]{1,0:T(8,128)(2,1)S(1)}, bf16[1552,128]{1,0:T(8,128)(2,1)S(1)}, u32[]{:S(2)}, u32[]{:S(2)}) collective-permute-start(bf16[1552,128]{1,0:T(8,128)(2,1)S(1)} %get-tuple-element.59.refs_4_), channel_id=1, source_target_pairs={{0,8},{4,0},{12,4},{20,12},{28,20},{24,28},{16,24},{8,16},{1,9},{5... | collective-permute-start | bytes 1191944 | tf_op jit(solution)/shard_map/ppermute | solution.py:442
  8.4 0.4 collective-permute-start
  8.8 7.7 %collective-permute-done.3.refs_9_.refs_11_ = bf16[1536,128]{1,0:T(8,128)(2,1)S(1)} collective-permute-done((bf16[1536,128]{1,0:T(8,128)(2,1)S(1)}, bf16[1536,128]{1,0:T(8,128)(2,1)S(1)}, u32[]{:S(2)}, u32[]{:S(2)}) %collective-permute-start.3) | collective-permute-done | bytes 393248 | tf_op jit(solution)/shard_map/ppermute | solution.py:442
  16.5 0.0 collective-permute-done.2.refs_6_.refs_8_
  16.5 1.6 %collective-permute-start.9 = (bf16[1552,128]{1,0:T(8,128)(2,1)S(1)}, bf16[1552,128]{1,0:T(8,128)(2,1)S(1)}, u32[]{:S(2)}, u32[]{:S(2)}) collective-permute-start(bf16[1552,128]{1,0:T(8,128)(2,1)S(1)} %collective-permute-done.2.refs_6_.refs_8_), channel_id=1, source_target_pairs={{0,4},{4,12},{12,20},{20,28},{28,24},{24,16},{16,8},{8,0},{1,5},{5... | collective-permute-start | bytes 1191944 | tf_op jit(solution)/shard_map/ppermute | solution.py:442
  18.1 0.4 collective-permute-start.10
  18.6 0.4 expand_tiles.3.refs_0_
  19.0 4.2 %collective-permute-done.refs_7_.refs_9_ = bf16[1536,128]{1,0:T(8,128)(2,1)S(1)} collective-permute-done((bf16[1536,128]{1,0:T(8,128)(2,1)S(1)}, bf16[1536,128]{1,0:T(8,128)(2,1)S(1)}, u32[]{:S(2)}, u32[]{:S(2)}) %collective-permute-start) | collective-permute-done | bytes 393248 | tf_op jit(solution)/shard_map/ppermute | solution.py:442
  23.1 1.9 %collective-permute-done.1.refs_8_.refs_10_ = bf16[1552,128]{1,0:T(8,128)(2,1)S(1)} collective-permute-done((bf16[1552,128]{1,0:T(8,128)(2,1)S(1)}, bf16[1552,128]{1,0:T(8,128)(2,1)S(1)}, u32[]{:S(2)}, u32[]{:S(2)}) %collective-permute-start.1) | collective-permute-done | bytes 397344 | tf_op jit(solution)/shard_map/ppermute | solution.py:442
  25.1 0.1 collective-permute-start.8
  25.2 1.9 %collective-permute-start.7 = (bf16[1536,128]{1,0:T(8,128)(2,1)S(1)}, bf16[1536,128]{1,0:T(8,128)(2,1)S(1)}, u32[]{:S(2)}, u32[]{:S(2)}) collective-permute-start(bf16[1536,128]{1,0:T(8,128)(2,1)S(1)} %collective-permute-done.refs_7_.refs_9_), channel_id=1, source_target_pairs={{0,4},{4,12},{12,20},{20,28},{28,24},{24,16},{16,8},{8,0},{1,5},{5... | collective-permute-start | bytes 1179656 | tf_op jit(solution)/shard_map/ppermute | solution.py:442
  27.1 0.6 keep_rows.1.keep_ref
  27.7 0.1 collective-permute-start.6
  27.7 0.4 expand_tiles.4.refs_1_
  28.1 5.3 %collective-permute-done.10.refs_7_ = bf16[1536,128]{1,0:T(8,128)(2,1)S(1)} collective-permute-done((bf16[1536,128]{1,0:T(8,128)(2,1)S(1)}, bf16[1536,128]{1,0:T(8,128)(2,1)S(1)}, u32[]{:S(2)}, u32[]{:S(2)}) %collective-permute-start.10) | collective-permute-done | bytes 393248 | tf_op jit(solution)/shard_map/ppermute | solution.py:442
  33.5 0.0 collective-permute-done.9.refs_4_
  33.5 1.6 %collective-permute-start.11 = (bf16[1552,128]{1,0:T(8,128)(2,1)S(1)}, bf16[1552,128]{1,0:T(8,128)(2,1)S(1)}, u32[]{:S(2)}, u32[]{:S(2)}) collective-permute-start(bf16[1552,128]{1,0:T(8,128)(2,1)S(1)} %collective-permute-done.9.refs_4_), channel_id=1, source_target_pairs={{0,4},{4,12},{12,20},{20,28},{28,24},{24,16},{16,8},{8,0},{1,5},{5... | collective-permute-start | bytes 1191944 | tf_op jit(solution)/shard_map/ppermute | solution.py:442
  35.1 0.4 collective-permute-start.12
  35.5 4.5 %collective-permute-done.7.refs_5_ = bf16[1536,128]{1,0:T(8,128)(2,1)S(1)} collective-permute-done((bf16[1536,128]{1,0:T(8,128)(2,1)S(1)}, bf16[1536,128]{1,0:T(8,128)(2,1)S(1)}, u32[]{:S(2)}, u32[]{:S(2)}) %collective-permute-start.7) | collective-permute-done | bytes 393248 | tf_op jit(solution)/shard_map/ppermute | solution.py:442
  40.1 1.9 %collective-permute-done.8.refs_6_ = bf16[1552,128]{1,0:T(8,128)(2,1)S(1)} collective-permute-done((bf16[1552,128]{1,0:T(8,128)(2,1)S(1)}, bf16[1552,128]{1,0:T(8,128)(2,1)S(1)}, u32[]{:S(2)}, u32[]{:S(2)}) %collective-permute-start.8) | collective-permute-done | bytes 397344 | tf_op jit(solution)/shard_map/ppermute | solution.py:442
  42.0 1.6 %collective-permute-start.15 = (bf16[1536,128]{1,0:T(8,128)(2,1)S(1)}, bf16[1536,128]{1,0:T(8,128)(2,1)S(1)}, u32[]{:S(2)}, u32[]{:S(2)}) collective-permute-start(bf16[1536,128]{1,0:T(8,128)(2,1)S(1)} %collective-permute-done.7.refs_5_), channel_id=1, source_target_pairs={{0,4},{4,12},{12,20},{20,28},{28,24},{24,16},{16,8},{8,0},{1,5},{5... | collective-permute-start | bytes 1179656 | tf_op jit(solution)/shard_map/ppermute | solution.py:442
  43.6 0.4 collective-permute-start.16
  44.0 0.8 %expand_tiles.5 = (bf16[512,1024]{1,0:T(8,128)(2,1)S(1)}, bf16[512,1024]{1,0:T(8,128)(2,1)S(1)}) custom-call(bf16[3088,128]{1,0:T(8,128)(2,1)S(1)} %collective-permute-done.5.refs_0_, bf16[3088,128]{1,0:T(8,128)(2,1)S(1)} %collective-permute-done.6.refs_1_), custom_call_target="tpu_custom_call" | custom-call | flops 536870912 | tf_op jit(solution)/shard_map/expand_tiles/pallas_call | solution.py:143
  44.8 4.5 %product.2 = (f32[512,1024]{1,0:T(8,128)S(1)}, bf16[512,512]{1,0:T(8,128)(2,1)S(1)}, bf16[512,512]{1,0:T(8,128)(2,1)S(1)}, bf16[512,512]{1,0:T(8,128)(2,1)S(1)}) custom-call(bf16[512,1024]{1,0:T(8,128)(2,1)S(1)} %expand_tiles.3.refs_0_, bf16[512,1024]{1,0:T(8,128)(2,1)S(1)} %expand_tiles.4.refs_1_, bf16[512,1024]{1,0:T(8,128)(2,1)S(1)} %get-tuple-element.57.refs_2_, ...), custom_call_target="tpu_custom_call" | custom-call | flops 536870912 | tf_op jit(solution)/shard_map/product/pallas_call | solution.py:254
  49.3 1.1 %collective-permute-done.12.refs_5_ = bf16[1536,128]{1,0:T(8,128)(2,1)S(1)} collective-permute-done((bf16[1536,128]{1,0:T(8,128)(2,1)S(1)}, bf16[1536,128]{1,0:T(8,128)(2,1)S(1)}, u32[]{:S(2)}, u32[]{:S(2)}) %collective-permute-start.12) | collective-permute-done | bytes 393248 | tf_op jit(solution)/shard_map/ppermute | solution.py:442
  50.4 1.6 %collective-permute-start.13 = (bf16[1552,128]{1,0:T(8,128)(2,1)S(1)}, bf16[1552,128]{1,0:T(8,128)(2,1)S(1)}, u32[]{:S(2)}, u32[]{:S(2)}) collective-permute-start(bf16[1552,128]{1,0:T(8,128)(2,1)S(1)} %collective-permute-done.11.refs_2_), channel_id=1, source_target_pairs={{0,4},{1,3},{2,6},{3,1},{4,12},{5,7},{6,14},{7,5},{12,20},{13,15},... | collective-permute-start | bytes 1191944 | tf_op jit(solution)/shard_map/ppermute | solution.py:452
  52.0 0.4 collective-permute-start.14
  52.5 2.8 %product.3.refs_6_ = f32[512,1024]{1,0:T(8,128)S(1)} custom-call(bf16[512,1024]{1,0:T(8,128)(2,1)S(1)} %expand_tiles.3.refs_0_, bf16[512,1024]{1,0:T(8,128)(2,1)S(1)} %expand_tiles.4.refs_1_, bf16[512,1024]{1,0:T(8,128)(2,1)S(1)} %get-tuple-element.57.refs_2_, bf16[512,1024]{1,0:T(8,128)(2,1)S(1)} %get-tuple-element.58.refs_3_, ...), custom_call_target="tpu_custom_call" | custom-call | flops 536870912 | tf_op jit(solution)/shard_map/product/pallas_call | solution.py:254
  55.3 0.7 collective-permute-start.17
  56.0 0.8 collective-permute-done.15.refs_3_
  56.8 0.7 collective-permute-start.18
  57.4 0.7 collective-permute-done.16.refs_4_
  58.2 1.4 %product_near.1.refs_2_ = f32[512,1024]{1,0:T(8,128)S(1)} custom-call(bf16[512,512]{1,0:T(8,128)(2,1)S(1)} %get-tuple-element.64.refs_0_, bf16[512,512]{1,0:T(8,128)(2,1)S(1)} %get-tuple-element.65.refs_1_, bf16[1552,128]{1,0:T(8,128)(2,1)S(1)} %collective-permute-done.11.refs_2_, bf16[1536,128]{1,0:T(8,128)(2,1)S(1)} %collective-permute-done.15.refs_3_, ...), custom_call_target="tpu_custom_call" | custom-call | flops 536870912 | tf_op jit(solution)/shard_map/product_near/pallas_call | solution.py:297
  59.6 2.8 %collective-permute-done.14.refs_1_ = bf16[1536,128]{1,0:T(8,128)(2,1)S(1)} collective-permute-done((bf16[1536,128]{1,0:T(8,128)(2,1)S(1)}, bf16[1536,128]{1,0:T(8,128)(2,1)S(1)}, u32[]{:S(2)}, u32[]{:S(2)}) %collective-permute-start.14) | collective-permute-done | bytes 393248 | tf_op jit(solution)/shard_map/ppermute | solution.py:452
  62.4 0.9 %product_last.2 = (f32[512,1024]{1,0:T(8,128)S(1)}, f32[1,1024]{1,0:T(1,128)S(1)}) custom-call(f32[16,1024]{1,0:T(8,128)S(1)} %keep_rows.1.keep_ref, bf16[512,512]{1,0:T(8,128)(2,1)S(1)} %get-tuple-element.60.left_ref, bf16[1552,128]{1,0:T(8,128)(2,1)S(1)} %collective-permute-done.13.refs_0_, bf16[1536,128]{1,0:T(8,128)(2,1)S(1)} %collective-permute-done.14.refs_1_, ...), custom_call_target="tpu_custom_call" | custom-call | flops 536870912 | tf_op jit(solution)/shard_map/product_last/pallas_call | solution.py:366
  63.3 1.6 %collective-permute-start.19 = (f32[1,1024]{1,0:T(1,128)S(1)}, f32[1,1024]{1,0:T(1,128)S(1)}, u32[]{:S(2)}, u32[]{:S(2)}) collective-permute-start(f32[1,1024]{1,0:T(1,128)S(1)} %get-tuple-element.72), channel_id=1, source_target_pairs={{0,4},{4,0},{8,12},{12,8},{16,20},{20,16},{24,28},{28,24},{1,5},{5... | collective-permute-start | bytes 12296 | tf_op jit(solution)/shard_map/ppermute | solution.py:421
  65.0 2.1 %collective-permute-done.19 = f32[1,1024]{1,0:T(1,128)S(1)} collective-permute-done((f32[1,1024]{1,0:T(1,128)S(1)}, f32[1,1024]{1,0:T(1,128)S(1)}, u32[]{:S(2)}, u32[]{:S(2)}) %collective-permute-start.19) | collective-permute-done | bytes 4128 | tf_op jit(solution)/shard_map/ppermute | solution.py:421
  67.1 1.7 %collective-permute-start.20 = (f32[1,1024]{1,0:T(1,128)S(1)}, f32[1,1024]{1,0:T(1,128)S(1)}, u32[]{:S(2)}, u32[]{:S(2)}) collective-permute-start(f32[1,1024]{1,0:T(1,128)S(1)} %add.12), channel_id=1, source_target_pairs={{0,8},{4,12},{8,16},{12,20},{16,24},{20,28},{24,0},{28,4},{1,9},{5... | collective-permute-start | bytes 12296 | tf_op jit(solution)/shard_map/ppermute | solution.py:423
  68.8 2.6 %collective-permute-start.21 = (f32[1,1024]{1,0:T(1,128)S(1)}, f32[1,1024]{1,0:T(1,128)S(1)}, u32[]{:S(2)}, u32[]{:S(2)}) collective-permute-start(f32[1,1024]{1,0:T(1,128)S(1)} %add.12), channel_id=1, source_target_pairs={{0,16},{4,20},{8,24},{12,28},{16,0},{20,4},{24,8},{28,12},{1,17},{... | collective-permute-start | bytes 12296 | tf_op jit(solution)/shard_map/ppermute | solution.py:423
  71.4 1.3 %collective-permute-start.22 = (f32[1,1024]{1,0:T(1,128)S(1)}, f32[1,1024]{1,0:T(1,128)S(1)}, u32[]{:S(2)}, u32[]{:S(2)}) collective-permute-start(f32[1,1024]{1,0:T(1,128)S(1)} %add.12), channel_id=1, source_target_pairs={{0,24},{4,28},{8,0},{12,4},{16,8},{20,12},{24,16},{28,20},{1,25},{... | collective-permute-start | bytes 12296 | tf_op jit(solution)/shard_map/ppermute | solution.py:423
  72.8 0.6 collective-permute-done.21
  73.3 1.7 %collective-permute-done.22 = f32[1,1024]{1,0:T(1,128)S(1)} collective-permute-done((f32[1,1024]{1,0:T(1,128)S(1)}, f32[1,1024]{1,0:T(1,128)S(1)}, u32[]{:S(2)}, u32[]{:S(2)}) %collective-permute-start.22) | collective-permute-done | bytes 4128 | tf_op jit(solution)/shard_map/ppermute | solution.py:423
  75.0 1.4 %scale.1 = f32[512,1024]{1,0:T(8,128)} custom-call(f32[512,1024]{1,0:T(8,128)S(1)} %get-tuple-element.67.first_ref, f32[512,1024]{1,0:T(8,128)S(1)} %get-tuple-element.71.second_ref, f32[1,1024]{1,0:T(1,128)S(1)} %add_add_fusion.totals_ref), custom_call_target="tpu_custom_call" | custom-call | flops 536870912 | tf_op jit(solution)/shard_map/scale/pallas_call | solution.py:403
  (13 shorter events, 0.1 us)
Async XLA Ops:
  1.5 3.2 %collective-permute-start.4 = (bf16[3088,128]{1,0:T(8,128)(2,1)S(1)}, bf16[3088,128]{1,0:T(8,128)(2,1)S(1)}, u32[]{:S(2)}, u32[]{:S(2)}) collective-permute-start(bf16[3088,128]{1,0:T(8,128)(2,1)S(1)} %get-tuple-element.49.refs_0_), channel_id=1, source_target_pairs={{0,1},{1,0},{2,3},{3,2},{4,5},{5,4},{6,7},{7,6},{8,9},{9,8},{10,11... | collective-permute-start | bytes 2371592 | tf_op jit(solution)/shard_map/ppermute | solution.py:455
  2.0 14.5 %collective-permute-start.2 = (bf16[1552,128]{1,0:T(8,128)(2,1)S(1)}, bf16[1552,128]{1,0:T(8,128)(2,1)S(1)}, u32[]{:S(2)}, u32[]{:S(2)}) collective-permute-start(bf16[1552,128]{1,0:T(8,128)(2,1)S(1)} %get-tuple-element.59.refs_4_), channel_id=1, source_target_pairs={{0,4},{4,12},{12,20},{20,28},{28,24},{24,16},{16,8},{8,0},{1,5},{5... | collective-permute-start | bytes 1191944 | tf_op jit(solution)/shard_map/ppermute | solution.py:442
  4.6 22.5 %copy-start = (s32[2,4]{1,0:T(2,128)S(1)}, s32[2,4]{1,0:T(2,128)}, u32[]{:S(2)}) copy-start(s32[2,4]{1,0:T(2,128)} %out_mask_ref) | copy-start | bytes 100
  4.6 12.0 %collective-permute-start.3 = (bf16[1536,128]{1,0:T(8,128)(2,1)S(1)}, bf16[1536,128]{1,0:T(8,128)(2,1)S(1)}, u32[]{:S(2)}, u32[]{:S(2)}) collective-permute-start(bf16[1536,128]{1,0:T(8,128)(2,1)S(1)} %get-tuple-element.39.refs_5_), channel_id=1, source_target_pairs={{0,8},{4,0},{12,4},{20,12},{28,20},{24,28},{16,24},{8,16},{1,9},{5... | collective-permute-start | bytes 1179656 | tf_op jit(solution)/shard_map/ppermute | solution.py:442
  4.7 22.9 %collective-permute-start.5 = (bf16[3088,128]{1,0:T(8,128)(2,1)S(1)}, bf16[3088,128]{1,0:T(8,128)(2,1)S(1)}, u32[]{:S(2)}, u32[]{:S(2)}) collective-permute-start(bf16[3088,128]{1,0:T(8,128)(2,1)S(1)} %get-tuple-element.49.refs_0_), channel_id=1, source_target_pairs={{0,2},{1,3},{2,0},{3,1},{4,6},{5,7},{6,4},{7,5},{8,10},{9,11},{10,... | collective-permute-start | bytes 2371592 | tf_op jit(solution)/shard_map/ppermute | solution.py:455
  6.8 18.3 %collective-permute-start.1 = (bf16[1552,128]{1,0:T(8,128)(2,1)S(1)}, bf16[1552,128]{1,0:T(8,128)(2,1)S(1)}, u32[]{:S(2)}, u32[]{:S(2)}) collective-permute-start(bf16[1552,128]{1,0:T(8,128)(2,1)S(1)} %get-tuple-element.59.refs_4_), channel_id=1, source_target_pairs={{0,8},{4,0},{12,4},{20,12},{28,20},{24,28},{16,24},{8,16},{1,9},{5... | collective-permute-start | bytes 1191944 | tf_op jit(solution)/shard_map/ppermute | solution.py:442
  8.4 14.8 %collective-permute-start = (bf16[1536,128]{1,0:T(8,128)(2,1)S(1)}, bf16[1536,128]{1,0:T(8,128)(2,1)S(1)}, u32[]{:S(2)}, u32[]{:S(2)}) collective-permute-start(bf16[1536,128]{1,0:T(8,128)(2,1)S(1)} %get-tuple-element.39.refs_5_), channel_id=1, source_target_pairs={{0,4},{4,12},{12,20},{20,28},{28,24},{24,16},{16,8},{8,0},{1,5},{5... | collective-permute-start | bytes 1179656 | tf_op jit(solution)/shard_map/ppermute | solution.py:442
  16.5 16.9 %collective-permute-start.9 = (bf16[1552,128]{1,0:T(8,128)(2,1)S(1)}, bf16[1552,128]{1,0:T(8,128)(2,1)S(1)}, u32[]{:S(2)}, u32[]{:S(2)}) collective-permute-start(bf16[1552,128]{1,0:T(8,128)(2,1)S(1)} %collective-permute-done.2.refs_6_.refs_8_), channel_id=1, source_target_pairs={{0,4},{4,12},{12,20},{20,28},{28,24},{24,16},{16,8},{8,0},{1,5},{5... | collective-permute-start | bytes 1191944 | tf_op jit(solution)/shard_map/ppermute | solution.py:442
  18.1 15.4 %collective-permute-start.10 = (bf16[1536,128]{1,0:T(8,128)(2,1)S(1)}, bf16[1536,128]{1,0:T(8,128)(2,1)S(1)}, u32[]{:S(2)}, u32[]{:S(2)}) collective-permute-start(bf16[1536,128]{1,0:T(8,128)(2,1)S(1)} %collective-permute-done.3.refs_9_.refs_11_), channel_id=1, source_target_pairs={{0,8},{4,0},{12,4},{20,12},{28,20},{24,28},{16,24},{8,16},{1,9},{5... | collective-permute-start | bytes 1179656 | tf_op jit(solution)/shard_map/ppermute | solution.py:442
  25.1 16.9 %collective-permute-start.8 = (bf16[1552,128]{1,0:T(8,128)(2,1)S(1)}, bf16[1552,128]{1,0:T(8,128)(2,1)S(1)}, u32[]{:S(2)}, u32[]{:S(2)}) collective-permute-start(bf16[1552,128]{1,0:T(8,128)(2,1)S(1)} %collective-permute-done.1.refs_8_.refs_10_), channel_id=1, source_target_pairs={{0,8},{4,0},{12,4},{20,12},{28,20},{24,28},{16,24},{8,16},{1,9},{5... | collective-permute-start | bytes 1191944 | tf_op jit(solution)/shard_map/ppermute | solution.py:442
  25.2 14.9 %collective-permute-start.7 = (bf16[1536,128]{1,0:T(8,128)(2,1)S(1)}, bf16[1536,128]{1,0:T(8,128)(2,1)S(1)}, u32[]{:S(2)}, u32[]{:S(2)}) collective-permute-start(bf16[1536,128]{1,0:T(8,128)(2,1)S(1)} %collective-permute-done.refs_7_.refs_9_), channel_id=1, source_target_pairs={{0,4},{4,12},{12,20},{20,28},{28,24},{24,16},{16,8},{8,0},{1,5},{5... | collective-permute-start | bytes 1179656 | tf_op jit(solution)/shard_map/ppermute | solution.py:442
  27.7 16.4 %collective-permute-start.6 = (bf16[3088,128]{1,0:T(8,128)(2,1)S(1)}, bf16[3088,128]{1,0:T(8,128)(2,1)S(1)}, u32[]{:S(2)}, u32[]{:S(2)}) collective-permute-start(bf16[3088,128]{1,0:T(8,128)(2,1)S(1)} %collective-permute-done.5.refs_0_), channel_id=1, source_target_pairs={{0,1},{1,0},{2,3},{3,2},{4,5},{5,4},{6,7},{7,6},{8,9},{9,8},{10,11... | collective-permute-start | bytes 2371592 | tf_op jit(solution)/shard_map/ppermute | solution.py:455
  33.5 16.9 %collective-permute-start.11 = (bf16[1552,128]{1,0:T(8,128)(2,1)S(1)}, bf16[1552,128]{1,0:T(8,128)(2,1)S(1)}, u32[]{:S(2)}, u32[]{:S(2)}) collective-permute-start(bf16[1552,128]{1,0:T(8,128)(2,1)S(1)} %collective-permute-done.9.refs_4_), channel_id=1, source_target_pairs={{0,4},{4,12},{12,20},{20,28},{28,24},{24,16},{16,8},{8,0},{1,5},{5... | collective-permute-start | bytes 1191944 | tf_op jit(solution)/shard_map/ppermute | solution.py:442
  35.1 15.4 %collective-permute-start.12 = (bf16[1536,128]{1,0:T(8,128)(2,1)S(1)}, bf16[1536,128]{1,0:T(8,128)(2,1)S(1)}, u32[]{:S(2)}, u32[]{:S(2)}) collective-permute-start(bf16[1536,128]{1,0:T(8,128)(2,1)S(1)} %collective-permute-done.10.refs_7_), channel_id=1, source_target_pairs={{0,8},{4,0},{12,4},{20,12},{28,20},{24,28},{16,24},{8,16},{1,9},{5... | collective-permute-start | bytes 1179656 | tf_op jit(solution)/shard_map/ppermute | solution.py:442
  42.0 14.8 %collective-permute-start.15 = (bf16[1536,128]{1,0:T(8,128)(2,1)S(1)}, bf16[1536,128]{1,0:T(8,128)(2,1)S(1)}, u32[]{:S(2)}, u32[]{:S(2)}) collective-permute-start(bf16[1536,128]{1,0:T(8,128)(2,1)S(1)} %collective-permute-done.7.refs_5_), channel_id=1, source_target_pairs={{0,4},{4,12},{12,20},{20,28},{28,24},{24,16},{16,8},{8,0},{1,5},{5... | collective-permute-start | bytes 1179656 | tf_op jit(solution)/shard_map/ppermute | solution.py:442
  43.6 14.6 %collective-permute-start.16 = (bf16[1552,128]{1,0:T(8,128)(2,1)S(1)}, bf16[1552,128]{1,0:T(8,128)(2,1)S(1)}, u32[]{:S(2)}, u32[]{:S(2)}) collective-permute-start(bf16[1552,128]{1,0:T(8,128)(2,1)S(1)} %collective-permute-done.8.refs_6_), channel_id=1, source_target_pairs={{0,8},{4,0},{12,4},{20,12},{28,20},{24,28},{16,24},{8,16},{1,9},{5... | collective-permute-start | bytes 1191944 | tf_op jit(solution)/shard_map/ppermute | solution.py:442
  50.4 12.0 %collective-permute-start.13 = (bf16[1552,128]{1,0:T(8,128)(2,1)S(1)}, bf16[1552,128]{1,0:T(8,128)(2,1)S(1)}, u32[]{:S(2)}, u32[]{:S(2)}) collective-permute-start(bf16[1552,128]{1,0:T(8,128)(2,1)S(1)} %collective-permute-done.11.refs_2_), channel_id=1, source_target_pairs={{0,4},{1,3},{2,6},{3,1},{4,12},{5,7},{6,14},{7,5},{12,20},{13,15},... | collective-permute-start | bytes 1191944 | tf_op jit(solution)/shard_map/ppermute | solution.py:452
  52.0 10.4 %collective-permute-start.14 = (bf16[1536,128]{1,0:T(8,128)(2,1)S(1)}, bf16[1536,128]{1,0:T(8,128)(2,1)S(1)}, u32[]{:S(2)}, u32[]{:S(2)}) collective-permute-start(bf16[1536,128]{1,0:T(8,128)(2,1)S(1)} %collective-permute-done.12.refs_5_), channel_id=1, source_target_pairs={{0,8},{1,3},{2,10},{3,1},{4,0},{5,7},{6,2},{7,5},{12,4},{13,15},{1... | collective-permute-start | bytes 1179656 | tf_op jit(solution)/shard_map/ppermute | solution.py:452
  55.3 8.0 %collective-permute-start.17 = (bf16[1552,128]{1,0:T(8,128)(2,1)S(1)}, bf16[1552,128]{1,0:T(8,128)(2,1)S(1)}, u32[]{:S(2)}, u32[]{:S(2)}) collective-permute-start(bf16[1552,128]{1,0:T(8,128)(2,1)S(1)} %collective-permute-done.11.refs_2_), channel_id=1, source_target_pairs={{0,0},{1,5},{2,2},{3,7},{4,4},{5,13},{6,6},{7,15},{12,12},{13,21},... | collective-permute-start | bytes 1191944 | tf_op jit(solution)/shard_map/ppermute | solution.py:452
  56.8 6.5 %collective-permute-start.18 = (bf16[1536,128]{1,0:T(8,128)(2,1)S(1)}, bf16[1536,128]{1,0:T(8,128)(2,1)S(1)}, u32[]{:S(2)}, u32[]{:S(2)}) collective-permute-start(bf16[1536,128]{1,0:T(8,128)(2,1)S(1)} %collective-permute-done.12.refs_5_), channel_id=1, source_target_pairs={{0,0},{1,9},{2,2},{3,11},{4,4},{5,1},{6,6},{7,3},{12,12},{13,5},{1... | collective-permute-start | bytes 1179656 | tf_op jit(solution)/shard_map/ppermute | solution.py:452
  63.3 3.8 %collective-permute-start.19 = (f32[1,1024]{1,0:T(1,128)S(1)}, f32[1,1024]{1,0:T(1,128)S(1)}, u32[]{:S(2)}, u32[]{:S(2)}) collective-permute-start(f32[1,1024]{1,0:T(1,128)S(1)} %get-tuple-element.72), channel_id=1, source_target_pairs={{0,4},{4,0},{8,12},{12,8},{16,20},{20,16},{24,28},{28,24},{1,5},{5... | collective-permute-start | bytes 12296 | tf_op jit(solution)/shard_map/ppermute | solution.py:421
  67.1 5.6 %collective-permute-start.20 = (f32[1,1024]{1,0:T(1,128)S(1)}, f32[1,1024]{1,0:T(1,128)S(1)}, u32[]{:S(2)}, u32[]{:S(2)}) collective-permute-start(f32[1,1024]{1,0:T(1,128)S(1)} %add.12), channel_id=1, source_target_pairs={{0,8},{4,12},{8,16},{12,20},{16,24},{20,28},{24,0},{28,4},{1,9},{5... | collective-permute-start | bytes 12296 | tf_op jit(solution)/shard_map/ppermute | solution.py:423
  68.8 4.5 %collective-permute-start.21 = (f32[1,1024]{1,0:T(1,128)S(1)}, f32[1,1024]{1,0:T(1,128)S(1)}, u32[]{:S(2)}, u32[]{:S(2)}) collective-permute-start(f32[1,1024]{1,0:T(1,128)S(1)} %add.12), channel_id=1, source_target_pairs={{0,16},{4,20},{8,24},{12,28},{16,0},{20,4},{24,8},{28,12},{1,17},{... | collective-permute-start | bytes 12296 | tf_op jit(solution)/shard_map/ppermute | solution.py:423
  71.4 3.6 %collective-permute-start.22 = (f32[1,1024]{1,0:T(1,128)S(1)}, f32[1,1024]{1,0:T(1,128)S(1)}, u32[]{:S(2)}, u32[]{:S(2)}) collective-permute-start(f32[1,1024]{1,0:T(1,128)S(1)} %add.12), channel_id=1, source_target_pairs={{0,24},{4,28},{8,0},{12,4},{16,8},{20,12},{24,16},{28,20},{1,25},{... | collective-permute-start | bytes 12296 | tf_op jit(solution)/shard_map/ppermute | solution.py:423
